TPU v7x, 512 devices: a whole 4x4x16 slice. The times are simulated.
512 devices in a mesh: lat: 32 (over y_hi, z), lon: 16 (over y_lo, x, core).
Axes of the slice: x: 4, y: 4 (y_hi: 2, y_lo: 2; y = y_hi * 2 + y_lo), z: 16, core: 2. Of those that a mesh axis runs over, the one named last changes fastest.
Arguments:
- field: bfloat16 [160, 2048, 256], P('lat', 'lon'), may hold values from -6 to 6
- cotangent: bfloat16 [160, 2048, 256], P('lat', 'lon'), may hold values from -6 to 6
- kernel_values: float32 [4, 160, 9, 128], P(None, 'lat'), may hold values from -0.3 to 0.3
- bounds: int32 [2, 160, 9], P(None, 'lat'), may hold values from -63 to 63, as said below
- weight: bfloat16 [1024, 256], replicated, may hold values from -0.1875 to 0.1875
Outputs:
- grad_field: float32 [160, 2048, 256], P('lat', 'lon')
- grad_weight: float32 [1024, 256], replicated
Inputs may be any that keep to these rules, and one draw needn't show every extreme that they name: bounds[0] <= 0 <= bounds[1]; some entry has magnitude 64 - 1 in every draw.
All inputs are finite; a program needn't handle non-finite values.
Results may differ from a plain program's by a relative error of at most 0.0041.
Values may be sent and summed in bfloat16 or wider, within the bound.
No kernel may reach another device: no remote copies, remote signals or barrier semaphores. Data moves between devices by JAX's collectives and lax.ppermute only.
A program may use at most 64 MiB of HBM per device.

v0:
```python
import math

import jax
import jax.numpy as jnp
from jax import lax
from jax.sharding import PartitionSpec as P


def extended_2(cells, sides, width, closed):
    for axis, dim in sides:
        count = lax.axis_size(axis)
        ends = count if closed else count - 1
        head = lax.slice_in_dim(cells, 0, width, axis=dim)
        tail = lax.slice_in_dim(cells, cells.shape[dim] - width, cells.shape[dim], axis=dim)
        cells = jnp.concatenate(
            [
                lax.ppermute(tail, axis, [(i, (i + 1) % count) for i in range(ends)]),
                cells,
                lax.ppermute(head, axis, [((i + 1) % count, i) for i in range(ends)]),
            ],
            axis=dim,
        )
    return cells


def banded(band_line, col_count, ext_width):
    leading = band_line.shape[:-1]
    padded = jnp.concatenate(
        [band_line, jnp.zeros(leading + (ext_width + 1 - band_line.shape[-1],), band_line.dtype)],
        axis=-1,
    )
    repeated = jnp.tile(padded, (1,) * len(leading) + (col_count,))
    return repeated[..., : col_count * ext_width].reshape(leading + (col_count, ext_width))


def per_device(field, cotangent, kernel_values, bounds, weight):
    row_count, col_count, channels = field.shape
    half_width = kernel_values.shape[3] // 2
    row_span = kernel_values.shape[2]
    radius = (row_span - 1) // 2
    offsets = jnp.arange(2 * half_width, dtype=jnp.int32) - half_width
    inside = (offsets >= bounds[0][:, :, None]) & (offsets <= bounds[1][:, :, None])
    kernel = jnp.where(inside[None], kernel_values, jnp.zeros_like(kernel_values)).astype(
        jnp.bfloat16
    )
    kernel_ext = extended_2(kernel, (("lat", 1),), radius, False)
    stacked = jnp.concatenate([field, cotangent], axis=2)
    widened = extended_2(stacked, (("lon", 1),), half_width, True)
    extended = extended_2(widened, (("lat", 0),), radius, False)
    ext_width = col_count + 2 * half_width
    mixing = weight.reshape(-1, channels, weight.shape[1])

    def one_row(running, row_step):
        window = lax.dynamic_slice_in_dim(extended, row_step, row_span, 0)
        kernel_slab = lax.dynamic_slice_in_dim(kernel_ext, row_step, row_span, 1)
        forward_band = banded(kernel_slab[:, radius], col_count, ext_width)
        basis_row = jnp.einsum(
            "krij,rjc->ikc",
            forward_band,
            window[:, :, :channels],
            preferred_element_type=jnp.float32,
        )
        basis_row = basis_row.astype(jnp.bfloat16).reshape(col_count, -1)
        cot_own = window[radius, half_width : half_width + col_count, channels:]
        running = running + lax.dot_general(
            basis_row, cot_own, (((0,), (0,)), ((), ())), preferred_element_type=jnp.float32
        )
        diag_rows = jnp.moveaxis(jnp.diagonal(kernel_slab[:, :, ::-1, :], axis1=1, axis2=2), -1, 1)
        band_line = jnp.concatenate(
            [jnp.zeros(diag_rows.shape[:2] + (1,), diag_rows.dtype), diag_rows[..., ::-1]], axis=-1
        )
        back_band = banded(band_line, col_count, ext_width)
        spread = jnp.einsum(
            "ksji,sic->jkc", back_band, window[:, :, channels:], preferred_element_type=jnp.float32
        ).astype(jnp.bfloat16)
        grad_row = jnp.einsum("jko,kio->ji", spread, mixing, preferred_element_type=jnp.float32)
        return (running, grad_row)

    zero_sum = jnp.zeros((weight.shape[0], weight.shape[1]), jnp.float32)
    running, grad_rows = lax.scan(one_row, zero_sum, jnp.arange(row_count, dtype=jnp.int32))
    summed = lax.psum(running, ("lat", "lon"))
    norm_scale = 1.0 / math.sqrt(
        row_count * lax.axis_size("lat") * col_count * lax.axis_size("lon")
    )
    return (grad_rows, summed * norm_scale)


def solution(mesh):
    return jax.shard_map(
        per_device,
        mesh=mesh,
        in_specs=(
            P("lat", "lon", None),
            P("lat", "lon", None),
            P(None, "lat", None, None),
            P(None, "lat", None),
            P(),
        ),
        out_specs=(P("lat", "lon", None), P()),
        check_vma=False,
    )
```

profile of v0, /device:TPU:1, one launch (start us, length us, event | category | flops | bytes accessed | tf_op | source)
XLA Modules:
  0.0 728.1 jit_solution(3680637919826743421)
XLA Ops:
  9.3 4.5 collective-permute-start
  13.8 6.2 collective-permute-start.1
  23.5 3.6 collective-permute-start.2
  28.6 4.7 collective-permute-start.4
  34.6 12.1 %collective-permute-done.4 = bf16[4,4,9,128]{3,0,2,1:T(4,128)(2,1)} collective-permute-done((bf16[4,4,9,128]{3,0,2,1:T(4,128)(2,1)S(1)}, bf16[4,4,9,128]{3,0,2,1:T(4,128)(2,1)}, u32[]{:S(2)}, u32[]{:S(2)}) %collective-permute-start.4) | collective-permute-done | bytes 36896 | tf_op jit(solution)/shard_map/ppermute | solution.py:17
  46.8 4.0 collective-permute-done.5
  51.7 3.0 pad_maximum_fusion
  54.6 189.4 %while.13 = (s32[]{:T(128)}, f32[1024,256]{1,0:T(8,128)}, f32[5,128,256]{2,1,0:T(8,128)}, s32[5]{0:T(128)S(1)}, bf16[13,256,512]{2,1,0:T(8,128)(2,1)}, /*index=5...) while((s32[]{:T(128)}, f32[1024,256]{1,0:T(8,128)}, ...), condition=%wide.region_1.2_spmd.clone, body=%wide.region_0.1_spmd.clone.sunk | while | flops 1343019264 | bytes 60151648 | solution.py:80
  57.4 7.7 %tile.27 = bf16[4,9,32896]{2,0,1:T(4,128)(2,1)} reshape(bf16[4,9,128,257]{3,2,0,1:T(8,128)(2,1)S(1)} %tile.26) | data formatting | bytes 4737024 | tf_op jit(solution)/shard_map/while/body/eval_jaxpr/tile | solution.py:32
  66.8 2.9 reshape.58
  69.8 2.9 fusion.27
  76.3 7.7 %tile.29 = bf16[4,9,32896]{2,0,1:T(4,128)(2,1)} reshape(bf16[4,9,128,257]{3,2,0,1:T(8,128)(2,1)S(1)} %tile.28) | data formatting | bytes 4737024 | tf_op jit(solution)/shard_map/while/body/eval_jaxpr/tile | solution.py:32
  85.7 2.9 reshape.59
  88.7 3.8 fusion.28
  95.3 7.7 %tile.27 = bf16[4,9,32896]{2,0,1:T(4,128)(2,1)} reshape(bf16[4,9,128,257]{3,2,0,1:T(8,128)(2,1)S(1)} %tile.26) | data formatting | bytes 4737024 | tf_op jit(solution)/shard_map/while/body/eval_jaxpr/tile | solution.py:32
  104.7 2.9 reshape.58
  107.6 2.9 fusion.27
  114.2 7.7 %tile.29 = bf16[4,9,32896]{2,0,1:T(4,128)(2,1)} reshape(bf16[4,9,128,257]{3,2,0,1:T(8,128)(2,1)S(1)} %tile.28) | data formatting | bytes 4737024 | tf_op jit(solution)/shard_map/while/body/eval_jaxpr/tile | solution.py:32
  126.6 3.9 fusion.28
  133.2 7.7 %tile.27 = bf16[4,9,32896]{2,0,1:T(4,128)(2,1)} reshape(bf16[4,9,128,257]{3,2,0,1:T(8,128)(2,1)S(1)} %tile.26) | data formatting | bytes 4737024 | tf_op jit(solution)/shard_map/while/body/eval_jaxpr/tile | solution.py:32
  145.5 2.9 fusion.27
  152.1 7.7 %tile.29 = bf16[4,9,32896]{2,0,1:T(4,128)(2,1)} reshape(bf16[4,9,128,257]{3,2,0,1:T(8,128)(2,1)S(1)} %tile.28) | data formatting | bytes 4737024 | tf_op jit(solution)/shard_map/while/body/eval_jaxpr/tile | solution.py:32
  164.4 3.8 fusion.28
  171.1 7.7 %tile.27 = bf16[4,9,32896]{2,0,1:T(4,128)(2,1)} reshape(bf16[4,9,128,257]{3,2,0,1:T(8,128)(2,1)S(1)} %tile.26) | data formatting | bytes 4737024 | tf_op jit(solution)/shard_map/while/body/eval_jaxpr/tile | solution.py:32
  183.4 2.9 fusion.27
  190.0 7.7 %tile.29 = bf16[4,9,32896]{2,0,1:T(4,128)(2,1)} reshape(bf16[4,9,128,257]{3,2,0,1:T(8,128)(2,1)S(1)} %tile.28) | data formatting | bytes 4737024 | tf_op jit(solution)/shard_map/while/body/eval_jaxpr/tile | solution.py:32
  202.3 3.9 fusion.28
  209.0 7.7 %tile.27 = bf16[4,9,32896]{2,0,1:T(4,128)(2,1)} reshape(bf16[4,9,128,257]{3,2,0,1:T(8,128)(2,1)S(1)} %tile.26) | data formatting | bytes 4737024 | tf_op jit(solution)/shard_map/while/body/eval_jaxpr/tile | solution.py:32
  221.3 2.9 fusion.27
  227.9 7.7 %tile.29 = bf16[4,9,32896]{2,0,1:T(4,128)(2,1)} reshape(bf16[4,9,128,257]{3,2,0,1:T(8,128)(2,1)S(1)} %tile.28) | data formatting | bytes 4737024 | tf_op jit(solution)/shard_map/while/body/eval_jaxpr/tile | solution.py:32
  240.2 3.8 fusion.28
  244.1 474.9 %all-reduce.3.cloned.1.call-done = f32[1024,256]{1,0:T(8,128)} async-done(((f32[1024,256]{1,0:T(8,128)}), f32[1024,256]{1,0:T(8,128)}) %all-reduce.3.cloned.1.call-update) | async-done | bytes 1048592 | tf_op jit(solution)/shard_map/psum | solution.py:81
  (182 shorter events, 71.1 us)
Async XLA Ops:
  7.2 12.9 %copy-start.6 = (s32[2,5,9]{2,0,1:T(2,128)S(1)}, s32[2,5,9]{2,0,1:T(2,128)}, u32[]{:S(2)}) copy-start(s32[2,5,9]{2,0,1:T(2,128)} %param.10) | copy-start | bytes 1084
  7.2 711.8 %all-reduce.3.cloned.1.call-start = ((), (), s32[]{:S(2)}) async-start(), calls=%async_computation | async-start | bytes 2097152 | tf_op jit(solution)/shard_map/psum | solution.py:81
  9.3 10.8 %collective-permute-start = (bf16[5,64,512]{2,1,0:T(8,128)(2,1)S(1)}, bf16[5,64,512]{2,1,0:T(8,128)(2,1)S(1)}, u32[]{:S(2)}, u32[]{:S(2)}) collective-permute-start(bf16[5,64,512]{2,1,0:T(8,128)(2,1)S(1)} %get-tuple-element.89), channel_id=1, source_target_pairs={{0,1},{1,2},{2,3},{3,4},{4,5},{5,6},{6,7},{7,8},{8,9},{9,10},{10,1... | collective-permute-start | bytes 983048 | tf_op jit(solution)/shard_map/ppermute | solution.py:17
  13.8 8.4 %collective-permute-start.1 = (bf16[5,64,512]{2,1,0:T(8,128)(2,1)S(1)}, bf16[5,64,512]{2,1,0:T(8,128)(2,1)S(1)}, u32[]{:S(2)}, u32[]{:S(2)}) collective-permute-start(bf16[5,64,512]{2,1,0:T(8,128)(2,1)S(1)} %get-tuple-element.90), channel_id=1, source_target_pairs={{1,0},{2,1},{3,2},{4,3},{5,4},{6,5},{7,6},{8,7},{9,8},{10,9},{11,1... | collective-permute-start | bytes 983048 | tf_op jit(solution)/shard_map/ppermute | solution.py:19
  22.3 6.2 copy-start.5
  23.5 28.2 %collective-permute-start.2 = (bf16[4,256,512]{2,1,0:T(8,128)(2,1)}, bf16[4,256,512]{2,1,0:T(8,128)(2,1)S(1)}, u32[]{:S(2)}, u32[]{:S(2)}) collective-permute-start(bf16[4,256,512]{2,1,0:T(8,128)(2,1)} %get-tuple-element.87), channel_id=1, source_target_pairs={{0,16},{16,32},{32,48},{48,64},{64,80},{80,96},{96,112},{112,128},... | collective-permute-start | bytes 3145736 | tf_op jit(solution)/shard_map/ppermute | solution.py:17
  27.1 24.6 %collective-permute-start.3 = (bf16[4,256,512]{2,1,0:T(8,128)(2,1)S(1)}, bf16[4,256,512]{2,1,0:T(8,128)(2,1)}, u32[]{:S(2)}, u32[]{:S(2)}) collective-permute-start(bf16[4,256,512]{2,1,0:T(8,128)(2,1)S(1)} %get-tuple-element.88), channel_id=1, source_target_pairs={{16,0},{32,16},{48,32},{64,48},{80,64},{96,80},{112,96},{128,112},... | collective-permute-start | bytes 3145736 | tf_op jit(solution)/shard_map/ppermute | solution.py:19
  28.5 18.2 %copy-start.4 = (bf16[4,5,9,128]{3,0,2,1:T(4,128)(2,1)}, bf16[4,5,9,128]{3,0,2,1:T(4,128)(2,1)S(1)}, u32[]{:S(2)}) copy-start(bf16[4,5,9,128]{3,0,2,1:T(4,128)(2,1)S(1)} %select_convert_fusion) | copy-start | bytes 138244
  28.6 18.2 %collective-permute-start.4 = (bf16[4,4,9,128]{3,0,2,1:T(4,128)(2,1)S(1)}, bf16[4,4,9,128]{3,0,2,1:T(4,128)(2,1)}, u32[]{:S(2)}, u32[]{:S(2)}) collective-permute-start(bf16[4,4,9,128]{3,0,2,1:T(4,128)(2,1)S(1)} %get-tuple-element.91), channel_id=1, source_target_pairs={{0,16},{16,32},{32,48},{48,64},{64,80},{80,96},{96,112},{112,128},... | collective-permute-start | bytes 110600 | tf_op jit(solution)/shard_map/ppermute | solution.py:17
  33.3 17.5 %collective-permute-start.5 = (bf16[4,4,9,128]{3,0,2,1:T(4,128)(2,1)S(1)}, bf16[4,4,9,128]{3,0,2,1:T(4,128)(2,1)}, u32[]{:S(2)}, u32[]{:S(2)}) collective-permute-start(bf16[4,4,9,128]{3,0,2,1:T(4,128)(2,1)S(1)} %get-tuple-element.92), channel_id=1, source_target_pairs={{16,0},{32,16},{48,32},{64,48},{80,64},{96,80},{112,96},{128,112},... | collective-permute-start | bytes 110600 | tf_op jit(solution)/shard_map/ppermute | solution.py:19
  54.6 2.5 copy-start.2
  69.8 2.9 copy-start
  84.1 1.7 slice-start.1
  85.7 2.9 copy-start.7
  88.7 3.8 copy-start.3
  92.5 2.5 copy-start.2
  107.6 2.9 copy-start
  123.6 2.9 copy-start.7
  126.5 3.9 copy-start.3
  130.4 2.5 copy-start.2
  140.9 1.7 slice-start
  145.5 2.9 copy-start
  161.5 2.9 copy-start.7
  164.4 3.8 copy-start.3
  168.3 2.5 copy-start.2
  183.4 2.9 copy-start
  199.4 2.9 copy-start.7
  202.3 3.9 copy-start.3
  206.2 2.5 copy-start.2
  221.3 2.9 copy-start
  237.3 2.9 copy-start.7
  240.2 3.8 copy-start.3
  (13 other events, 18.7 us)
Sparse Core Ops, SparseCore 0:
  244.2 474.7 all-reduce.2
where the time goes:
time: 730 us; the launch traced here: 728 us
  waiting for transfers between devices  493 us (68%)
  local copies, waits for them, and re-layouts  142 us (19%)
  matrix products  40.2 us (6%)
  starting transfers between devices  21.6 us (3%)
  between operations  14.2 us (2%)
  loops' own time  9.86 us (1%)
    psum x1, waiting for transfers between devices, per_device(): summed = lax.psum(running, ('lat', 'lon'))  475 us
    another operation x20, local copies, waits for them, and re-layouts, banded(): repeated = jnp.tile(padded, (1,) * len(leading) + (col_count,))  80.4 us
    reshape x10, local copies, waits for them, and re-layouts, banded(): repeated[..., :col_count * ext_width]  29.2 us
    dot_general x5, matrix products, one_row(): jnp.einsum('jko,kio->ji', spread, mixing, preferred_element_type=jnp.floa...  19.2 us
    slice x20, local copies, waits for them, and re-layouts, banded(): repeated[..., :col_count * ext_width]  16.6 us
    dot_general x5, matrix products, one_row(): jnp.einsum('krij,rjc->ikc', forward_band, window[:, :, :channels], prefer...  14.7 us
  transfers between devices with their start and end apart: 7, of which 4 were waited for; matrix products, arithmetic and copies ran while one was open for 0% of the time, Pallas kernels for 0%

commit v1 on v0

v1 whole, which is shorter than its diff:
```python
import functools
import math

import jax
import jax.numpy as jnp
from jax import lax
from jax.experimental import pallas as pl
from jax.experimental.pallas import tpu as pltpu
from jax.sharding import Mesh, PartitionSpec as P

LAT_AXES = ("yh", "z")
LON_AXES = ("yl", "x", "core")
PLANE = ("yh", "yl", "x", "core")

ROWS, COLS, CH, NK, NR, RAD, HALF = 5, 128, 256, 4, 9, 4, 64
EXT = ROWS + 2 * RAD
LINES = NK * NR


def shifted(x, axes, step, closed):
    count = 1
    for a in axes:
        count *= lax.axis_size(a)
    if closed:
        pairs = [(i, (i + step) % count) for i in range(count)]
    else:
        pairs = [(i, i + step) for i in range(count) if 0 <= i + step < count]
    return lax.ppermute(x, axes, pairs)


def reverse_lines(up_ref, own_ref, down_ref, lines_ref):
    i = lax.broadcasted_iota(jnp.int32, (COLS, COLS), 0)
    j = lax.broadcasted_iota(jnp.int32, (COLS, COLS), 1)
    flip = ((i + j == 0) | (i + j == COLS)).astype(jnp.bfloat16)
    at = 0
    for ref in (up_ref, own_ref, down_ref):
        n = ref.shape[0]
        lines_ref[at : at + n, :] = jnp.dot(
            ref[...].astype(jnp.bfloat16), flip, preferred_element_type=jnp.float32
        )
        at += n


def own_mask():
    n = lax.broadcasted_iota(jnp.int32, (COLS, COLS), 0)
    i = lax.broadcasted_iota(jnp.int32, (COLS, COLS), 1)
    return ((i >= HALF) & (i > n)) | ((i < HALF) & (i <= n))


def fill_band(band_ref, lines_ref, mask, l):
    for k in range(NK):
        for s in range(NR):
            at = LINES * (l + s) + NR * k + NR - 1 - s
            row = jnp.broadcast_to(lines_ref[pl.ds(at, 1), :], (16, COLS))
            base = pltpu.roll(row, 0, 1, stride=1, stride_axis=0).astype(jnp.bfloat16)
            for g in range(COLS // 16):
                tile = base if g == 0 else pltpu.roll(base, 16 * g, 1)
                band_ref[
                    k * COLS + 16 * g : k * COLS + 16 * (g + 1), s * COLS : (s + 1) * COLS
                ] = tile * mask[16 * g : 16 * (g + 1), :]


def inner_kernel(kup, kown, kdown, cup, cown, cdown, part_ref, lines, cells, bands):
    reverse_lines(kup, kown, kdown, lines)
    at = 0
    for ref in (cup, cown, cdown):
        for row in range(ref.shape[0]):
            cells[at : at + HALF, :] = ref[row, HALF:, :]
            cells[at + HALF : at + COLS, :] = ref[row, :HALF, :]
            at += COLS
    mask = own_mask().astype(jnp.bfloat16)
    for l in range(ROWS):
        band = bands.at[l % 2]
        fill_band(band, lines, mask, l)
        part_ref[l] = jnp.dot(
            band[...],
            cells[l * COLS : (l + NR) * COLS, :],
            preferred_element_type=jnp.float32,
        )


def outer_kernel(
    scale, kup, kown, kdown, left, right, part_ref, field_t, mixing, grad_ref, gw_ref,
    lines, cells, bands, spreads,
):
    reverse_lines(kup, kown, kdown, lines)
    for row in range(EXT):
        cells[row * COLS : row * COLS + HALF, :] = left[row]
        cells[row * COLS + HALF : (row + 1) * COLS, :] = right[row]
    mask = 1.0 - own_mask().astype(jnp.float32)
    mask = mask.astype(jnp.bfloat16)
    for l in range(ROWS):
        band = bands.at[l % 2]
        fill_band(band, lines, mask, l)
        spread = part_ref[l] + jnp.dot(
            band[...],
            cells[l * COLS : (l + NR) * COLS, :],
            preferred_element_type=jnp.float32,
        )
        spread = spread.astype(jnp.bfloat16)
        grad = jnp.zeros((COLS, CH), jnp.float32)
        for k in range(NK):
            one = spread[k * COLS : (k + 1) * COLS, :]
            spreads[k, l * COLS : (l + 1) * COLS, :] = one
            grad += jnp.dot(
                one, mixing[k * CH : (k + 1) * CH, :], preferred_element_type=jnp.float32
            )
        grad_ref[l] = grad
    for k in range(NK):
        total = jnp.dot(field_t[...], spreads[k], preferred_element_type=jnp.float32)
        gw_ref[k * CH : (k + 1) * CH, :] = (total * scale).astype(jnp.bfloat16)


def exchange(x, axes):
    return lax.all_to_all(x, axes, 0, 0, tiled=True)


def per_device(field, cotangent, kernel_values, bounds, weight):
    sizes = {a: lax.axis_size(a) for a in LAT_AXES + LON_AXES}
    lat_count = sizes["yh"] * sizes["z"]
    lon_count = sizes["yl"] * sizes["x"] * sizes["core"]
    offsets = jnp.arange(2 * HALF, dtype=jnp.int32) - HALF
    inside = (offsets >= bounds[0][:, :, None]) & (offsets <= bounds[1][:, :, None])
    kernel = jnp.where(inside[None], kernel_values, jnp.zeros_like(kernel_values))
    kernel = kernel.astype(jnp.bfloat16)
    lines = jnp.swapaxes(kernel, 0, 1).reshape(ROWS, LINES, COLS)

    kup = shifted(lines[ROWS - RAD :], LAT_AXES, 1, False)
    kdown = shifted(lines[:RAD], LAT_AXES, -1, False)
    cup = shifted(cotangent[ROWS - RAD :], LAT_AXES, 1, False)
    cdown = shifted(cotangent[:RAD], LAT_AXES, -1, False)
    kargs = (
        kup.reshape(RAD * LINES, COLS),
        lines.reshape(ROWS * LINES, COLS),
        kdown.reshape(RAD * LINES, COLS),
    )
    tall = jnp.concatenate([cup, cotangent, cdown], axis=0)
    left = shifted(tall[:, HALF:], LON_AXES, 1, True)
    right = shifted(tall[:, :HALF], LON_AXES, -1, True)

    params = pltpu.CompilerParams(vmem_limit_bytes=48 * 1024 * 1024)
    scratch = [
        pltpu.VMEM((EXT * LINES, COLS), jnp.float32),
        pltpu.VMEM((EXT * COLS, CH), jnp.bfloat16),
        pltpu.VMEM((2, NK * COLS, NR * COLS), jnp.bfloat16),
    ]
    band_flops = 2 * ROWS * NK * COLS * NR * COLS * CH
    part = pl.pallas_call(
        inner_kernel,
        out_shape=jax.ShapeDtypeStruct((ROWS, NK * COLS, CH), jnp.float32),
        scratch_shapes=scratch,
        compiler_params=params,
        cost_estimate=pl.CostEstimate(
            flops=band_flops, bytes_accessed=4 * 1024 * 1024, transcendentals=0
        ),
        name="inner_band",
    )(*kargs, cup, cotangent, cdown)

    field_t = field.reshape(ROWS * COLS, CH).T
    mixing = jnp.swapaxes(weight.reshape(NK, CH, CH), 1, 2).reshape(NK * CH, CH)
    scale = 1.0 / math.sqrt(ROWS * lat_count * COLS * lon_count)
    grad_field, gw = pl.pallas_call(
        functools.partial(outer_kernel, scale),
        out_shape=(
            jax.ShapeDtypeStruct((ROWS, COLS, CH), jnp.float32),
            jax.ShapeDtypeStruct((NK * CH, CH), jnp.bfloat16),
        ),
        scratch_shapes=scratch + [pltpu.VMEM((NK, ROWS * COLS, CH), jnp.bfloat16)],
        compiler_params=params,
        cost_estimate=pl.CostEstimate(
            flops=band_flops * 2, bytes_accessed=6 * 1024 * 1024, transcendentals=0
        ),
        name="outer_band",
    )(*kargs, left, right, part, field_t, mixing)

    plane, depth = sizes["yh"] * lon_count, sizes["z"]
    piece = gw.shape[0] // plane
    got = exchange(gw.reshape(plane, piece, CH), PLANE)
    mine = jnp.sum(got.astype(jnp.float32), axis=0).astype(jnp.bfloat16)
    got = exchange(jnp.broadcast_to(mine[None], (depth, piece, CH)), "z")
    mine = jnp.sum(got.astype(jnp.float32), axis=0).astype(jnp.bfloat16)
    got = exchange(jnp.broadcast_to(mine[None], (plane, piece, CH)), PLANE)
    return (grad_field, got.reshape(NK * CH, CH).astype(jnp.float32))


def solution(mesh):
    fine = Mesh(mesh.devices.reshape(2, 16, 2, 4, 2), LAT_AXES + LON_AXES)
    return jax.shard_map(
        per_device,
        mesh=fine,
        in_specs=(
            P(LAT_AXES, LON_AXES, None),
            P(LAT_AXES, LON_AXES, None),
            P(None, LAT_AXES, None, None),
            P(None, LAT_AXES, None),
            P(),
        ),
        out_specs=(P(LAT_AXES, LON_AXES, None), P()),
        check_vma=False,
    )
```

time: 730 us -> 120 us (0.16)
  waiting for transfers between devices: 493 us -> 4.62 us
  local copies, waits for them, and re-layouts: 142 us -> 6.68 us
  blocking collectives: 0 us -> 73 us
  matrix products: 40.2 us -> 0 us
  between operations: 14.2 us -> 0.87 us
  loops' own time: 9.86 us -> 0 us
  Pallas kernels: 0 us -> 9.43 us
    psum x1 -> x0, waiting for transfers between devices: 475 us -> none  [per_device(): summed = lax.psum(running, ('lat', 'lon'))]
    another operation x25 -> x1, local copies, waits for them, and re-layouts: 80.4 us -> 0.03 us  [per_device(): lines.reshape(ROWS * LINES, COLS)]
    all_to_all x0 -> x3, blocking collectives: none -> 73 us  [exchange(): return lax.all_to_all(x, axes, 0, 0, tiled=True)]
    dot_general x15 -> x0, matrix products: 40.2 us -> none  [the longest x5 19.2 us: one_row(): jnp.einsum('jko,kio->ji', spread, mixing, preferred_element_type=jnp.floa...]
    reshape x10 -> x4, local copies, waits for them, and re-layouts: 29.2 us -> 0.43 us  [the longest x1 0.2 us: per_device(): mixing = jnp.swapaxes(weight.reshape(NK, CH, CH), 1, 2).reshape(NK * CH, CH)]
    slice x23 -> x5, local copies, waits for them, and re-layouts: 17.9 us -> 2.74 us  [the longest x1 1.12 us: per_device(): cdown = shifted(cotangent[:RAD], LAT_AXES, -1, False)]
    ppermute x6, waiting for transfers between devices: 18.3 us -> 4.62 us  [shifted(): return lax.ppermute(x, axes, pairs)]
    another operation x1 -> x0, loops' own time: 9.86 us -> none  [per_device(): lax.scan(one_row, zero_sum, jnp.arange(row_count, dtype=jnp.int32))]
  transfers between devices with their start and end apart: 7 -> 6, of which waited for: 4 -> 2; matrix products, arithmetic and copies ran while one was open for 0% -> 4% of each run, Pallas kernels for 0% -> 3%
where the time goes in v1:
time: 120 us; the launch traced here: 119 us
  blocking collectives  73 us (61%)
  starting transfers between devices  23.3 us (19%)
  Pallas kernels  9.43 us (8%)
  local copies, waits for them, and re-layouts  6.68 us (6%)
  waiting for transfers between devices  4.62 us (4%)
  other arithmetic  1.34 us (1%)
    all_to_all x3, blocking collectives, exchange(): return lax.all_to_all(x, axes, 0, 0, tiled=True)  73 us
    ppermute x6, starting transfers between devices, shifted(): return lax.ppermute(x, axes, pairs)  23.3 us
    pallas_call x1, Pallas kernels, per_device(): pl.pallas_call(functools.partial(outer_kernel, scale), out_shape=(jax.Sha...  5.82 us
    ppermute x6, waiting for transfers between devices, shifted(): return lax.ppermute(x, axes, pairs)  4.62 us
    pallas_call x1, Pallas kernels, per_device(): pl.pallas_call(inner_kernel, out_shape=jax.ShapeDtypeStruct((ROWS, NK * C...  3.6 us
  transfers between devices with their start and end apart: 6, of which 2 were waited for; matrix products, arithmetic and copies ran while one was open for 4% of the time, Pallas kernels for 3%

profile of v1, /device:TPU:1, one launch (start us, length us, event | category | flops | bytes accessed | tf_op | source)
XLA Modules:
  0.0 119.2 jit_solution(8106447171434533065)
XLA Ops:
  0.6 1.1 fusion.2
  1.8 0.0 copy-start.1
  1.8 1.4 %collective-permute-start.3 = (bf16[4,128,256]{2,1,0:T(8,128)(2,1)S(1)}, bf16[4,128,256]{2,1,0:T(8,128)(2,1)S(1)}, u32[]{:S(2)}, u32[]{:S(2)}) collective-permute-start(bf16[4,128,256]{2,1,0:T(8,128)(2,1)S(1)} %get-tuple-element.8), channel_id=1, source_target_pairs={{16,0},{32,16},{48,32},{64,48},{80,64},{96,80},{112,96},{128,112},... | collective-permute-start | bytes 786440 | tf_op jit(solution)/shard_map/ppermute | solution.py:28
  3.2 5.0 %collective-permute-start.2 = (bf16[4,128,256]{2,1,0:T(8,128)(2,1)S(1)}, bf16[4,128,256]{2,1,0:T(8,128)(2,1)S(1)}, u32[]{:S(2)}, u32[]{:S(2)}) collective-permute-start(bf16[4,128,256]{2,1,0:T(8,128)(2,1)S(1)} %get-tuple-element.9), channel_id=1, source_target_pairs={{0,16},{16,32},{32,48},{48,64},{64,80},{80,96},{96,112},{112,128},... | collective-permute-start | bytes 786440 | tf_op jit(solution)/shard_map/ppermute | solution.py:28
  8.2 0.8 fusion.4
  9.0 0.1 compare_and_fusion
  9.1 2.4 %collective-permute-done.2.cup = bf16[4,128,256]{2,1,0:T(8,128)(2,1)S(1)} collective-permute-done((bf16[4,128,256]{2,1,0:T(8,128)(2,1)S(1)}, bf16[4,128,256]{2,1,0:T(8,128)(2,1)S(1)}, u32[]{:S(2)}, u32[]{:S(2)}) %collective-permute-start.2) | collective-permute-done | bytes 262176 | tf_op jit(solution)/shard_map/ppermute | solution.py:28
  11.5 1.0 constant_dynamic-update-slice_fusion.1
  12.5 0.0 copy-start
  12.6 0.0 collective-permute-done.3.cdown
  12.6 1.0 fusion.1
  13.5 8.9 %collective-permute-start.5 = (bf16[13,64,256]{2,1,0:T(8,128)(2,1)}, bf16[13,64,256]{2,1,0:T(8,128)(2,1)S(1)}, u32[]{:S(2)}, u32[]{:S(2)}) collective-permute-start(bf16[13,64,256]{2,1,0:T(8,128)(2,1)} %get-tuple-element.6), channel_id=1, source_target_pairs={{0,15},{1,0},{2,1},{3,2},{4,3},{5,4},{6,5},{7,6},{8,7},{9,8},{10,9... | collective-permute-start | bytes 1277960 | tf_op jit(solution)/shard_map/ppermute | solution.py:28
  22.4 1.9 %collective-permute-start.4 = (bf16[13,64,256]{2,1,0:T(8,128)(2,1)}, bf16[13,64,256]{2,1,0:T(8,128)(2,1)S(1)}, u32[]{:S(2)}, u32[]{:S(2)}) collective-permute-start(bf16[13,64,256]{2,1,0:T(8,128)(2,1)} %get-tuple-element.7), channel_id=1, source_target_pairs={{0,1},{1,2},{2,3},{3,4},{4,5},{5,6},{6,7},{7,8},{8,9},{9,10},{10,1... | collective-permute-start | bytes 1277960 | tf_op jit(solution)/shard_map/ppermute | solution.py:28
  24.5 0.6 copy.23
  25.1 4.7 %collective-permute-start = (bf16[4,36,128]{2,0,1:T(4,128)(2,1)}, bf16[4,36,128]{2,0,1:T(4,128)(2,1)}, u32[]{:S(2)}, u32[]{:S(2)}) collective-permute-start(bf16[4,36,128]{2,0,1:T(4,128)(2,1)} %bitcast.3), channel_id=1, source_target_pairs={{0,16},{16,32},{32,48},{48,64},{64,80},{80,96},{96,112},{112,128},... | collective-permute-start | bytes 110600 | tf_op jit(solution)/shard_map/ppermute | solution.py:28
  29.8 1.3 %collective-permute-start.1 = (bf16[4,36,128]{2,0,1:T(4,128)(2,1)S(1)}, bf16[4,36,128]{2,0,1:T(4,128)(2,1)}, u32[]{:S(2)}, u32[]{:S(2)}) collective-permute-start(bf16[4,36,128]{2,0,1:T(4,128)(2,1)S(1)} %bitcast.23), channel_id=1, source_target_pairs={{16,0},{32,16},{48,32},{64,48},{80,64},{96,80},{112,96},{128,112},... | collective-permute-start | bytes 110600 | tf_op jit(solution)/shard_map/ppermute | solution.py:28
  31.2 0.2 copy.28
  31.4 0.2 copy.29
  31.6 0.0 collective-permute-done
  31.6 0.8 copy.24
  32.4 2.2 %collective-permute-done.1 = bf16[4,36,128]{2,0,1:T(4,128)(2,1)} collective-permute-done((bf16[4,36,128]{2,0,1:T(4,128)(2,1)S(1)}, bf16[4,36,128]{2,0,1:T(4,128)(2,1)}, u32[]{:S(2)}, u32[]{:S(2)}) %collective-permute-start.1) | collective-permute-done | bytes 36896 | tf_op jit(solution)/shard_map/ppermute | solution.py:28
  34.6 0.8 copy.27
  35.4 3.6 %inner_band.1.part_ref = f32[5,512,256]{2,1,0:T(8,128)S(1)} custom-call(bf16[144,128]{1,0:T(8,128)(2,1)S(1)} %reshape.39.kup, bf16[180,128]{1,0:T(8,128)(2,1)S(1)} %reshape_reshape.3.kown, bf16[144,128]{1,0:T(8,128)(2,1)S(1)} %reshape.40.kdown, bf16[4,128,256]{2,1,0:T(8,128)(2,1)S(1)} %collective-permute-done.2.cup, bf16[5,128,256]{2,1,0:T(8,128)(2,1)S(1)} %copy-done, ...), custom_call_target="tpu_custom_call" | custom-call | flops 1509949440 | bytes 4194304 | tf_op jit(solution)/shard_map/inner_band/pallas_call | solution.py:148
  39.0 0.0 collective-permute-done.5.right
  39.0 0.0 collective-permute-done.4.left
  39.1 5.8 %outer_band.1 = (f32[5,128,256]{2,1,0:T(8,128)}, bf16[1024,256]{1,0:T(8,128)(2,1)S(1)}) custom-call(bf16[144,128]{1,0:T(8,128)(2,1)S(1)} %reshape.39.kup, bf16[180,128]{1,0:T(8,128)(2,1)S(1)} %reshape_reshape.3.kown, bf16[144,128]{1,0:T(8,128)(2,1)S(1)} %reshape.40.kdown, bf16[13,64,256]{2,1,0:T(8,128)(2,1)S(1)} %collective-permute-done.4.left, ...), custom_call_target="tpu_custom_call" | custom-call | flops 3019898880 | bytes 6291456 | tf_op jit(solution)/shard_map/outer_band/pallas_call | solution.py:162
  44.9 34.8 %all_to_all.15 = bf16[32,32,256]{2,1,0:T(8,128)(2,1)S(1)} all-to-all(bf16[32,32,256]{2,1,0:T(8,128)(2,1)S(1)} %bitcast.19), channel_id=1, replica_groups=mesh['yh'=2,'z'=16,'yl'=2,'x'=4,'core'=2] {'yh','yl','x','core'}, dimensions={0} | all-to-all | bytes 1048576 | tf_op jit(solution)/shard_map/all_to_all | solution.py:115
  79.7 0.1 reduce_sum.24
  79.8 18.2 %all_to_all.16 = bf16[16,32,256]{2,1,0:T(8,128)(2,1)S(1)} all-to-all(bf16[16,32,256]{2,1,0:T(8,128)(2,1)S(1)} %broadcast_in_dim.16), channel_id=1, replica_groups=mesh['yh'=2,'z'=16,'yl'=2,'x'=4,'core'=2] {'z'}, dimensions={0} | all-to-all | bytes 524288 | tf_op jit(solution)/shard_map/all_to_all | solution.py:115
  98.0 0.1 broadcast_in_dim.17
  98.1 20.1 %all_to_all.17 = bf16[32,32,256]{2,1,0:T(8,128)(2,1)S(1)} all-to-all(bf16[32,32,256]{2,1,0:T(8,128)(2,1)S(1)} %broadcast_in_dim.17), channel_id=1, replica_groups=mesh['yh'=2,'z'=16,'yl'=2,'x'=4,'core'=2] {'yh','yl','x','core'}, dimensions={0} | all-to-all | bytes 1048576 | tf_op jit(solution)/shard_map/all_to_all | solution.py:115
  118.2 1.1 bitcast_convert_fusion
  (19 shorter events, 0.3 us)
Async XLA Ops:
  0.6 23.7 %copy-start.3 = (f32[4,5,9,128]{3,0,2,1:T(4,128)S(1)}, f32[4,5,9,128]{3,0,2,1:T(4,128)}, u32[]{:S(2)}) copy-start(f32[4,5,9,128]{3,0,2,1:T(4,128)} %param.7) | copy-start | bytes 276484
  0.6 30.6 %copy-start.2 = (bf16[5,128,256]{2,1,0:T(8,128)(2,1)S(1)}, bf16[5,128,256]{2,1,0:T(8,128)(2,1)}, u32[]{:S(2)}) copy-start(bf16[5,128,256]{2,1,0:T(8,128)(2,1)} %param.5) | copy-start | bytes 983044
  1.8 29.6 %copy-start.1 = (bf16[1024,256]{1,0:T(8,128)(2,1)S(1)}, bf16[1024,256]{1,0:T(8,128)(2,1)}, u32[]{:S(2)}) copy-start(bf16[1024,256]{1,0:T(8,128)(2,1)} %param.9) | copy-start | bytes 1572868
  1.8 10.8 %collective-permute-start.3 = (bf16[4,128,256]{2,1,0:T(8,128)(2,1)S(1)}, bf16[4,128,256]{2,1,0:T(8,128)(2,1)S(1)}, u32[]{:S(2)}, u32[]{:S(2)}) collective-permute-start(bf16[4,128,256]{2,1,0:T(8,128)(2,1)S(1)} %get-tuple-element.8), channel_id=1, source_target_pairs={{16,0},{32,16},{48,32},{64,48},{80,64},{96,80},{112,96},{128,112},... | collective-permute-start | bytes 786440 | tf_op jit(solution)/shard_map/ppermute | solution.py:28
  3.2 8.3 %collective-permute-start.2 = (bf16[4,128,256]{2,1,0:T(8,128)(2,1)S(1)}, bf16[4,128,256]{2,1,0:T(8,128)(2,1)S(1)}, u32[]{:S(2)}, u32[]{:S(2)}) collective-permute-start(bf16[4,128,256]{2,1,0:T(8,128)(2,1)S(1)} %get-tuple-element.9), channel_id=1, source_target_pairs={{0,16},{16,32},{32,48},{48,64},{64,80},{80,96},{96,112},{112,128},... | collective-permute-start | bytes 786440 | tf_op jit(solution)/shard_map/ppermute | solution.py:28
  12.5 22.9 %copy-start = (bf16[5,128,256]{2,1,0:T(8,128)(2,1)S(1)}, bf16[5,128,256]{2,1,0:T(8,128)(2,1)}, u32[]{:S(2)}) copy-start(bf16[5,128,256]{2,1,0:T(8,128)(2,1)} %cown.1) | copy-start | bytes 983044
  13.5 25.5 %collective-permute-start.5 = (bf16[13,64,256]{2,1,0:T(8,128)(2,1)}, bf16[13,64,256]{2,1,0:T(8,128)(2,1)S(1)}, u32[]{:S(2)}, u32[]{:S(2)}) collective-permute-start(bf16[13,64,256]{2,1,0:T(8,128)(2,1)} %get-tuple-element.6), channel_id=1, source_target_pairs={{0,15},{1,0},{2,1},{3,2},{4,3},{5,4},{6,5},{7,6},{8,7},{9,8},{10,9... | collective-permute-start | bytes 1277960 | tf_op jit(solution)/shard_map/ppermute | solution.py:28
  22.4 16.6 %collective-permute-start.4 = (bf16[13,64,256]{2,1,0:T(8,128)(2,1)}, bf16[13,64,256]{2,1,0:T(8,128)(2,1)S(1)}, u32[]{:S(2)}, u32[]{:S(2)}) collective-permute-start(bf16[13,64,256]{2,1,0:T(8,128)(2,1)} %get-tuple-element.7), channel_id=1, source_target_pairs={{0,1},{1,2},{2,3},{3,4},{4,5},{5,6},{6,7},{7,8},{8,9},{9,10},{10,1... | collective-permute-start | bytes 1277960 | tf_op jit(solution)/shard_map/ppermute | solution.py:28
  25.1 6.5 %collective-permute-start = (bf16[4,36,128]{2,0,1:T(4,128)(2,1)}, bf16[4,36,128]{2,0,1:T(4,128)(2,1)}, u32[]{:S(2)}, u32[]{:S(2)}) collective-permute-start(bf16[4,36,128]{2,0,1:T(4,128)(2,1)} %bitcast.3), channel_id=1, source_target_pairs={{0,16},{16,32},{32,48},{48,64},{64,80},{80,96},{96,112},{112,128},... | collective-permute-start | bytes 110600 | tf_op jit(solution)/shard_map/ppermute | solution.py:28
  29.8 4.8 %collective-permute-start.1 = (bf16[4,36,128]{2,0,1:T(4,128)(2,1)S(1)}, bf16[4,36,128]{2,0,1:T(4,128)(2,1)}, u32[]{:S(2)}, u32[]{:S(2)}) collective-permute-start(bf16[4,36,128]{2,0,1:T(4,128)(2,1)S(1)} %bitcast.23), channel_id=1, source_target_pairs={{16,0},{32,16},{48,32},{64,48},{80,64},{96,80},{112,96},{128,112},... | collective-permute-start | bytes 110600 | tf_op jit(solution)/shard_map/ppermute | solution.py:28

commit v2 on v1

--- a/solution.py
+++ b/solution.py
@@ -15,6 +15,8 @@
 ROWS, COLS, CH, NK, NR, RAD, HALF = 5, 128, 256, 4, 9, 4, 64
 EXT = ROWS + 2 * RAD
 LINES = NK * NR
+LINES_ROWS = RAD * LINES // 2
+PACKED = RAD * COLS + 80
 
 
 def shifted(x, axes, step, closed):
@@ -28,17 +30,53 @@
     return lax.ppermute(x, axes, pairs)
 
 
-def reverse_lines(up_ref, own_ref, down_ref, lines_ref):
+def prep_kernel(bounds_ref, values_ref, cells_ref, up_ref, down_ref, own_ref, lines):
+    offset = lax.broadcasted_iota(jnp.int32, (NK, COLS), 1) - HALF
+    for l in range(ROWS):
+        for r in range(NR):
+            inside = (offset >= bounds_ref[0, l, r]) & (offset <= bounds_ref[1, l, r])
+            at = LINES * l + NK * r
+            lines[at : at + NK, :] = jnp.where(inside, values_ref[l, r], 0.0)
+    lines[ROWS * LINES :, :] = jnp.zeros((192 - ROWS * LINES, COLS), jnp.float32)
     i = lax.broadcasted_iota(jnp.int32, (COLS, COLS), 0)
     j = lax.broadcasted_iota(jnp.int32, (COLS, COLS), 1)
     flip = ((i + j == 0) | (i + j == COLS)).astype(jnp.bfloat16)
-    at = 0
-    for ref in (up_ref, own_ref, down_ref):
-        n = ref.shape[0]
-        lines_ref[at : at + n, :] = jnp.dot(
-            ref[...].astype(jnp.bfloat16), flip, preferred_element_type=jnp.float32
+    own_ref[...] = jnp.dot(
+        lines[...].astype(jnp.bfloat16), flip, preferred_element_type=jnp.float32
+    )
+    for ref, row in ((up_ref, ROWS - RAD), (down_ref, 0)):
+        for n in range(RAD):
+            ref[n * COLS : (n + 1) * COLS, :] = cells_ref[row + n]
+        for half in range(2):
+            at = LINES * row + half * LINES_ROWS
+            ref[RAD * COLS : RAD * COLS + LINES_ROWS, half * COLS : (half + 1) * COLS] = own_ref[
+                at : at + LINES_ROWS, :
+            ].astype(jnp.bfloat16)
+        ref[RAD * COLS + LINES_ROWS :, :] = jnp.zeros(
+            (PACKED - RAD * COLS - LINES_ROWS, CH), jnp.bfloat16
         )
-        at += n
+
+
+def middle_kernel(up_ref, own_ref, down_ref, east_ref, west_ref):
+    for row in range(EXT):
+        if row < RAD:
+            cells = up_ref[row * COLS : (row + 1) * COLS, :]
+        elif row < RAD + ROWS:
+            cells = own_ref[row - RAD]
+        else:
+            at = (row - RAD - ROWS) * COLS
+            cells = down_ref[at : at + COLS, :]
+        east_ref[row] = cells[HALF:]
+        west_ref[row] = cells[:HALF]
+
+
+def gather_lines(up_ref, own_ref, down_ref, lines_ref):
+    for ref, at in ((up_ref, 0), (down_ref, (RAD + ROWS) * LINES)):
+        for half in range(2):
+            lines_ref[at + half * LINES_ROWS : at + (half + 1) * LINES_ROWS, :] = ref[
+                RAD * COLS : RAD * COLS + LINES_ROWS, half * COLS : (half + 1) * COLS
+            ].astype(jnp.float32)
+    lines_ref[RAD * LINES : (RAD + ROWS) * LINES, :] = own_ref[: ROWS * LINES, :]
 
 
 def own_mask():
@@ -50,7 +88,7 @@
 def fill_band(band_ref, lines_ref, mask, l):
     for k in range(NK):
         for s in range(NR):
-            at = LINES * (l + s) + NR * k + NR - 1 - s
+            at = LINES * (l + s) + NK * (NR - 1 - s) + k
             row = jnp.broadcast_to(lines_ref[pl.ds(at, 1), :], (16, COLS))
             base = pltpu.roll(row, 0, 1, stride=1, stride_axis=0).astype(jnp.bfloat16)
             for g in range(COLS // 16):
@@ -60,14 +98,18 @@
                 ] = tile * mask[16 * g : 16 * (g + 1), :]
 
 
-def inner_kernel(kup, kown, kdown, cup, cown, cdown, part_ref, lines, cells, bands):
-    reverse_lines(kup, kown, kdown, lines)
-    at = 0
-    for ref in (cup, cown, cdown):
-        for row in range(ref.shape[0]):
-            cells[at : at + HALF, :] = ref[row, HALF:, :]
-            cells[at + HALF : at + COLS, :] = ref[row, :HALF, :]
-            at += COLS
+def inner_kernel(up_ref, lines_own, down_ref, own_ref, part_ref, lines, cells, bands):
+    gather_lines(up_ref, lines_own, down_ref, lines)
+    for row in range(EXT):
+        if row < RAD:
+            one = up_ref[row * COLS : (row + 1) * COLS, :]
+        elif row < RAD + ROWS:
+            one = own_ref[row - RAD]
+        else:
+            at = (row - RAD - ROWS) * COLS
+            one = down_ref[at : at + COLS, :]
+        cells[row * COLS : row * COLS + HALF, :] = one[HALF:]
+        cells[row * COLS + HALF : (row + 1) * COLS, :] = one[:HALF]
     mask = own_mask().astype(jnp.bfloat16)
     for l in range(ROWS):
         band = bands.at[l % 2]
@@ -80,10 +122,10 @@
 
 
 def outer_kernel(
-    scale, kup, kown, kdown, left, right, part_ref, field_t, mixing, grad_ref, gw_ref,
+    scale, up_ref, lines_own, down_ref, left, right, part_ref, field_t, mixing, grad_ref, gw_ref,
     lines, cells, bands, spreads,
 ):
-    reverse_lines(kup, kown, kdown, lines)
+    gather_lines(up_ref, lines_own, down_ref, lines)
     for row in range(EXT):
         cells[row * COLS : row * COLS + HALF, :] = left[row]
         cells[row * COLS + HALF : (row + 1) * COLS, :] = right[row]
@@ -119,26 +161,26 @@
     sizes = {a: lax.axis_size(a) for a in LAT_AXES + LON_AXES}
     lat_count = sizes["yh"] * sizes["z"]
     lon_count = sizes["yl"] * sizes["x"] * sizes["core"]
-    offsets = jnp.arange(2 * HALF, dtype=jnp.int32) - HALF
-    inside = (offsets >= bounds[0][:, :, None]) & (offsets <= bounds[1][:, :, None])
-    kernel = jnp.where(inside[None], kernel_values, jnp.zeros_like(kernel_values))
-    kernel = kernel.astype(jnp.bfloat16)
-    lines = jnp.swapaxes(kernel, 0, 1).reshape(ROWS, LINES, COLS)
-
-    kup = shifted(lines[ROWS - RAD :], LAT_AXES, 1, False)
-    kdown = shifted(lines[:RAD], LAT_AXES, -1, False)
-    cup = shifted(cotangent[ROWS - RAD :], LAT_AXES, 1, False)
-    cdown = shifted(cotangent[:RAD], LAT_AXES, -1, False)
-    kargs = (
-        kup.reshape(RAD * LINES, COLS),
-        lines.reshape(ROWS * LINES, COLS),
-        kdown.reshape(RAD * LINES, COLS),
-    )
-    tall = jnp.concatenate([cup, cotangent, cdown], axis=0)
-    left = shifted(tall[:, HALF:], LON_AXES, 1, True)
-    right = shifted(tall[:, :HALF], LON_AXES, -1, True)
-
-    params = pltpu.CompilerParams(vmem_limit_bytes=48 * 1024 * 1024)
+    params = pltpu.CompilerParams(vmem_limit_bytes=24 * 1024 * 1024)
+    vmem = pl.BlockSpec(memory_space=pltpu.VMEM)
+    packed = jax.ShapeDtypeStruct((PACKED, CH), jnp.bfloat16)
+    up, down, lines_own = pl.pallas_call(
+        prep_kernel,
+        out_shape=(packed, packed, jax.ShapeDtypeStruct((192, COLS), jnp.float32)),
+        in_specs=[pl.BlockSpec(memory_space=pltpu.SMEM), vmem, vmem],
+        scratch_shapes=[pltpu.VMEM((192, COLS), jnp.float32)],
+        compiler_params=params,
+        name="prep",
+    )(bounds, jnp.transpose(kernel_values, (1, 2, 0, 3)), cotangent)
+    up = shifted(up, LAT_AXES, 1, False)
+    down = shifted(down, LAT_AXES, -1, False)
+    side = jax.ShapeDtypeStruct((EXT, HALF, CH), jnp.bfloat16)
+    east, west = pl.pallas_call(
+        middle_kernel, out_shape=(side, side), compiler_params=params, name="middle"
+    )(up, cotangent, down)
+    left = shifted(east, LON_AXES, 1, True)
+    right = shifted(west, LON_AXES, -1, True)
+
     scratch = [
         pltpu.VMEM((EXT * LINES, COLS), jnp.float32),
         pltpu.VMEM((EXT * COLS, CH), jnp.bfloat16),
@@ -154,7 +196,7 @@
             flops=band_flops, bytes_accessed=4 * 1024 * 1024, transcendentals=0
         ),
         name="inner_band",
-    )(*kargs, cup, cotangent, cdown)
+    )(up, lines_own, down, cotangent)
 
     field_t = field.reshape(ROWS * COLS, CH).T
     mixing = jnp.swapaxes(weight.reshape(NK, CH, CH), 1, 2).reshape(NK * CH, CH)
@@ -171,7 +213,7 @@
             flops=band_flops * 2, bytes_accessed=6 * 1024 * 1024, transcendentals=0
         ),
         name="outer_band",
-    )(*kargs, left, right, part, field_t, mixing)
+    )(up, lines_own, down, left, right, part, field_t, mixing)
 
     plane, depth = sizes["yh"] * lon_count, sizes["z"]
     piece = gw.shape[0] // plane

time: 120 us -> 109 us (0.908)
  starting transfers between devices: 23.3 us -> 14.5 us
  blocking collectives: 73 us -> 68.4 us
  waiting for transfers between devices: 4.62 us -> 7.17 us
    ppermute x6 -> x4, starting transfers between devices: 23.3 us -> 14.5 us  [shifted(): return lax.ppermute(x, axes, pairs)]
    all_to_all x3, blocking collectives: 73 us -> 68.4 us  [exchange(): return lax.all_to_all(x, axes, 0, 0, tiled=True)]
    slice x6 -> x0, local copies, waits for them, and re-layouts: 3.51 us -> none  [the longest x1 1.12 us: per_device(): cdown = shifted(cotangent[:RAD], LAT_AXES, -1, False)]
    unnamed x10 -> x13, local copies, waits for them, and re-layouts: 1.04 us -> 4.42 us
    ppermute x6 -> x4, waiting for transfers between devices: 4.62 us -> 7.17 us  [shifted(): return lax.ppermute(x, axes, pairs)]
    ppermute x2 -> x0, local copies, waits for them, and re-layouts: 1.55 us -> none  [shifted(): return lax.ppermute(x, axes, pairs)]
  transfers between devices with their start and end apart: 6 -> 4, of which waited for: 2 -> 3; matrix products, arithmetic and copies ran while one was open for 4% -> 2% of each run, Pallas kernels for 3% -> 3%
where the time goes in v2:
time: 109 us
  blocking collectives  68.4 us (63%)
  starting transfers between devices  14.5 us (13%)
  Pallas kernels  10 us (9%)
  waiting for transfers between devices  7.17 us (7%)
  local copies, waits for them, and re-layouts  6.91 us (6%)
  other arithmetic  1.21 us (1%)
    all_to_all x3, blocking collectives, exchange(): return lax.all_to_all(x, axes, 0, 0, tiled=True)  68.4 us
    ppermute x4, starting transfers between devices, shifted(): return lax.ppermute(x, axes, pairs)  14.5 us
    ppermute x4, waiting for transfers between devices, shifted(): return lax.ppermute(x, axes, pairs)  7.17 us
    pallas_call x1, Pallas kernels, per_device(): pl.pallas_call(functools.partial(outer_kernel, scale), out_shape=(jax.Sha...  5.66 us
    unnamed x13, local copies, waits for them, and re-layouts  4.42 us
    pallas_call x1, Pallas kernels, per_device(): pl.pallas_call(inner_kernel, out_shape=jax.ShapeDtypeStruct((ROWS, NK * C...  3.42 us
  transfers between devices with their start and end apart: 4, of which 3 were waited for; matrix products, arithmetic and copies ran while one was open for 2% of the time, Pallas kernels for 3%

profile of v2, /device:TPU:1, one launch (start us, length us, event | category | flops | bytes accessed | tf_op | source)
XLA Modules:
  0.0 108.9 jit_solution(329246999605151740)
XLA Ops:
  0.6 0.7 copy.13.bounds_ref
  1.3 0.0 copy-start
  1.3 1.0 copy-done
  2.3 0.0 copy-start.3
  2.3 0.9 copy-done.3
  3.2 0.0 copy-start.2
  3.2 0.9 prep.1
  4.1 4.4 %collective-permute-start = (bf16[592,256]{1,0:T(8,128)(2,1)S(1)}, bf16[592,256]{1,0:T(8,128)(2,1)S(1)}, u32[]{:S(2)}, u32[]{:S(2)}) collective-permute-start(bf16[592,256]{1,0:T(8,128)(2,1)S(1)} %get-tuple-element.9), channel_id=1, source_target_pairs={{0,16},{16,32},{32,48},{48,64},{64,80},{80,96},{96,112},{112,128},... | collective-permute-start | bytes 909320 | tf_op jit(solution)/shard_map/ppermute | solution.py:30
  8.5 1.3 %collective-permute-start.1 = (bf16[592,256]{1,0:T(8,128)(2,1)S(1)}, bf16[592,256]{1,0:T(8,128)(2,1)S(1)}, u32[]{:S(2)}, u32[]{:S(2)}) collective-permute-start(bf16[592,256]{1,0:T(8,128)(2,1)S(1)} %get-tuple-element.11), channel_id=1, source_target_pairs={{16,0},{32,16},{48,32},{64,48},{80,64},{96,80},{112,96},{128,112},... | collective-permute-start | bytes 909320 | tf_op jit(solution)/shard_map/ppermute | solution.py:30
  9.8 2.4 %collective-permute-done.up_ref = bf16[592,256]{1,0:T(8,128)(2,1)S(1)} collective-permute-done((bf16[592,256]{1,0:T(8,128)(2,1)S(1)}, bf16[592,256]{1,0:T(8,128)(2,1)S(1)}, u32[]{:S(2)}, u32[]{:S(2)}) %collective-permute-start) | collective-permute-done | bytes 303136 | tf_op jit(solution)/shard_map/ppermute | solution.py:30
  12.2 4.0 %collective-permute-done.1.down_ref = bf16[592,256]{1,0:T(8,128)(2,1)S(1)} collective-permute-done((bf16[592,256]{1,0:T(8,128)(2,1)S(1)}, bf16[592,256]{1,0:T(8,128)(2,1)S(1)}, u32[]{:S(2)}, u32[]{:S(2)}) %collective-permute-start.1) | collective-permute-done | bytes 303136 | tf_op jit(solution)/shard_map/ppermute | solution.py:30
  16.2 0.0 copy-start.1
  16.2 1.0 copy-done.1
  17.1 0.1 middle.1
  17.2 6.9 %collective-permute-start.2 = (bf16[13,64,256]{2,1,0:T(8,128)(2,1)S(1)}, bf16[13,64,256]{2,1,0:T(8,128)(2,1)S(1)}, u32[]{:S(2)}, u32[]{:S(2)}) collective-permute-start(bf16[13,64,256]{2,1,0:T(8,128)(2,1)S(1)} %get-tuple-element.12), channel_id=1, source_target_pairs={{0,1},{1,2},{2,3},{3,4},{4,5},{5,6},{6,7},{7,8},{8,9},{9,10},{10,1... | collective-permute-start | bytes 1277960 | tf_op jit(solution)/shard_map/ppermute | solution.py:30
  24.2 1.9 %collective-permute-start.3 = (bf16[13,64,256]{2,1,0:T(8,128)(2,1)S(1)}, bf16[13,64,256]{2,1,0:T(8,128)(2,1)S(1)}, u32[]{:S(2)}, u32[]{:S(2)}) collective-permute-start(bf16[13,64,256]{2,1,0:T(8,128)(2,1)S(1)} %get-tuple-element.13), channel_id=1, source_target_pairs={{0,15},{1,0},{2,1},{3,2},{4,3},{5,4},{6,5},{7,6},{8,7},{9,8},{10,9... | collective-permute-start | bytes 1277960 | tf_op jit(solution)/shard_map/ppermute | solution.py:30
  26.1 0.0 copy-done.4
  26.1 1.2 %copy.14 = bf16[640,256]{0,1:T(8,128)(2,1)S(1)} copy(bf16[640,256]{1,0:T(8,128)(2,1)} %bitcast.16) | data formatting | bytes 655360 | tf_op jit(solution)/shard_map/reshape | solution.py:201
  27.3 1.2 %copy.15 = bf16[4,256,256]{1,2,0:T(8,128)(2,1)S(1)} copy(bf16[4,256,256]{2,1,0:T(8,128)(2,1)} %bitcast.15) | data formatting | bytes 1048576 | tf_op jit(solution)/shard_map/reshape | solution.py:202
  28.5 0.0 copy-done.2
  28.5 0.0 copy-start.5
  28.5 0.9 copy-done.5
  29.4 3.4 %inner_band.1.part_ref = f32[5,512,256]{2,1,0:T(8,128)S(1)} custom-call(bf16[592,256]{1,0:T(8,128)(2,1)S(1)} %collective-permute-done.up_ref, f32[192,128]{1,0:T(8,128)S(1)} %copy-done.5, bf16[592,256]{1,0:T(8,128)(2,1)S(1)} %collective-permute-done.1.down_ref, bf16[5,128,256]{2,1,0:T(8,128)(2,1)S(1)} %copy-done.2), custom_call_target="tpu_custom_call" | custom-call | flops 1509949440 | bytes 4194304 | tf_op jit(solution)/shard_map/inner_band/pallas_call | solution.py:190
  32.9 0.0 collective-permute-done.2.left
  32.9 0.7 collective-permute-done.3.right
  33.6 5.7 %outer_band.1 = (f32[5,128,256]{2,1,0:T(8,128)}, bf16[1024,256]{1,0:T(8,128)(2,1)S(1)}) custom-call(bf16[592,256]{1,0:T(8,128)(2,1)S(1)} %collective-permute-done.up_ref, f32[192,128]{1,0:T(8,128)S(1)} %copy-done.5, bf16[592,256]{1,0:T(8,128)(2,1)S(1)} %collective-permute-done.1.down_ref, bf16[13,64,256]{2,1,0:T(8,128)(2,1)S(1)} %collective-permute-done.2.left, ...), custom_call_target="tpu_custom_call" | custom-call | flops 3019898880 | bytes 6291456 | tf_op jit(solution)/shard_map/outer_band/pallas_call | solution.py:204
  39.3 26.0 %all_to_all.15 = bf16[32,32,256]{2,1,0:T(8,128)(2,1)S(1)} all-to-all(bf16[32,32,256]{2,1,0:T(8,128)(2,1)S(1)} %bitcast.12), channel_id=1, replica_groups=mesh['yh'=2,'z'=16,'yl'=2,'x'=4,'core'=2] {'yh','yl','x','core'}, dimensions={0} | all-to-all | bytes 1048576 | tf_op jit(solution)/shard_map/all_to_all | solution.py:157
  65.2 0.1 reduce_sum.24
  65.3 22.3 %all_to_all.16 = bf16[16,32,256]{2,1,0:T(8,128)(2,1)S(1)} all-to-all(bf16[16,32,256]{2,1,0:T(8,128)(2,1)S(1)} %broadcast_in_dim.4), channel_id=1, replica_groups=mesh['yh'=2,'z'=16,'yl'=2,'x'=4,'core'=2] {'z'}, dimensions={0} | all-to-all | bytes 524288 | tf_op jit(solution)/shard_map/all_to_all | solution.py:157
  87.7 0.1 broadcast_in_dim.5
  87.8 20.1 %all_to_all.17 = bf16[32,32,256]{2,1,0:T(8,128)(2,1)S(1)} all-to-all(bf16[32,32,256]{2,1,0:T(8,128)(2,1)S(1)} %broadcast_in_dim.5), channel_id=1, replica_groups=mesh['yh'=2,'z'=16,'yl'=2,'x'=4,'core'=2] {'yh','yl','x','core'}, dimensions={0} | all-to-all | bytes 1048576 | tf_op jit(solution)/shard_map/all_to_all | solution.py:157
  107.8 1.1 bitcast_convert_fusion
  (3 shorter events, 0.1 us)
Async XLA Ops:
  1.3 1.0 copy-start
  2.3 0.9 copy-start.3
  3.2 25.3 %copy-start.2 = (bf16[5,128,256]{2,1,0:T(8,128)(2,1)S(1)}, bf16[5,128,256]{2,1,0:T(8,128)(2,1)}, u32[]{:S(2)}) copy-start(bf16[5,128,256]{2,1,0:T(8,128)(2,1)} %own_ref.3) | copy-start | bytes 983044
  4.0 22.0 %copy-start.4 = (f32[192,128]{1,0:T(8,128)}, f32[192,128]{1,0:T(8,128)S(1)}, u32[]{:S(2)}) copy-start(f32[192,128]{1,0:T(8,128)S(1)} %get-tuple-element.10.lines_own) | copy-start | bytes 294916
  4.1 8.1 %collective-permute-start = (bf16[592,256]{1,0:T(8,128)(2,1)S(1)}, bf16[592,256]{1,0:T(8,128)(2,1)S(1)}, u32[]{:S(2)}, u32[]{:S(2)}) collective-permute-start(bf16[592,256]{1,0:T(8,128)(2,1)S(1)} %get-tuple-element.9), channel_id=1, source_target_pairs={{0,16},{16,32},{32,48},{48,64},{64,80},{80,96},{96,112},{112,128},... | collective-permute-start | bytes 909320 | tf_op jit(solution)/shard_map/ppermute | solution.py:30
  8.5 7.7 %collective-permute-start.1 = (bf16[592,256]{1,0:T(8,128)(2,1)S(1)}, bf16[592,256]{1,0:T(8,128)(2,1)S(1)}, u32[]{:S(2)}, u32[]{:S(2)}) collective-permute-start(bf16[592,256]{1,0:T(8,128)(2,1)S(1)} %get-tuple-element.11), channel_id=1, source_target_pairs={{16,0},{32,16},{48,32},{64,48},{80,64},{96,80},{112,96},{128,112},... | collective-permute-start | bytes 909320 | tf_op jit(solution)/shard_map/ppermute | solution.py:30
  16.2 1.0 copy-start.1
  17.2 15.6 %collective-permute-start.2 = (bf16[13,64,256]{2,1,0:T(8,128)(2,1)S(1)}, bf16[13,64,256]{2,1,0:T(8,128)(2,1)S(1)}, u32[]{:S(2)}, u32[]{:S(2)}) collective-permute-start(bf16[13,64,256]{2,1,0:T(8,128)(2,1)S(1)} %get-tuple-element.12), channel_id=1, source_target_pairs={{0,1},{1,2},{2,3},{3,4},{4,5},{5,6},{6,7},{7,8},{8,9},{9,10},{10,1... | collective-permute-start | bytes 1277960 | tf_op jit(solution)/shard_map/ppermute | solution.py:30
  24.2 9.4 %collective-permute-start.3 = (bf16[13,64,256]{2,1,0:T(8,128)(2,1)S(1)}, bf16[13,64,256]{2,1,0:T(8,128)(2,1)S(1)}, u32[]{:S(2)}, u32[]{:S(2)}) collective-permute-start(bf16[13,64,256]{2,1,0:T(8,128)(2,1)S(1)} %get-tuple-element.13), channel_id=1, source_target_pairs={{0,15},{1,0},{2,1},{3,2},{4,3},{5,4},{6,5},{7,6},{8,7},{9,8},{10,9... | collective-permute-start | bytes 1277960 | tf_op jit(solution)/shard_map/ppermute | solution.py:30
  28.5 0.9 copy-start.5

commit v3 on v2

v3 whole, which is shorter than its diff:
```python
import functools
import math

import jax
import jax.numpy as jnp
from jax import lax
from jax.experimental import pallas as pl
from jax.experimental.pallas import tpu as pltpu
from jax.sharding import Mesh, PartitionSpec as P

LAT_AXES = ("yh", "z")
LON_AXES = ("yl", "x", "core")
PLANE = ("yh", "yl", "x", "core")

ROWS, COLS, CH, NK, NR, RAD, HALF = 5, 128, 256, 4, 9, 4, 64
EXT = ROWS + 2 * RAD
LINES = NK * NR
LINES_ROWS = RAD * LINES // 2
PACKED = RAD * COLS + 80
VMEM_LIMIT = 32 * 1024 * 1024


def shifted(x, axes, step, closed):
    count = 1
    for a in axes:
        count *= lax.axis_size(a)
    if closed:
        pairs = [(i, (i + step) % count) for i in range(count)]
    else:
        pairs = [(i, i + step) for i in range(count) if 0 <= i + step < count]
    return lax.ppermute(x, axes, pairs)


def prep_kernel(
    bounds_hbm, values_hbm, cells_hbm, up_ref, down_ref, own_ref, bounds, values, lines, sems
):
    cell_rows = RAD * COLS
    copies = [
        pltpu.make_async_copy(bounds_hbm, bounds, sems.at[0]),
        pltpu.make_async_copy(values_hbm, values, sems.at[1]),
        pltpu.make_async_copy(
            cells_hbm.at[pl.ds((ROWS - RAD) * COLS, cell_rows)],
            up_ref.at[pl.ds(0, cell_rows)],
            sems.at[2],
        ),
        pltpu.make_async_copy(
            cells_hbm.at[pl.ds(0, cell_rows)], down_ref.at[pl.ds(0, cell_rows)], sems.at[3]
        ),
    ]
    for copy in copies:
        copy.start()
    copies[0].wait()
    copies[1].wait()
    offset = lax.broadcasted_iota(jnp.int32, (NK, COLS), 1) - HALF
    for l in range(ROWS):
        for r in range(NR):
            inside = (offset >= bounds[l, 0, r]) & (offset <= bounds[l, 1, r])
            at = LINES * l + NK * r
            lines[at : at + NK, :] = jnp.where(inside, values[l, r], 0.0)
    lines[ROWS * LINES :, :] = jnp.zeros((192 - ROWS * LINES, COLS), jnp.float32)
    i = lax.broadcasted_iota(jnp.int32, (COLS, COLS), 0)
    j = lax.broadcasted_iota(jnp.int32, (COLS, COLS), 1)
    flip = ((i + j == 0) | (i + j == COLS)).astype(jnp.bfloat16)
    own_ref[...] = jnp.dot(
        lines[...].astype(jnp.bfloat16), flip, preferred_element_type=jnp.float32
    )
    for ref, row in ((up_ref, ROWS - RAD), (down_ref, 0)):
        for half in range(2):
            at = LINES * row + half * LINES_ROWS
            ref[cell_rows : cell_rows + LINES_ROWS, half * COLS : (half + 1) * COLS] = own_ref[
                at : at + LINES_ROWS, :
            ].astype(jnp.bfloat16)
        ref[cell_rows + LINES_ROWS :, :] = jnp.zeros(
            (PACKED - cell_rows - LINES_ROWS, CH), jnp.bfloat16
        )
    copies[2].wait()
    copies[3].wait()


def rows_in_reach(up_ref, up_own, down_own, down_ref):
    for n in range(RAD):
        yield up_ref[n * COLS : (n + 1) * COLS, :]
    yield down_own[:COLS, :]
    for ref in (up_own, down_ref):
        for n in range(RAD):
            yield ref[n * COLS : (n + 1) * COLS, :]


def middle_kernel(up_ref, up_own, down_own, down_ref, east_ref, west_ref):
    for row, cells in enumerate(rows_in_reach(up_ref, up_own, down_own, down_ref)):
        east_ref[row] = cells[HALF:]
        west_ref[row] = cells[:HALF]


def gather_lines(up_ref, own_ref, down_ref, lines_ref):
    for ref, at in ((up_ref, 0), (down_ref, (RAD + ROWS) * LINES)):
        for half in range(2):
            lines_ref[at + half * LINES_ROWS : at + (half + 1) * LINES_ROWS, :] = ref[
                RAD * COLS : RAD * COLS + LINES_ROWS, half * COLS : (half + 1) * COLS
            ].astype(jnp.float32)
    lines_ref[RAD * LINES : (RAD + ROWS) * LINES, :] = own_ref[: ROWS * LINES, :]


def own_mask():
    n = lax.broadcasted_iota(jnp.int32, (COLS, COLS), 0)
    i = lax.broadcasted_iota(jnp.int32, (COLS, COLS), 1)
    return ((i >= HALF) & (i > n)) | ((i < HALF) & (i <= n))


def fill_bands(inner_ref, outer_ref, lines_ref, inner_mask, outer_mask, l):
    for k in range(NK):
        for s in range(NR):
            at = LINES * (l + s) + NK * (NR - 1 - s) + k
            row = jnp.broadcast_to(lines_ref[pl.ds(at, 1), :], (16, COLS))
            base = pltpu.roll(row, 0, 1, stride=1, stride_axis=0).astype(jnp.bfloat16)
            for g in range(COLS // 16):
                tile = base if g == 0 else pltpu.roll(base, 16 * g, 1)
                rows = slice(k * COLS + 16 * g, k * COLS + 16 * (g + 1))
                cols = slice(s * COLS, (s + 1) * COLS)
                inner_ref[rows, cols] = tile * inner_mask[16 * g : 16 * (g + 1), :]
                outer_ref[rows, cols] = tile * outer_mask[16 * g : 16 * (g + 1), :]


def inner_kernel(
    up_ref, up_own, down_own, down_ref, lines_own, part_ref, outer_ref, lines, cells, bands
):
    gather_lines(up_ref, lines_own, down_ref, lines)
    for row, one in enumerate(rows_in_reach(up_ref, up_own, down_own, down_ref)):
        cells[row * COLS : row * COLS + HALF, :] = one[HALF:]
        cells[row * COLS + HALF : (row + 1) * COLS, :] = one[:HALF]
    mask = own_mask().astype(jnp.float32)
    inner_mask, outer_mask = mask.astype(jnp.bfloat16), (1.0 - mask).astype(jnp.bfloat16)
    for l in range(ROWS):
        band = bands.at[l % 2]
        fill_bands(band, outer_ref.at[l], lines, inner_mask, outer_mask, l)
        part_ref[l] = jnp.dot(
            band[...],
            cells[l * COLS : (l + NR) * COLS, :],
            preferred_element_type=jnp.float32,
        )


def outer_kernel(
    scale, bands, left, right, part_ref, field_t, mixing, grad_ref, gw_ref, cells, spreads
):
    for row in range(EXT):
        cells[row * COLS : row * COLS + HALF, :] = left[row]
        cells[row * COLS + HALF : (row + 1) * COLS, :] = right[row]
    for l in range(ROWS):
        spread = part_ref[l] + jnp.dot(
            bands[l],
            cells[l * COLS : (l + NR) * COLS, :],
            preferred_element_type=jnp.float32,
        )
        spread = spread.astype(jnp.bfloat16)
        grad = jnp.zeros((COLS, CH), jnp.float32)
        for k in range(NK):
            one = spread[k * COLS : (k + 1) * COLS, :]
            spreads[k, l * COLS : (l + 1) * COLS, :] = one
            grad += jnp.dot(
                one, mixing[k * CH : (k + 1) * CH, :], preferred_element_type=jnp.float32
            )
        grad_ref[l] = grad
    for k in range(NK):
        total = jnp.dot(field_t[...], spreads[k], preferred_element_type=jnp.float32)
        gw_ref[k * CH : (k + 1) * CH, :] = (total * scale).astype(jnp.bfloat16)


def exchange(x, axes):
    return lax.all_to_all(x, axes, 0, 0, tiled=True)


def per_device(field, cotangent, kernel_values, bounds, weight):
    sizes = {a: lax.axis_size(a) for a in LAT_AXES + LON_AXES}
    lat_count = math.prod(sizes[a] for a in LAT_AXES)
    lon_count = math.prod(sizes[a] for a in LON_AXES)
    params = pltpu.CompilerParams(vmem_limit_bytes=VMEM_LIMIT)
    hbm = pl.BlockSpec(memory_space=pltpu.HBM)
    packed = jax.ShapeDtypeStruct((PACKED, CH), jnp.bfloat16)
    up_own, down_own, lines_own = pl.pallas_call(
        prep_kernel,
        out_shape=(packed, packed, jax.ShapeDtypeStruct((192, COLS), jnp.float32)),
        in_specs=[hbm, hbm, hbm],
        scratch_shapes=[
            pltpu.SMEM((ROWS, 2, NR), jnp.int32),
            pltpu.VMEM((ROWS, NR, NK, COLS), jnp.float32),
            pltpu.VMEM((192, COLS), jnp.float32),
            pltpu.SemaphoreType.DMA((4,)),
        ],
        compiler_params=pltpu.CompilerParams(vmem_limit_bytes=60 * 1024 * 1024),
        name="prep",
    )(
        jnp.transpose(bounds, (1, 0, 2)),
        jnp.transpose(kernel_values, (1, 2, 0, 3)),
        cotangent.reshape(ROWS * COLS, CH),
    )
    field_t = field.reshape(ROWS * COLS, CH).T
    mixing = jnp.swapaxes(weight.reshape(NK, CH, CH), 1, 2).reshape(NK * CH, CH)
    up = shifted(up_own, LAT_AXES, 1, False)
    down = shifted(down_own, LAT_AXES, -1, False)
    up, down, field_t, mixing = lax.optimization_barrier((up, down, field_t, mixing))
    side = jax.ShapeDtypeStruct((EXT, HALF, CH), jnp.bfloat16)
    east, west = pl.pallas_call(
        middle_kernel, out_shape=(side, side), compiler_params=params, name="middle"
    )(up, up_own, down_own, down)
    left = shifted(east, LON_AXES, 1, True)
    right = shifted(west, LON_AXES, -1, True)

    cells = pltpu.VMEM((EXT * COLS, CH), jnp.bfloat16)
    band_flops = 2 * ROWS * NK * COLS * NR * COLS * CH
    part, bands = pl.pallas_call(
        inner_kernel,
        out_shape=(
            jax.ShapeDtypeStruct((ROWS, NK * COLS, CH), jnp.float32),
            jax.ShapeDtypeStruct((ROWS, NK * COLS, NR * COLS), jnp.bfloat16),
        ),
        scratch_shapes=[
            pltpu.VMEM((EXT * LINES, COLS), jnp.float32),
            cells,
            pltpu.VMEM((2, NK * COLS, NR * COLS), jnp.bfloat16),
        ],
        compiler_params=params,
        cost_estimate=pl.CostEstimate(
            flops=band_flops, bytes_accessed=4 * 1024 * 1024, transcendentals=0
        ),
        name="inner_band",
    )(up, up_own, down_own, down, lines_own)

    scale = 1.0 / math.sqrt(ROWS * lat_count * COLS * lon_count)
    grad_field, gw = pl.pallas_call(
        functools.partial(outer_kernel, scale),
        out_shape=(
            jax.ShapeDtypeStruct((ROWS, COLS, CH), jnp.float32),
            jax.ShapeDtypeStruct((NK * CH, CH), jnp.bfloat16),
        ),
        scratch_shapes=[cells, pltpu.VMEM((NK, ROWS * COLS, CH), jnp.bfloat16)],
        compiler_params=params,
        cost_estimate=pl.CostEstimate(
            flops=band_flops * 2, bytes_accessed=6 * 1024 * 1024, transcendentals=0
        ),
        name="outer_band",
    )(bands, left, right, part, field_t, mixing)

    plane, depth = sizes["yh"] * lon_count, lat_count // sizes["yh"]
    piece = gw.shape[0] // plane
    got = exchange(gw.reshape(plane, piece, CH), PLANE)
    mine = jnp.sum(got.astype(jnp.float32), axis=0)
    got = exchange(jnp.broadcast_to(mine[None], (depth, piece, CH)), "z")
    mine = jnp.sum(got, axis=0).astype(jnp.bfloat16)
    got = exchange(jnp.broadcast_to(mine[None], (plane, piece, CH)), PLANE)
    return (grad_field, got.reshape(NK * CH, CH).astype(jnp.float32))


def solution(mesh):
    fine = Mesh(mesh.devices.reshape(2, 16, 2, 4, 2), LAT_AXES + LON_AXES)
    return jax.shard_map(
        per_device,
        mesh=fine,
        in_specs=(
            P(LAT_AXES, LON_AXES, None),
            P(LAT_AXES, LON_AXES, None),
            P(None, LAT_AXES, None, None),
            P(None, LAT_AXES, None),
            P(),
        ),
        out_specs=(P(LAT_AXES, LON_AXES, None), P()),
        check_vma=False,
    )
```

time: 109 us -> 119 us (1.092)
  blocking collectives: 68.4 us -> 78.9 us
  local copies, waits for them, and re-layouts: 6.91 us -> 5.33 us
    all_to_all x3, blocking collectives: 68.4 us -> 78.9 us  [exchange(): return lax.all_to_all(x, axes, 0, 0, tiled=True)]
    unnamed x13 -> x6, local copies, waits for them, and re-layouts: 4.42 us -> 2.81 us
where the time goes in v3:
time: 119 us
  blocking collectives  78.9 us (66%)
  starting transfers between devices  14.5 us (12%)
  Pallas kernels  10.7 us (9%)
  waiting for transfers between devices  7.3 us (6%)
  local copies, waits for them, and re-layouts  5.33 us (4%)
  other arithmetic  1.2 us (1%)
    all_to_all x3, blocking collectives, exchange(): return lax.all_to_all(x, axes, 0, 0, tiled=True)  78.9 us
    ppermute x4, starting transfers between devices, shifted(): return lax.ppermute(x, axes, pairs)  14.5 us
    ppermute x4, waiting for transfers between devices, shifted(): return lax.ppermute(x, axes, pairs)  7.3 us
    pallas_call x1, Pallas kernels, per_device(): pl.pallas_call(functools.partial(outer_kernel, scale), out_shape=(jax.Sha...  5.13 us
    pallas_call x1, Pallas kernels, per_device(): pl.pallas_call(inner_kernel, out_shape=(jax.ShapeDtypeStruct((ROWS, NK *...  3.52 us
    unnamed x6, local copies, waits for them, and re-layouts  2.81 us
  transfers between devices with their start and end apart: 4, of which 3 were waited for; matrix products, arithmetic and copies ran while one was open for 2% of the time, Pallas kernels for 3%

profile of v3, /device:TPU:1, one launch (start us, length us, event | category | flops | bytes accessed | tf_op | source)
XLA Modules:
  0.0 118.7 jit_solution(13907711843232823164)
XLA Ops:
  0.6 1.9 %prep.1 = (bf16[592,256]{1,0:T(8,128)(2,1)}, bf16[592,256]{1,0:T(8,128)(2,1)}, f32[192,128]{1,0:T(8,128)}) custom-call(s32[5,2,9]{2,1,0:T(2,128)} %bitcast.20, f32[5,9,4,128]{3,2,1,0:T(4,128)} %bitcast.19, bf16[640,256]{1,0:T(8,128)(2,1)} %bitcast.17), custom_call_target="tpu_custom_call" | custom-call | tf_op jit(solution)/shard_map/prep/pallas_call | solution.py:180
  2.6 4.4 %collective-permute-start = (bf16[592,256]{1,0:T(8,128)(2,1)}, bf16[592,256]{1,0:T(8,128)(2,1)S(1)}, u32[]{:S(2)}, u32[]{:S(2)}) collective-permute-start(bf16[592,256]{1,0:T(8,128)(2,1)} %get-tuple-element.15.up_own), channel_id=1, source_target_pairs={{0,16},{16,32},{32,48},{48,64},{64,80},{80,96},{96,112},{112,128},... | collective-permute-start | bytes 909320 | tf_op jit(solution)/shard_map/ppermute | solution.py:31
  7.0 1.3 %collective-permute-start.1 = (bf16[592,256]{1,0:T(8,128)(2,1)}, bf16[592,256]{1,0:T(8,128)(2,1)S(1)}, u32[]{:S(2)}, u32[]{:S(2)}) collective-permute-start(bf16[592,256]{1,0:T(8,128)(2,1)} %get-tuple-element.16.down_own), channel_id=1, source_target_pairs={{16,0},{32,16},{48,32},{64,48},{80,64},{96,80},{112,96},{128,112},... | collective-permute-start | bytes 909320 | tf_op jit(solution)/shard_map/ppermute | solution.py:31
  8.3 1.2 %copy.12 = bf16[4,256,256]{1,2,0:T(8,128)(2,1)S(1)} copy(bf16[4,256,256]{2,1,0:T(8,128)(2,1)} %bitcast.16) | data formatting | bytes 1048576 | tf_op jit(solution)/shard_map/reshape | solution.py:198
  9.5 1.2 copy.11
  10.7 0.3 collective-permute-done.up_ref
  11.0 3.9 %collective-permute-done.1.down_ref = bf16[592,256]{1,0:T(8,128)(2,1)S(1)} collective-permute-done((bf16[592,256]{1,0:T(8,128)(2,1)}, bf16[592,256]{1,0:T(8,128)(2,1)S(1)}, u32[]{:S(2)}, u32[]{:S(2)}) %collective-permute-start.1) | collective-permute-done | bytes 303136 | tf_op jit(solution)/shard_map/ppermute | solution.py:31
  14.9 0.0 copy-start
  14.9 1.0 copy-done
  15.9 0.0 copy-start.1
  15.9 1.0 copy-done.1
  16.8 0.1 middle.1
  16.9 6.9 %collective-permute-start.2 = (bf16[13,64,256]{2,1,0:T(8,128)(2,1)S(1)}, bf16[13,64,256]{2,1,0:T(8,128)(2,1)S(1)}, u32[]{:S(2)}, u32[]{:S(2)}) collective-permute-start(bf16[13,64,256]{2,1,0:T(8,128)(2,1)S(1)} %get-tuple-element.21), channel_id=1, source_target_pairs={{0,1},{1,2},{2,3},{3,4},{4,5},{5,6},{6,7},{7,8},{8,9},{9,10},{10,1... | collective-permute-start | bytes 1277960 | tf_op jit(solution)/shard_map/ppermute | solution.py:31
  23.9 1.9 %collective-permute-start.3 = (bf16[13,64,256]{2,1,0:T(8,128)(2,1)S(1)}, bf16[13,64,256]{2,1,0:T(8,128)(2,1)S(1)}, u32[]{:S(2)}, u32[]{:S(2)}) collective-permute-start(bf16[13,64,256]{2,1,0:T(8,128)(2,1)S(1)} %get-tuple-element.22), channel_id=1, source_target_pairs={{0,15},{1,0},{2,1},{3,2},{4,3},{5,4},{6,5},{7,6},{8,7},{9,8},{10,9... | collective-permute-start | bytes 1277960 | tf_op jit(solution)/shard_map/ppermute | solution.py:31
  25.8 0.0 copy-start.2
  25.8 0.9 copy-done.2
  26.7 3.5 %inner_band.1 = (f32[5,512,256]{2,1,0:T(8,128)S(1)}, bf16[5,512,1152]{2,1,0:T(8,128)(2,1)S(1)}) custom-call(bf16[592,256]{1,0:T(8,128)(2,1)S(1)} %collective-permute-done.up_ref, bf16[592,256]{1,0:T(8,128)(2,1)S(1)} %copy-done, bf16[592,256]{1,0:T(8,128)(2,1)S(1)} %copy-done.1, bf16[592,256]{1,0:T(8,128)(2,1)S(1)} %collective-permute-done.1.down_ref, ...), custom_call_target="tpu_custom_call" | custom-call | flops 1509949440 | bytes 4194304 | tf_op jit(solution)/shard_map/inner_band/pallas_call | solution.py:211
  30.2 0.0 collective-permute-done.2.left
  30.2 3.1 %collective-permute-done.3.right = bf16[13,64,256]{2,1,0:T(8,128)(2,1)S(1)} collective-permute-done((bf16[13,64,256]{2,1,0:T(8,128)(2,1)S(1)}, bf16[13,64,256]{2,1,0:T(8,128)(2,1)S(1)}, u32[]{:S(2)}, u32[]{:S(2)}) %collective-permute-start.3) | collective-permute-done | bytes 426016 | tf_op jit(solution)/shard_map/ppermute | solution.py:31
  33.3 5.1 %outer_band.1 = (f32[5,128,256]{2,1,0:T(8,128)}, bf16[1024,256]{1,0:T(8,128)(2,1)S(1)}) custom-call(bf16[5,512,1152]{2,1,0:T(8,128)(2,1)S(1)} %get-tuple-element.20.bands, bf16[13,64,256]{2,1,0:T(8,128)(2,1)S(1)} %collective-permute-done.2.left, bf16[13,64,256]{2,1,0:T(8,128)(2,1)S(1)} %collective-permute-done.3.right, ...), custom_call_target="tpu_custom_call" | custom-call | flops 3019898880 | bytes 6291456 | tf_op jit(solution)/shard_map/outer_band/pallas_call | solution.py:230
  38.4 26.1 %all_to_all.15 = bf16[32,32,256]{2,1,0:T(8,128)(2,1)S(1)} all-to-all(bf16[32,32,256]{2,1,0:T(8,128)(2,1)S(1)} %bitcast.14), channel_id=1, replica_groups=mesh['yh'=2,'z'=16,'yl'=2,'x'=4,'core'=2] {'yh','yl','x','core'}, dimensions={0} | all-to-all | bytes 1048576 | tf_op jit(solution)/shard_map/all_to_all | solution.py:170
  64.5 0.1 convert_reduce_fusion
  64.6 31.2 %all_to_all.16 = f32[16,32,256]{2,1,0:T(8,128)S(1)} all-to-all(f32[16,32,256]{2,1,0:T(8,128)S(1)} %broadcast_in_dim.4), channel_id=1, replica_groups=mesh['yh'=2,'z'=16,'yl'=2,'x'=4,'core'=2] {'z'}, dimensions={0} | all-to-all | bytes 1048576 | tf_op jit(solution)/shard_map/all_to_all | solution.py:170
  95.9 0.1 broadcast_in_dim.5
  95.9 21.7 %all_to_all.17 = bf16[32,32,256]{2,1,0:T(8,128)(2,1)S(1)} all-to-all(bf16[32,32,256]{2,1,0:T(8,128)(2,1)S(1)} %broadcast_in_dim.5), channel_id=1, replica_groups=mesh['yh'=2,'z'=16,'yl'=2,'x'=4,'core'=2] {'yh','yl','x','core'}, dimensions={0} | all-to-all | bytes 1048576 | tf_op jit(solution)/shard_map/all_to_all | solution.py:170
  117.6 1.1 bitcast_convert_fusion
  (2 shorter events, 0.1 us)
Async XLA Ops:
  2.6 8.4 %collective-permute-start = (bf16[592,256]{1,0:T(8,128)(2,1)}, bf16[592,256]{1,0:T(8,128)(2,1)S(1)}, u32[]{:S(2)}, u32[]{:S(2)}) collective-permute-start(bf16[592,256]{1,0:T(8,128)(2,1)} %get-tuple-element.15.up_own), channel_id=1, source_target_pairs={{0,16},{16,32},{32,48},{48,64},{64,80},{80,96},{96,112},{112,128},... | collective-permute-start | bytes 909320 | tf_op jit(solution)/shard_map/ppermute | solution.py:31
  7.0 7.9 %collective-permute-start.1 = (bf16[592,256]{1,0:T(8,128)(2,1)}, bf16[592,256]{1,0:T(8,128)(2,1)S(1)}, u32[]{:S(2)}, u32[]{:S(2)}) collective-permute-start(bf16[592,256]{1,0:T(8,128)(2,1)} %get-tuple-element.16.down_own), channel_id=1, source_target_pairs={{16,0},{32,16},{48,32},{64,48},{80,64},{96,80},{112,96},{128,112},... | collective-permute-start | bytes 909320 | tf_op jit(solution)/shard_map/ppermute | solution.py:31
  14.9 1.0 copy-start
  15.9 1.0 copy-start.1
  16.9 13.3 %collective-permute-start.2 = (bf16[13,64,256]{2,1,0:T(8,128)(2,1)S(1)}, bf16[13,64,256]{2,1,0:T(8,128)(2,1)S(1)}, u32[]{:S(2)}, u32[]{:S(2)}) collective-permute-start(bf16[13,64,256]{2,1,0:T(8,128)(2,1)S(1)} %get-tuple-element.21), channel_id=1, source_target_pairs={{0,1},{1,2},{2,3},{3,4},{4,5},{5,6},{6,7},{7,8},{8,9},{9,10},{10,1... | collective-permute-start | bytes 1277960 | tf_op jit(solution)/shard_map/ppermute | solution.py:31
  23.9 9.4 %collective-permute-start.3 = (bf16[13,64,256]{2,1,0:T(8,128)(2,1)S(1)}, bf16[13,64,256]{2,1,0:T(8,128)(2,1)S(1)}, u32[]{:S(2)}, u32[]{:S(2)}) collective-permute-start(bf16[13,64,256]{2,1,0:T(8,128)(2,1)S(1)} %get-tuple-element.22), channel_id=1, source_target_pairs={{0,15},{1,0},{2,1},{3,2},{4,3},{5,4},{6,5},{7,6},{8,7},{9,8},{10,9... | collective-permute-start | bytes 1277960 | tf_op jit(solution)/shard_map/ppermute | solution.py:31
  25.8 0.9 copy-start.2

commit v4 on v3

--- a/solution.py
+++ b/solution.py
@@ -77,17 +77,25 @@
     copies[3].wait()
 
 
-def rows_in_reach(up_ref, up_own, down_own, down_ref):
+def own_kernel(cells_ref, lines_ref, field_ref, weight_ref, own_ref, lines_own, field_t, mixing):
+    own_ref[...] = cells_ref[...]
+    lines_own[...] = lines_ref[...]
+    field_t[...] = field_ref[...].T
+    for k in range(NK):
+        mixing[k * CH : (k + 1) * CH, :] = weight_ref[k * CH : (k + 1) * CH, :].T
+
+
+def rows_in_reach(up_ref, own_ref, down_ref):
     for n in range(RAD):
         yield up_ref[n * COLS : (n + 1) * COLS, :]
-    yield down_own[:COLS, :]
-    for ref in (up_own, down_ref):
-        for n in range(RAD):
-            yield ref[n * COLS : (n + 1) * COLS, :]
-
-
-def middle_kernel(up_ref, up_own, down_own, down_ref, east_ref, west_ref):
-    for row, cells in enumerate(rows_in_reach(up_ref, up_own, down_own, down_ref)):
+    for n in range(ROWS):
+        yield own_ref[n]
+    for n in range(RAD):
+        yield down_ref[n * COLS : (n + 1) * COLS, :]
+
+
+def middle_kernel(up_ref, own_ref, down_ref, east_ref, west_ref):
+    for row, cells in enumerate(rows_in_reach(up_ref, own_ref, down_ref)):
         east_ref[row] = cells[HALF:]
         west_ref[row] = cells[:HALF]
 
@@ -122,10 +130,10 @@
 
 
 def inner_kernel(
-    up_ref, up_own, down_own, down_ref, lines_own, part_ref, outer_ref, lines, cells, bands
+    up_ref, own_ref, down_ref, lines_own, part_ref, outer_ref, lines, cells, bands
 ):
     gather_lines(up_ref, lines_own, down_ref, lines)
-    for row, one in enumerate(rows_in_reach(up_ref, up_own, down_own, down_ref)):
+    for row, one in enumerate(rows_in_reach(up_ref, own_ref, down_ref)):
         cells[row * COLS : row * COLS + HALF, :] = one[HALF:]
         cells[row * COLS + HALF : (row + 1) * COLS, :] = one[:HALF]
     mask = own_mask().astype(jnp.float32)
@@ -147,23 +155,19 @@
         cells[row * COLS : row * COLS + HALF, :] = left[row]
         cells[row * COLS + HALF : (row + 1) * COLS, :] = right[row]
     for l in range(ROWS):
-        spread = part_ref[l] + jnp.dot(
-            bands[l],
-            cells[l * COLS : (l + NR) * COLS, :],
-            preferred_element_type=jnp.float32,
-        )
-        spread = spread.astype(jnp.bfloat16)
-        grad = jnp.zeros((COLS, CH), jnp.float32)
+        window = cells[l * COLS : (l + NR) * COLS, :]
         for k in range(NK):
-            one = spread[k * COLS : (k + 1) * COLS, :]
-            spreads[k, l * COLS : (l + 1) * COLS, :] = one
-            grad += jnp.dot(
-                one, mixing[k * CH : (k + 1) * CH, :], preferred_element_type=jnp.float32
+            rows = slice(k * COLS, (k + 1) * COLS)
+            spread = part_ref[l, rows, :] + jnp.dot(
+                bands[l, rows, :], window, preferred_element_type=jnp.float32
             )
-        grad_ref[l] = grad
+            spreads[l * COLS : (l + 1) * COLS, k * CH : (k + 1) * CH] = spread.astype(jnp.bfloat16)
+    total = jnp.dot(field_t[...], spreads[...], preferred_element_type=jnp.float32) * scale
     for k in range(NK):
-        total = jnp.dot(field_t[...], spreads[k], preferred_element_type=jnp.float32)
-        gw_ref[k * CH : (k + 1) * CH, :] = (total * scale).astype(jnp.bfloat16)
+        gw_ref[k * CH : (k + 1) * CH, :] = total[:, k * CH : (k + 1) * CH].astype(jnp.bfloat16)
+    grad = jnp.dot(spreads[...], mixing[...], preferred_element_type=jnp.float32)
+    for l in range(ROWS):
+        grad_ref[l] = grad[l * COLS : (l + 1) * COLS, :]
 
 
 def exchange(x, axes):
@@ -194,15 +198,27 @@
         jnp.transpose(kernel_values, (1, 2, 0, 3)),
         cotangent.reshape(ROWS * COLS, CH),
     )
-    field_t = field.reshape(ROWS * COLS, CH).T
-    mixing = jnp.swapaxes(weight.reshape(NK, CH, CH), 1, 2).reshape(NK * CH, CH)
+    own, lines_own, field_t, mixing = pl.pallas_call(
+        own_kernel,
+        out_shape=(
+            jax.ShapeDtypeStruct(cotangent.shape, jnp.bfloat16),
+            jax.ShapeDtypeStruct(lines_own.shape, jnp.float32),
+            jax.ShapeDtypeStruct((CH, ROWS * COLS), jnp.bfloat16),
+            jax.ShapeDtypeStruct((NK * CH, CH), jnp.bfloat16),
+        ),
+        compiler_params=params,
+        cost_estimate=pl.CostEstimate(flops=0, bytes_accessed=4 * 1024 * 1024, transcendentals=0),
+        name="own",
+    )(cotangent, lines_own, field.reshape(ROWS * COLS, CH), weight)
     up = shifted(up_own, LAT_AXES, 1, False)
     down = shifted(down_own, LAT_AXES, -1, False)
-    up, down, field_t, mixing = lax.optimization_barrier((up, down, field_t, mixing))
+    up, down, own, lines_own, field_t, mixing = lax.optimization_barrier(
+        (up, down, own, lines_own, field_t, mixing)
+    )
     side = jax.ShapeDtypeStruct((EXT, HALF, CH), jnp.bfloat16)
     east, west = pl.pallas_call(
         middle_kernel, out_shape=(side, side), compiler_params=params, name="middle"
-    )(up, up_own, down_own, down)
+    )(up, own, down)
     left = shifted(east, LON_AXES, 1, True)
     right = shifted(west, LON_AXES, -1, True)
 
@@ -224,7 +240,7 @@
             flops=band_flops, bytes_accessed=4 * 1024 * 1024, transcendentals=0
         ),
         name="inner_band",
-    )(up, up_own, down_own, down, lines_own)
+    )(up, own, down, lines_own)
 
     scale = 1.0 / math.sqrt(ROWS * lat_count * COLS * lon_count)
     grad_field, gw = pl.pallas_call(
@@ -233,7 +249,7 @@
             jax.ShapeDtypeStruct((ROWS, COLS, CH), jnp.float32),
             jax.ShapeDtypeStruct((NK * CH, CH), jnp.bfloat16),
         ),
-        scratch_shapes=[cells, pltpu.VMEM((NK, ROWS * COLS, CH), jnp.bfloat16)],
+        scratch_shapes=[cells, pltpu.VMEM((ROWS * COLS, NK * CH), jnp.bfloat16)],
         compiler_params=params,
         cost_estimate=pl.CostEstimate(
             flops=band_flops * 2, bytes_accessed=6 * 1024 * 1024, transcendentals=0
@@ -244,9 +260,9 @@
     plane, depth = sizes["yh"] * lon_count, lat_count // sizes["yh"]
     piece = gw.shape[0] // plane
     got = exchange(gw.reshape(plane, piece, CH), PLANE)
-    mine = jnp.sum(got.astype(jnp.float32), axis=0)
+    mine = jnp.sum(got.astype(jnp.float32), axis=0).astype(jnp.bfloat16)
     got = exchange(jnp.broadcast_to(mine[None], (depth, piece, CH)), "z")
-    mine = jnp.sum(got, axis=0).astype(jnp.bfloat16)
+    mine = jnp.sum(got.astype(jnp.float32), axis=0).astype(jnp.bfloat16)
     got = exchange(jnp.broadcast_to(mine[None], (plane, piece, CH)), PLANE)
     return (grad_field, got.reshape(NK * CH, CH).astype(jnp.float32))
 

time: 119 us -> 105 us (0.88)
  blocking collectives: 78.9 us -> 68.3 us
  Pallas kernels: 10.7 us -> 9.25 us
  local copies, waits for them, and re-layouts: 5.33 us -> 3.94 us
    all_to_all x3, blocking collectives: 78.9 us -> 68.3 us  [exchange(): return lax.all_to_all(x, axes, 0, 0, tiled=True)]
    reshape x2 -> x0, local copies, waits for them, and re-layouts: 2.42 us -> none  [the longest x1 1.25 us: per_device(): mixing = jnp.swapaxes(weight.reshape(NK, CH, CH), 1, 2).reshape(NK * CH, CH)]
    pallas_call x1, Pallas kernels: 5.13 us -> 3.46 us  [per_device(): pl.pallas_call(functools.partial(outer_kernel, scale), out_shape=(jax.Sha...]
    unnamed x6 -> x8, local copies, waits for them, and re-layouts: 2.81 us -> 3.87 us
  transfers between devices with their start and end apart: 4 -> 4, of which waited for: 3 -> 2; matrix products, arithmetic and copies ran while one was open for 2% -> 0% of each run, Pallas kernels for 3% -> 4%
where the time goes in v4:
time: 105 us; the launch traced here: 104 us
  blocking collectives  68.3 us (65%)
  starting transfers between devices  14.5 us (14%)
  Pallas kernels  9.25 us (9%)
  waiting for transfers between devices  6.46 us (6%)
  local copies, waits for them, and re-layouts  3.94 us (4%)
  other arithmetic  1.21 us (1%)
    all_to_all x3, blocking collectives, exchange(): return lax.all_to_all(x, axes, 0, 0, tiled=True)  68.3 us
    ppermute x4, starting transfers between devices, shifted(): return lax.ppermute(x, axes, pairs)  14.5 us
    ppermute x4, waiting for transfers between devices, shifted(): return lax.ppermute(x, axes, pairs)  6.46 us
    unnamed x8, local copies, waits for them, and re-layouts  3.87 us
    pallas_call x1, Pallas kernels, per_device(): pl.pallas_call(inner_kernel, out_shape=(jax.ShapeDtypeStruct((ROWS, NK *...  3.51 us
    pallas_call x1, Pallas kernels, per_device(): pl.pallas_call(functools.partial(outer_kernel, scale), out_shape=(jax.Sha...  3.46 us
  transfers between devices with their start and end apart: 4, of which 2 were waited for; matrix products, arithmetic and copies ran while one was open for 0% of the time, Pallas kernels for 4%

profile of v4, /device:TPU:1, one launch (start us, length us, event | category | flops | bytes accessed | tf_op | source)
XLA Modules:
  0.0 104.5 jit_solution(15080386987390092770)
XLA Ops:
  0.6 2.0 %prep.1 = (bf16[592,256]{1,0:T(8,128)(2,1)}, bf16[592,256]{1,0:T(8,128)(2,1)}, f32[192,128]{1,0:T(8,128)}) custom-call(s32[5,2,9]{2,1,0:T(2,128)} %bitcast.12, f32[5,9,4,128]{3,2,1,0:T(4,128)} %bitcast.11, bf16[640,256]{1,0:T(8,128)(2,1)} %bitcast.8), custom_call_target="tpu_custom_call" | custom-call | tf_op jit(solution)/shard_map/prep/pallas_call | solution.py:184
  2.6 4.4 %collective-permute-start = (bf16[592,256]{1,0:T(8,128)(2,1)}, bf16[592,256]{1,0:T(8,128)(2,1)S(1)}, u32[]{:S(2)}, u32[]{:S(2)}) collective-permute-start(bf16[592,256]{1,0:T(8,128)(2,1)} %get-tuple-element.21), channel_id=1, source_target_pairs={{0,16},{16,32},{32,48},{48,64},{64,80},{80,96},{96,112},{112,128},... | collective-permute-start | bytes 909320 | tf_op jit(solution)/shard_map/ppermute | solution.py:31
  7.0 1.3 %collective-permute-start.1 = (bf16[592,256]{1,0:T(8,128)(2,1)}, bf16[592,256]{1,0:T(8,128)(2,1)S(1)}, u32[]{:S(2)}, u32[]{:S(2)}) collective-permute-start(bf16[592,256]{1,0:T(8,128)(2,1)} %get-tuple-element.22), channel_id=1, source_target_pairs={{16,0},{32,16},{48,32},{64,48},{80,64},{96,80},{112,96},{128,112},... | collective-permute-start | bytes 909320 | tf_op jit(solution)/shard_map/ppermute | solution.py:31
  8.3 0.0 copy-start
  8.3 1.0 copy-done
  9.3 0.0 copy-start.1
  9.3 1.0 copy-done.1
  10.3 0.0 copy-start.2
  10.3 1.0 copy-done.2
  11.3 0.0 copy-start.3
  11.3 0.9 copy-done.3
  12.2 0.3 own.1
  12.4 0.0 collective-permute-done.up_ref
  12.5 2.5 %collective-permute-done.1.down_ref = bf16[592,256]{1,0:T(8,128)(2,1)S(1)} collective-permute-done((bf16[592,256]{1,0:T(8,128)(2,1)}, bf16[592,256]{1,0:T(8,128)(2,1)S(1)}, u32[]{:S(2)}, u32[]{:S(2)}) %collective-permute-start.1) | collective-permute-done | bytes 303136 | tf_op jit(solution)/shard_map/ppermute | solution.py:31
  14.9 0.1 middle.1
  15.0 6.9 %collective-permute-start.2 = (bf16[13,64,256]{2,1,0:T(8,128)(2,1)S(1)}, bf16[13,64,256]{2,1,0:T(8,128)(2,1)S(1)}, u32[]{:S(2)}, u32[]{:S(2)}) collective-permute-start(bf16[13,64,256]{2,1,0:T(8,128)(2,1)S(1)} %get-tuple-element.33), channel_id=1, source_target_pairs={{0,1},{1,2},{2,3},{3,4},{4,5},{5,6},{6,7},{7,8},{8,9},{9,10},{10,1... | collective-permute-start | bytes 1277960 | tf_op jit(solution)/shard_map/ppermute | solution.py:31
  21.9 1.9 %collective-permute-start.3 = (bf16[13,64,256]{2,1,0:T(8,128)(2,1)S(1)}, bf16[13,64,256]{2,1,0:T(8,128)(2,1)S(1)}, u32[]{:S(2)}, u32[]{:S(2)}) collective-permute-start(bf16[13,64,256]{2,1,0:T(8,128)(2,1)S(1)} %get-tuple-element.34), channel_id=1, source_target_pairs={{0,15},{1,0},{2,1},{3,2},{4,3},{5,4},{6,5},{7,6},{8,7},{9,8},{10,9... | collective-permute-start | bytes 1277960 | tf_op jit(solution)/shard_map/ppermute | solution.py:31
  23.9 3.5 %inner_band.1 = (f32[5,512,256]{2,1,0:T(8,128)S(1)}, bf16[5,512,1152]{2,1,0:T(8,128)(2,1)S(1)}) custom-call(bf16[592,256]{1,0:T(8,128)(2,1)S(1)} %collective-permute-done.up_ref, bf16[5,128,256]{2,1,0:T(8,128)(2,1)S(1)} %get-tuple-element.29.own_ref, bf16[592,256]{1,0:T(8,128)(2,1)S(1)} %collective-permute-done.1.down_ref, ...), custom_call_target="tpu_custom_call" | custom-call | flops 1509949440 | bytes 4194304 | tf_op jit(solution)/shard_map/inner_band/pallas_call | solution.py:227
  27.4 0.0 collective-permute-done.2.left
  27.4 4.0 %collective-permute-done.3.right = bf16[13,64,256]{2,1,0:T(8,128)(2,1)S(1)} collective-permute-done((bf16[13,64,256]{2,1,0:T(8,128)(2,1)S(1)}, bf16[13,64,256]{2,1,0:T(8,128)(2,1)S(1)}, u32[]{:S(2)}, u32[]{:S(2)}) %collective-permute-start.3) | collective-permute-done | bytes 426016 | tf_op jit(solution)/shard_map/ppermute | solution.py:31
  31.4 3.5 %outer_band.1 = (f32[5,128,256]{2,1,0:T(8,128)}, bf16[1024,256]{1,0:T(8,128)(2,1)S(1)}) custom-call(bf16[5,512,1152]{2,1,0:T(8,128)(2,1)S(1)} %get-tuple-element.32.bands, bf16[13,64,256]{2,1,0:T(8,128)(2,1)S(1)} %collective-permute-done.2.left, bf16[13,64,256]{2,1,0:T(8,128)(2,1)S(1)} %collective-permute-done.3.right, ...), custom_call_target="tpu_custom_call" | custom-call | flops 3019898880 | bytes 6291456 | tf_op jit(solution)/shard_map/outer_band/pallas_call | solution.py:246
  34.8 26.1 %all_to_all.15 = bf16[32,32,256]{2,1,0:T(8,128)(2,1)S(1)} all-to-all(bf16[32,32,256]{2,1,0:T(8,128)(2,1)S(1)} %bitcast.9), channel_id=1, replica_groups=mesh['yh'=2,'z'=16,'yl'=2,'x'=4,'core'=2] {'yh','yl','x','core'}, dimensions={0} | all-to-all | bytes 1048576 | tf_op jit(solution)/shard_map/all_to_all | solution.py:174
  60.9 0.1 reduce_sum.24
  61.0 22.2 %all_to_all.16 = bf16[16,32,256]{2,1,0:T(8,128)(2,1)S(1)} all-to-all(bf16[16,32,256]{2,1,0:T(8,128)(2,1)S(1)} %broadcast_in_dim.4), channel_id=1, replica_groups=mesh['yh'=2,'z'=16,'yl'=2,'x'=4,'core'=2] {'z'}, dimensions={0} | all-to-all | bytes 524288 | tf_op jit(solution)/shard_map/all_to_all | solution.py:174
  83.3 0.1 broadcast_in_dim.5
  83.3 20.1 %all_to_all.17 = bf16[32,32,256]{2,1,0:T(8,128)(2,1)S(1)} all-to-all(bf16[32,32,256]{2,1,0:T(8,128)(2,1)S(1)} %broadcast_in_dim.5), channel_id=1, replica_groups=mesh['yh'=2,'z'=16,'yl'=2,'x'=4,'core'=2] {'yh','yl','x','core'}, dimensions={0} | all-to-all | bytes 1048576 | tf_op jit(solution)/shard_map/all_to_all | solution.py:174
  103.4 1.1 %bitcast_convert_fusion = f32[1024,256]{1,0:T(8,128)} fusion(bf16[32,32,256]{2,1,0:T(8,128)(2,1)S(1)} %all_to_all.17), kind=kLoop, calls=%fused_computation | loop fusion | flops 262144 | bytes 1572864 | tf_op jit(solution)/shard_map/convert_element_type | solution.py:267
  (2 shorter events, 0.1 us)
Async XLA Ops:
  2.6 9.9 %collective-permute-start = (bf16[592,256]{1,0:T(8,128)(2,1)}, bf16[592,256]{1,0:T(8,128)(2,1)S(1)}, u32[]{:S(2)}, u32[]{:S(2)}) collective-permute-start(bf16[592,256]{1,0:T(8,128)(2,1)} %get-tuple-element.21), channel_id=1, source_target_pairs={{0,16},{16,32},{32,48},{48,64},{64,80},{80,96},{96,112},{112,128},... | collective-permute-start | bytes 909320 | tf_op jit(solution)/shard_map/ppermute | solution.py:31
  7.0 7.9 %collective-permute-start.1 = (bf16[592,256]{1,0:T(8,128)(2,1)}, bf16[592,256]{1,0:T(8,128)(2,1)S(1)}, u32[]{:S(2)}, u32[]{:S(2)}) collective-permute-start(bf16[592,256]{1,0:T(8,128)(2,1)} %get-tuple-element.22), channel_id=1, source_target_pairs={{16,0},{32,16},{48,32},{64,48},{80,64},{96,80},{112,96},{128,112},... | collective-permute-start | bytes 909320 | tf_op jit(solution)/shard_map/ppermute | solution.py:31
  8.3 1.0 copy-start
  9.3 1.0 copy-start.1
  10.3 1.0 copy-start.2
  11.3 0.9 copy-start.3
  15.0 12.4 %collective-permute-start.2 = (bf16[13,64,256]{2,1,0:T(8,128)(2,1)S(1)}, bf16[13,64,256]{2,1,0:T(8,128)(2,1)S(1)}, u32[]{:S(2)}, u32[]{:S(2)}) collective-permute-start(bf16[13,64,256]{2,1,0:T(8,128)(2,1)S(1)} %get-tuple-element.33), channel_id=1, source_target_pairs={{0,1},{1,2},{2,3},{3,4},{4,5},{5,6},{6,7},{7,8},{8,9},{9,10},{10,1... | collective-permute-start | bytes 1277960 | tf_op jit(solution)/shard_map/ppermute | solution.py:31
  21.9 9.4 %collective-permute-start.3 = (bf16[13,64,256]{2,1,0:T(8,128)(2,1)S(1)}, bf16[13,64,256]{2,1,0:T(8,128)(2,1)S(1)}, u32[]{:S(2)}, u32[]{:S(2)}) collective-permute-start(bf16[13,64,256]{2,1,0:T(8,128)(2,1)S(1)} %get-tuple-element.34), channel_id=1, source_target_pairs={{0,15},{1,0},{2,1},{3,2},{4,3},{5,4},{6,5},{7,6},{8,7},{9,8},{10,9... | collective-permute-start | bytes 1277960 | tf_op jit(solution)/shard_map/ppermute | solution.py:31

commit v5 on v4

--- a/solution.py
+++ b/solution.py
@@ -20,14 +20,9 @@
 VMEM_LIMIT = 32 * 1024 * 1024
 
 
-def shifted(x, axes, step, closed):
-    count = 1
-    for a in axes:
-        count *= lax.axis_size(a)
-    if closed:
-        pairs = [(i, (i + step) % count) for i in range(count)]
-    else:
-        pairs = [(i, i + step) for i in range(count) if 0 <= i + step < count]
+def shifted(x, axes, step):
+    count = math.prod(lax.axis_size(a) for a in axes)
+    pairs = [(i, i + step) for i in range(count) if 0 <= i + step < count]
     return lax.ppermute(x, axes, pairs)
 
 
@@ -94,10 +89,17 @@
         yield down_ref[n * COLS : (n + 1) * COLS, :]
 
 
-def middle_kernel(up_ref, own_ref, down_ref, east_ref, west_ref):
-    for row, cells in enumerate(rows_in_reach(up_ref, own_ref, down_ref)):
-        east_ref[row] = cells[HALF:]
-        west_ref[row] = cells[:HALF]
+def middle_kernel(up_ref, own_ref, down_ref, across_ref, beside_ref):
+    first = pl.multiple_of(lax.axis_index("core") * HALF, HALF)
+    other = pl.multiple_of(HALF - first, HALF)
+    for n in range(RAD):
+        across_ref[n] = up_ref[pl.ds(n * COLS + first, HALF), :]
+        beside_ref[n] = up_ref[pl.ds(n * COLS + other, HALF), :]
+        across_ref[RAD + ROWS + n] = down_ref[pl.ds(n * COLS + first, HALF), :]
+        beside_ref[RAD + ROWS + n] = down_ref[pl.ds(n * COLS + other, HALF), :]
+    for n in range(ROWS):
+        across_ref[RAD + n] = own_ref[n, pl.ds(first, HALF), :]
+        beside_ref[RAD + n] = own_ref[n, pl.ds(other, HALF), :]
 
 
 def gather_lines(up_ref, own_ref, down_ref, lines_ref):
@@ -149,11 +151,13 @@
 
 
 def outer_kernel(
-    scale, bands, left, right, part_ref, field_t, mixing, grad_ref, gw_ref, cells, spreads
+    scale, bands, across, beside, part_ref, field_t, mixing, grad_ref, gw_ref, cells, spreads
 ):
+    first = pl.multiple_of(lax.axis_index("core") * HALF, HALF)
+    other = pl.multiple_of(HALF - first, HALF)
     for row in range(EXT):
-        cells[row * COLS : row * COLS + HALF, :] = left[row]
-        cells[row * COLS + HALF : (row + 1) * COLS, :] = right[row]
+        cells[pl.ds(row * COLS + first, HALF), :] = across[row]
+        cells[pl.ds(row * COLS + other, HALF), :] = beside[row]
     for l in range(ROWS):
         window = cells[l * COLS : (l + NR) * COLS, :]
         for k in range(NK):
@@ -210,17 +214,19 @@
         cost_estimate=pl.CostEstimate(flops=0, bytes_accessed=4 * 1024 * 1024, transcendentals=0),
         name="own",
     )(cotangent, lines_own, field.reshape(ROWS * COLS, CH), weight)
-    up = shifted(up_own, LAT_AXES, 1, False)
-    down = shifted(down_own, LAT_AXES, -1, False)
+    up = shifted(up_own, LAT_AXES, 1)
+    down = shifted(down_own, LAT_AXES, -1)
     up, down, own, lines_own, field_t, mixing = lax.optimization_barrier(
         (up, down, own, lines_own, field_t, mixing)
     )
     side = jax.ShapeDtypeStruct((EXT, HALF, CH), jnp.bfloat16)
-    east, west = pl.pallas_call(
+    across, beside = pl.pallas_call(
         middle_kernel, out_shape=(side, side), compiler_params=params, name="middle"
     )(up, own, down)
-    left = shifted(east, LON_AXES, 1, True)
-    right = shifted(west, LON_AXES, -1, True)
+    across = lax.ppermute(
+        across, LON_AXES, [(i, (i - 1 + 2 * (i % 2)) % lon_count) for i in range(lon_count)]
+    )
+    beside = lax.ppermute(beside, "core", [(0, 1), (1, 0)])
 
     cells = pltpu.VMEM((EXT * COLS, CH), jnp.bfloat16)
     band_flops = 2 * ROWS * NK * COLS * NR * COLS * CH
@@ -255,7 +261,7 @@
             flops=band_flops * 2, bytes_accessed=6 * 1024 * 1024, transcendentals=0
         ),
         name="outer_band",
-    )(bands, left, right, part, field_t, mixing)
+    )(bands, across, beside, part, field_t, mixing)
 
     plane, depth = sizes["yh"] * lon_count, lat_count // sizes["yh"]
     piece = gw.shape[0] // plane

time: 105 us -> 100 us (0.952)
  waiting for transfers between devices: 6.46 us -> 2.47 us
  blocking collectives: 68.3 us -> 66.6 us
  starting transfers between devices: 14.5 us -> 15.6 us
    ppermute x0 -> x2, starting transfers between devices: none -> 9.96 us  [the longest x1 6.94 us: per_device(): lax.ppermute(across, LON_AXES, [(i, (i - 1 + 2 * (i % 2)) % lon_count) fo...]
    ppermute x4 -> x2, starting transfers between devices: 14.5 us -> 5.68 us  [shifted(): return lax.ppermute(x, axes, pairs)]
    ppermute x4 -> x2, waiting for transfers between devices: 6.46 us -> 2.47 us  [shifted(): return lax.ppermute(x, axes, pairs)]
    all_to_all x3, blocking collectives: 68.3 us -> 66.6 us  [exchange(): return lax.all_to_all(x, axes, 0, 0, tiled=True)]
  transfers between devices with their start and end apart: 4 -> 4, of which waited for: 2 -> 1; matrix products, arithmetic and copies ran while one was open for 0% -> 0% of each run, Pallas kernels for 4% -> 4%
where the time goes in v5:
time: 100 us
  blocking collectives  66.6 us (67%)
  starting transfers between devices  15.6 us (16%)
  Pallas kernels  9.38 us (9%)
  local copies, waits for them, and re-layouts  3.94 us (4%)
  waiting for transfers between devices  2.47 us (2%)
  other arithmetic  1.21 us (1%)
    all_to_all x3, blocking collectives, exchange(): return lax.all_to_all(x, axes, 0, 0, tiled=True)  66.6 us
    ppermute x1, starting transfers between devices, per_device(): lax.ppermute(across, LON_AXES, [(i, (i - 1 + 2 * (i % 2)) % lon_count) fo...  6.94 us
    ppermute x2, starting transfers between devices, shifted(): return lax.ppermute(x, axes, pairs)  5.68 us
    unnamed x8, local copies, waits for them, and re-layouts  3.87 us
    pallas_call x1, Pallas kernels, per_device(): pl.pallas_call(functools.partial(outer_kernel, scale), out_shape=(jax.Sha...  3.59 us
    pallas_call x1, Pallas kernels, per_device(): pl.pallas_call(inner_kernel, out_shape=(jax.ShapeDtypeStruct((ROWS, NK *...  3.51 us
    ppermute x1, starting transfers between devices, per_device(): beside = lax.ppermute(beside, 'core', [(0, 1), (1, 0)])  3.02 us
    ppermute x2, waiting for transfers between devices, shifted(): return lax.ppermute(x, axes, pairs)  2.47 us
  transfers between devices with their start and end apart: 4, of which 1 were waited for; matrix products, arithmetic and copies ran while one was open for 0% of the time, Pallas kernels for 4%

profile of v5, /device:TPU:1, one launch (start us, length us, event | category | flops | bytes accessed | tf_op | source)
XLA Modules:
  0.0 100.0 jit_solution(10759053880096527812)
XLA Ops:
  0.6 2.0 %prep.1 = (bf16[592,256]{1,0:T(8,128)(2,1)}, bf16[592,256]{1,0:T(8,128)(2,1)}, f32[192,128]{1,0:T(8,128)}) custom-call(s32[5,2,9]{2,1,0:T(2,128)} %bitcast.12, f32[5,9,4,128]{3,2,1,0:T(4,128)} %bitcast.11, bf16[640,256]{1,0:T(8,128)(2,1)} %bitcast.8), custom_call_target="tpu_custom_call" | custom-call | tf_op jit(solution)/shard_map/prep/pallas_call | solution.py:188
  2.6 4.4 %collective-permute-start = (bf16[592,256]{1,0:T(8,128)(2,1)}, bf16[592,256]{1,0:T(8,128)(2,1)S(1)}, u32[]{:S(2)}, u32[]{:S(2)}) collective-permute-start(bf16[592,256]{1,0:T(8,128)(2,1)} %get-tuple-element.21), channel_id=1, source_target_pairs={{0,16},{16,32},{32,48},{48,64},{64,80},{80,96},{96,112},{112,128},... | collective-permute-start | bytes 909320 | tf_op jit(solution)/shard_map/ppermute | solution.py:26
  7.0 1.3 %collective-permute-start.1 = (bf16[592,256]{1,0:T(8,128)(2,1)}, bf16[592,256]{1,0:T(8,128)(2,1)S(1)}, u32[]{:S(2)}, u32[]{:S(2)}) collective-permute-start(bf16[592,256]{1,0:T(8,128)(2,1)} %get-tuple-element.22), channel_id=1, source_target_pairs={{16,0},{32,16},{48,32},{64,48},{80,64},{96,80},{112,96},{128,112},... | collective-permute-start | bytes 909320 | tf_op jit(solution)/shard_map/ppermute | solution.py:26
  8.3 0.0 copy-start
  8.3 1.0 copy-done
  9.3 0.0 copy-start.1
  9.3 1.0 %copy-done.1 = bf16[1024,256]{1,0:T(8,128)(2,1)S(1)} copy-done((bf16[1024,256]{1,0:T(8,128)(2,1)S(1)}, bf16[1024,256]{1,0:T(8,128)(2,1)}, u32[]{:S(2)}) %copy-start.1) | copy-done | bytes 524312
  10.3 0.0 copy-start.2
  10.3 1.0 copy-done.2
  11.3 0.0 copy-start.3
  11.3 0.9 copy-done.3
  12.2 0.3 own.1
  12.4 0.0 collective-permute-done.up_ref
  12.5 2.5 %collective-permute-done.1.down_ref = bf16[592,256]{1,0:T(8,128)(2,1)S(1)} collective-permute-done((bf16[592,256]{1,0:T(8,128)(2,1)}, bf16[592,256]{1,0:T(8,128)(2,1)S(1)}, u32[]{:S(2)}, u32[]{:S(2)}) %collective-permute-start.1) | collective-permute-done | bytes 303136 | tf_op jit(solution)/shard_map/ppermute | solution.py:26
  14.9 0.1 middle.1
  15.0 6.9 %collective-permute-start.2 = (bf16[13,64,256]{2,1,0:T(8,128)(2,1)S(1)}, bf16[13,64,256]{2,1,0:T(8,128)(2,1)S(1)}, u32[]{:S(2)}, u32[]{:S(2)}) collective-permute-start(bf16[13,64,256]{2,1,0:T(8,128)(2,1)S(1)} %get-tuple-element.33), channel_id=1, source_target_pairs={{0,15},{1,2},{2,1},{3,4},{4,3},{5,6},{6,5},{7,8},{8,7},{9,10},{10,... | collective-permute-start | bytes 1277960 | tf_op jit(solution)/shard_map/ppermute | solution.py:226
  21.9 3.0 %collective-permute-start.3 = (bf16[13,64,256]{2,1,0:T(8,128)(2,1)S(1)}, bf16[13,64,256]{2,1,0:T(8,128)(2,1)S(1)}, u32[]{:S(2)}, u32[]{:S(2)}) collective-permute-start(bf16[13,64,256]{2,1,0:T(8,128)(2,1)S(1)} %get-tuple-element.34), channel_id=1, source_target_pairs={{0,1},{1,0},{2,3},{3,2},{4,5},{5,4},{6,7},{7,6},{8,9},{9,8},{10,11... | collective-permute-start | bytes 1277960 | tf_op jit(solution)/shard_map/ppermute | solution.py:229
  25.0 3.5 %inner_band.1 = (f32[5,512,256]{2,1,0:T(8,128)S(1)}, bf16[5,512,1152]{2,1,0:T(8,128)(2,1)S(1)}) custom-call(bf16[592,256]{1,0:T(8,128)(2,1)S(1)} %collective-permute-done.up_ref, bf16[5,128,256]{2,1,0:T(8,128)(2,1)S(1)} %get-tuple-element.29.own_ref, bf16[592,256]{1,0:T(8,128)(2,1)S(1)} %collective-permute-done.1.down_ref, ...), custom_call_target="tpu_custom_call" | custom-call | flops 1509949440 | bytes 4194304 | tf_op jit(solution)/shard_map/inner_band/pallas_call | solution.py:233
  28.5 0.0 collective-permute-done.2.across
  28.5 0.0 collective-permute-done.3.beside
  28.5 3.6 %outer_band.1 = (f32[5,128,256]{2,1,0:T(8,128)}, bf16[1024,256]{1,0:T(8,128)(2,1)S(1)}) custom-call(bf16[5,512,1152]{2,1,0:T(8,128)(2,1)S(1)} %get-tuple-element.32.bands, bf16[13,64,256]{2,1,0:T(8,128)(2,1)S(1)} %collective-permute-done.2.across, bf16[13,64,256]{2,1,0:T(8,128)(2,1)S(1)} %collective-permute-done.3.beside, ...), custom_call_target="tpu_custom_call" | custom-call | flops 3019898880 | bytes 6291456 | tf_op jit(solution)/shard_map/outer_band/pallas_call | solution.py:252
  32.1 24.5 %all_to_all.15 = bf16[32,32,256]{2,1,0:T(8,128)(2,1)S(1)} all-to-all(bf16[32,32,256]{2,1,0:T(8,128)(2,1)S(1)} %bitcast.9), channel_id=1, replica_groups=mesh['yh'=2,'z'=16,'yl'=2,'x'=4,'core'=2] {'yh','yl','x','core'}, dimensions={0} | all-to-all | bytes 1048576 | tf_op jit(solution)/shard_map/all_to_all | solution.py:178
  56.6 0.1 reduce_sum.24
  56.7 22.1 %all_to_all.16 = bf16[16,32,256]{2,1,0:T(8,128)(2,1)S(1)} all-to-all(bf16[16,32,256]{2,1,0:T(8,128)(2,1)S(1)} %broadcast_in_dim.4), channel_id=1, replica_groups=mesh['yh'=2,'z'=16,'yl'=2,'x'=4,'core'=2] {'z'}, dimensions={0} | all-to-all | bytes 524288 | tf_op jit(solution)/shard_map/all_to_all | solution.py:178
  78.8 0.1 broadcast_in_dim.5
  78.9 20.1 %all_to_all.17 = bf16[32,32,256]{2,1,0:T(8,128)(2,1)S(1)} all-to-all(bf16[32,32,256]{2,1,0:T(8,128)(2,1)S(1)} %broadcast_in_dim.5), channel_id=1, replica_groups=mesh['yh'=2,'z'=16,'yl'=2,'x'=4,'core'=2] {'yh','yl','x','core'}, dimensions={0} | all-to-all | bytes 1048576 | tf_op jit(solution)/shard_map/all_to_all | solution.py:178
  98.9 1.1 %bitcast_convert_fusion = f32[1024,256]{1,0:T(8,128)} fusion(bf16[32,32,256]{2,1,0:T(8,128)(2,1)S(1)} %all_to_all.17), kind=kLoop, calls=%fused_computation | loop fusion | flops 262144 | bytes 1572864 | tf_op jit(solution)/shard_map/convert_element_type | solution.py:273
  (2 shorter events, 0.1 us)
Async XLA Ops:
  2.6 9.9 %collective-permute-start = (bf16[592,256]{1,0:T(8,128)(2,1)}, bf16[592,256]{1,0:T(8,128)(2,1)S(1)}, u32[]{:S(2)}, u32[]{:S(2)}) collective-permute-start(bf16[592,256]{1,0:T(8,128)(2,1)} %get-tuple-element.21), channel_id=1, source_target_pairs={{0,16},{16,32},{32,48},{48,64},{64,80},{80,96},{96,112},{112,128},... | collective-permute-start | bytes 909320 | tf_op jit(solution)/shard_map/ppermute | solution.py:26
  7.0 7.9 %collective-permute-start.1 = (bf16[592,256]{1,0:T(8,128)(2,1)}, bf16[592,256]{1,0:T(8,128)(2,1)S(1)}, u32[]{:S(2)}, u32[]{:S(2)}) collective-permute-start(bf16[592,256]{1,0:T(8,128)(2,1)} %get-tuple-element.22), channel_id=1, source_target_pairs={{16,0},{32,16},{48,32},{64,48},{80,64},{96,80},{112,96},{128,112},... | collective-permute-start | bytes 909320 | tf_op jit(solution)/shard_map/ppermute | solution.py:26
  8.3 1.0 copy-start
  9.3 1.0 %copy-start.1 = (bf16[1024,256]{1,0:T(8,128)(2,1)S(1)}, bf16[1024,256]{1,0:T(8,128)(2,1)}, u32[]{:S(2)}) copy-start(bf16[1024,256]{1,0:T(8,128)(2,1)} %weight_ref.1) | copy-start | bytes 1572868
  10.3 1.0 copy-start.2
  11.3 0.9 copy-start.3
  15.0 13.5 %collective-permute-start.2 = (bf16[13,64,256]{2,1,0:T(8,128)(2,1)S(1)}, bf16[13,64,256]{2,1,0:T(8,128)(2,1)S(1)}, u32[]{:S(2)}, u32[]{:S(2)}) collective-permute-start(bf16[13,64,256]{2,1,0:T(8,128)(2,1)S(1)} %get-tuple-element.33), channel_id=1, source_target_pairs={{0,15},{1,2},{2,1},{3,4},{4,3},{5,6},{6,5},{7,8},{8,7},{9,10},{10,... | collective-permute-start | bytes 1277960 | tf_op jit(solution)/shard_map/ppermute | solution.py:226
  21.9 6.6 %collective-permute-start.3 = (bf16[13,64,256]{2,1,0:T(8,128)(2,1)S(1)}, bf16[13,64,256]{2,1,0:T(8,128)(2,1)S(1)}, u32[]{:S(2)}, u32[]{:S(2)}) collective-permute-start(bf16[13,64,256]{2,1,0:T(8,128)(2,1)S(1)} %get-tuple-element.34), channel_id=1, source_target_pairs={{0,1},{1,0},{2,3},{3,2},{4,5},{5,4},{6,7},{7,6},{8,9},{9,8},{10,11... | collective-permute-start | bytes 1277960 | tf_op jit(solution)/shard_map/ppermute | solution.py:229

commit v6 on v5

--- a/solution.py
+++ b/solution.py
@@ -8,7 +8,7 @@
 from jax.experimental.pallas import tpu as pltpu
 from jax.sharding import Mesh, PartitionSpec as P
 
-LAT_AXES = ("yh", "z")
+LAT_AXES = ("yh", "zh", "zl")
 LON_AXES = ("yl", "x", "core")
 PLANE = ("yh", "yl", "x", "core")
 
@@ -75,7 +75,9 @@
 def own_kernel(cells_ref, lines_ref, field_ref, weight_ref, own_ref, lines_own, field_t, mixing):
     own_ref[...] = cells_ref[...]
     lines_own[...] = lines_ref[...]
-    field_t[...] = field_ref[...].T
+    turned = field_ref[...].T
+    field_t[:, : ROWS * COLS] = turned
+    field_t[:, ROWS * COLS :] = turned
     for k in range(NK):
         mixing[k * CH : (k + 1) * CH, :] = weight_ref[k * CH : (k + 1) * CH, :].T
 
@@ -165,11 +167,15 @@
             spread = part_ref[l, rows, :] + jnp.dot(
                 bands[l, rows, :], window, preferred_element_type=jnp.float32
             )
-            spreads[l * COLS : (l + 1) * COLS, k * CH : (k + 1) * CH] = spread.astype(jnp.bfloat16)
+            high = spread.astype(jnp.bfloat16)
+            low = (spread - high.astype(jnp.float32)).astype(jnp.bfloat16)
+            at = slice(k * CH, (k + 1) * CH)
+            spreads[l * COLS : (l + 1) * COLS, at] = high
+            spreads[(ROWS + l) * COLS : (ROWS + l + 1) * COLS, at] = low
     total = jnp.dot(field_t[...], spreads[...], preferred_element_type=jnp.float32) * scale
     for k in range(NK):
         gw_ref[k * CH : (k + 1) * CH, :] = total[:, k * CH : (k + 1) * CH].astype(jnp.bfloat16)
-    grad = jnp.dot(spreads[...], mixing[...], preferred_element_type=jnp.float32)
+    grad = jnp.dot(spreads[: ROWS * COLS, :], mixing[...], preferred_element_type=jnp.float32)
     for l in range(ROWS):
         grad_ref[l] = grad[l * COLS : (l + 1) * COLS, :]
 
@@ -207,7 +213,7 @@
         out_shape=(
             jax.ShapeDtypeStruct(cotangent.shape, jnp.bfloat16),
             jax.ShapeDtypeStruct(lines_own.shape, jnp.float32),
-            jax.ShapeDtypeStruct((CH, ROWS * COLS), jnp.bfloat16),
+            jax.ShapeDtypeStruct((CH, 2 * ROWS * COLS), jnp.bfloat16),
             jax.ShapeDtypeStruct((NK * CH, CH), jnp.bfloat16),
         ),
         compiler_params=params,
@@ -255,7 +261,7 @@
             jax.ShapeDtypeStruct((ROWS, COLS, CH), jnp.float32),
             jax.ShapeDtypeStruct((NK * CH, CH), jnp.bfloat16),
         ),
-        scratch_shapes=[cells, pltpu.VMEM((ROWS * COLS, NK * CH), jnp.bfloat16)],
+        scratch_shapes=[cells, pltpu.VMEM((2 * ROWS * COLS, NK * CH), jnp.bfloat16)],
         compiler_params=params,
         cost_estimate=pl.CostEstimate(
             flops=band_flops * 2, bytes_accessed=6 * 1024 * 1024, transcendentals=0
@@ -263,18 +269,17 @@
         name="outer_band",
     )(bands, across, beside, part, field_t, mixing)
 
-    plane, depth = sizes["yh"] * lon_count, lat_count // sizes["yh"]
+    plane = sizes["yh"] * lon_count
     piece = gw.shape[0] // plane
     got = exchange(gw.reshape(plane, piece, CH), PLANE)
-    mine = jnp.sum(got.astype(jnp.float32), axis=0).astype(jnp.bfloat16)
-    got = exchange(jnp.broadcast_to(mine[None], (depth, piece, CH)), "z")
-    mine = jnp.sum(got.astype(jnp.float32), axis=0).astype(jnp.bfloat16)
-    got = exchange(jnp.broadcast_to(mine[None], (plane, piece, CH)), PLANE)
+    for axes, count in (("zl", sizes["zl"]), ("zh", sizes["zh"]), (PLANE, plane)):
+        mine = jnp.sum(got.astype(jnp.float32), axis=0).astype(jnp.bfloat16)
+        got = exchange(jnp.broadcast_to(mine[None], (count, piece, CH)), axes)
     return (grad_field, got.reshape(NK * CH, CH).astype(jnp.float32))
 
 
 def solution(mesh):
-    fine = Mesh(mesh.devices.reshape(2, 16, 2, 4, 2), LAT_AXES + LON_AXES)
+    fine = Mesh(mesh.devices.reshape(2, 4, 4, 2, 4, 2), LAT_AXES + LON_AXES)
     return jax.shard_map(
         per_device,
         mesh=fine,

time: 100 us -> 105 us (1.050)
  blocking collectives: 66.6 us -> 70.4 us
    all_to_all x3 -> x4, blocking collectives: 66.6 us -> 70.4 us  [exchange(): return lax.all_to_all(x, axes, 0, 0, tiled=True)]
where the time goes in v6:
time: 105 us; the launch traced here: 104 us
  blocking collectives  70.4 us (67%)
  starting transfers between devices  15.6 us (15%)
  Pallas kernels  9.66 us (9%)
  local copies, waits for them, and re-layouts  3.94 us (4%)
  waiting for transfers between devices  2.47 us (2%)
  other arithmetic  1.19 us (1%)
    all_to_all x4, blocking collectives, exchange(): return lax.all_to_all(x, axes, 0, 0, tiled=True)  70.4 us
    ppermute x1, starting transfers between devices, per_device(): lax.ppermute(across, LON_AXES, [(i, (i - 1 + 2 * (i % 2)) % lon_count) fo...  6.94 us
    ppermute x2, starting transfers between devices, shifted(): return lax.ppermute(x, axes, pairs)  5.68 us
    pallas_call x1, Pallas kernels, per_device(): pl.pallas_call(functools.partial(outer_kernel, scale), out_shape=(jax.Sha...  3.88 us
    unnamed x8, local copies, waits for them, and re-layouts  3.87 us
    pallas_call x1, Pallas kernels, per_device(): pl.pallas_call(inner_kernel, out_shape=(jax.ShapeDtypeStruct((ROWS, NK *...  3.5 us
    ppermute x1, starting transfers between devices, per_device(): beside = lax.ppermute(beside, 'core', [(0, 1), (1, 0)])  3.02 us
    ppermute x2, waiting for transfers between devices, shifted(): return lax.ppermute(x, axes, pairs)  2.47 us
  transfers between devices with their start and end apart: 4, of which 1 were waited for; matrix products, arithmetic and copies ran while one was open for 0% of the time, Pallas kernels for 4%

profile of v6, /device:TPU:1, one launch (start us, length us, event | category | flops | bytes accessed | tf_op | source)
XLA Modules:
  0.0 104.0 jit_solution(13571002572342100035)
XLA Ops:
  0.6 2.0 %prep.1 = (bf16[592,256]{1,0:T(8,128)(2,1)}, bf16[592,256]{1,0:T(8,128)(2,1)}, f32[192,128]{1,0:T(8,128)}) custom-call(s32[5,2,9]{2,1,0:T(2,128)} %bitcast.12, f32[5,9,4,128]{3,2,1,0:T(4,128)} %bitcast.11, bf16[640,256]{1,0:T(8,128)(2,1)} %bitcast.8), custom_call_target="tpu_custom_call" | custom-call | tf_op jit(solution)/shard_map/prep/pallas_call | solution.py:194
  2.6 4.4 %collective-permute-start = (bf16[592,256]{1,0:T(8,128)(2,1)}, bf16[592,256]{1,0:T(8,128)(2,1)S(1)}, u32[]{:S(2)}, u32[]{:S(2)}) collective-permute-start(bf16[592,256]{1,0:T(8,128)(2,1)} %get-tuple-element.21), channel_id=1, source_target_pairs={{0,16},{16,32},{32,48},{48,64},{64,80},{80,96},{96,112},{112,128},... | collective-permute-start | bytes 909320 | tf_op jit(solution)/shard_map/ppermute | solution.py:26
  7.0 1.3 %collective-permute-start.1 = (bf16[592,256]{1,0:T(8,128)(2,1)}, bf16[592,256]{1,0:T(8,128)(2,1)S(1)}, u32[]{:S(2)}, u32[]{:S(2)}) collective-permute-start(bf16[592,256]{1,0:T(8,128)(2,1)} %get-tuple-element.22), channel_id=1, source_target_pairs={{16,0},{32,16},{48,32},{64,48},{80,64},{96,80},{112,96},{128,112},... | collective-permute-start | bytes 909320 | tf_op jit(solution)/shard_map/ppermute | solution.py:26
  8.3 0.0 copy-start
  8.3 1.0 copy-done
  9.3 0.0 copy-start.1
  9.3 1.0 copy-done.1
  10.3 0.0 copy-start.2
  10.3 1.0 copy-done.2
  11.3 0.0 copy-start.3
  11.3 0.9 copy-done.3
  12.2 0.3 own.1
  12.4 0.0 collective-permute-done.up_ref
  12.5 2.5 %collective-permute-done.1.down_ref = bf16[592,256]{1,0:T(8,128)(2,1)S(1)} collective-permute-done((bf16[592,256]{1,0:T(8,128)(2,1)}, bf16[592,256]{1,0:T(8,128)(2,1)S(1)}, u32[]{:S(2)}, u32[]{:S(2)}) %collective-permute-start.1) | collective-permute-done | bytes 303136 | tf_op jit(solution)/shard_map/ppermute | solution.py:26
  14.9 0.1 middle.1
  15.0 6.9 %collective-permute-start.2 = (bf16[13,64,256]{2,1,0:T(8,128)(2,1)S(1)}, bf16[13,64,256]{2,1,0:T(8,128)(2,1)S(1)}, u32[]{:S(2)}, u32[]{:S(2)}) collective-permute-start(bf16[13,64,256]{2,1,0:T(8,128)(2,1)S(1)} %get-tuple-element.33), channel_id=1, source_target_pairs={{0,15},{1,2},{2,1},{3,4},{4,3},{5,6},{6,5},{7,8},{8,7},{9,10},{10,... | collective-permute-start | bytes 1277960 | tf_op jit(solution)/shard_map/ppermute | solution.py:232
  21.9 3.0 %collective-permute-start.3 = (bf16[13,64,256]{2,1,0:T(8,128)(2,1)S(1)}, bf16[13,64,256]{2,1,0:T(8,128)(2,1)S(1)}, u32[]{:S(2)}, u32[]{:S(2)}) collective-permute-start(bf16[13,64,256]{2,1,0:T(8,128)(2,1)S(1)} %get-tuple-element.34), channel_id=1, source_target_pairs={{0,1},{1,0},{2,3},{3,2},{4,5},{5,4},{6,7},{7,6},{8,9},{9,8},{10,11... | collective-permute-start | bytes 1277960 | tf_op jit(solution)/shard_map/ppermute | solution.py:235
  25.0 3.5 %inner_band.1 = (f32[5,512,256]{2,1,0:T(8,128)S(1)}, bf16[5,512,1152]{2,1,0:T(8,128)(2,1)S(1)}) custom-call(bf16[592,256]{1,0:T(8,128)(2,1)S(1)} %collective-permute-done.up_ref, bf16[5,128,256]{2,1,0:T(8,128)(2,1)S(1)} %get-tuple-element.29.own_ref, bf16[592,256]{1,0:T(8,128)(2,1)S(1)} %collective-permute-done.1.down_ref, ...), custom_call_target="tpu_custom_call" | custom-call | flops 1509949440 | bytes 4194304 | tf_op jit(solution)/shard_map/inner_band/pallas_call | solution.py:239
  28.5 0.0 collective-permute-done.2.across
  28.5 0.0 collective-permute-done.3.beside
  28.5 3.9 %outer_band.1 = (f32[5,128,256]{2,1,0:T(8,128)}, bf16[1024,256]{1,0:T(8,128)(2,1)S(1)}) custom-call(bf16[5,512,1152]{2,1,0:T(8,128)(2,1)S(1)} %get-tuple-element.32.bands, bf16[13,64,256]{2,1,0:T(8,128)(2,1)S(1)} %collective-permute-done.2.across, bf16[13,64,256]{2,1,0:T(8,128)(2,1)S(1)} %collective-permute-done.3.beside, ...), custom_call_target="tpu_custom_call" | custom-call | flops 3019898880 | bytes 6291456 | tf_op jit(solution)/shard_map/outer_band/pallas_call | solution.py:258
  32.4 24.5 %all_to_all.20 = bf16[32,32,256]{2,1,0:T(8,128)(2,1)S(1)} all-to-all(bf16[32,32,256]{2,1,0:T(8,128)(2,1)S(1)} %bitcast.9), channel_id=1, replica_groups=mesh['yh'=2,'zh'=4,'zl'=4,'yl'=2,'x'=4,'core'=2] {'yh','yl','x','core'}, dimensions={0} | all-to-all | bytes 1048576 | tf_op jit(solution)/shard_map/all_to_all | solution.py:184
  56.9 0.1 reduce_sum.36
  57.0 7.0 %all_to_all.21 = bf16[4,32,256]{2,1,0:T(8,128)(2,1)S(1)} all-to-all(bf16[4,32,256]{2,1,0:T(8,128)(2,1)S(1)} %broadcast_in_dim.6), channel_id=1, replica_groups=mesh['yh'=2,'zh'=4,'zl'=4,'yl'=2,'x'=4,'core'=2] {'zl'}, dimensions={0} | all-to-all | bytes 131072 | tf_op jit(solution)/shard_map/all_to_all | solution.py:184
  64.0 21.2 %all_to_all.22 = bf16[4,32,256]{2,1,0:T(8,128)(2,1)S(1)} all-to-all(bf16[4,32,256]{2,1,0:T(8,128)(2,1)S(1)} %broadcast_in_dim.7), channel_id=1, replica_groups=mesh['yh'=2,'zh'=4,'zl'=4,'yl'=2,'x'=4,'core'=2] {'zh'}, dimensions={0} | all-to-all | bytes 131072 | tf_op jit(solution)/shard_map/all_to_all | solution.py:184
  85.1 0.1 broadcast_in_dim.8
  85.2 17.7 %all_to_all.23 = bf16[32,32,256]{2,1,0:T(8,128)(2,1)S(1)} all-to-all(bf16[32,32,256]{2,1,0:T(8,128)(2,1)S(1)} %broadcast_in_dim.8), channel_id=1, replica_groups=mesh['yh'=2,'zh'=4,'zl'=4,'yl'=2,'x'=4,'core'=2] {'yh','yl','x','core'}, dimensions={0} | all-to-all | bytes 1048576 | tf_op jit(solution)/shard_map/all_to_all | solution.py:184
  102.9 1.1 %bitcast_convert_fusion = f32[1024,256]{1,0:T(8,128)} fusion(bf16[32,32,256]{2,1,0:T(8,128)(2,1)S(1)} %all_to_all.23), kind=kLoop, calls=%fused_computation | loop fusion | flops 262144 | bytes 1572864 | tf_op jit(solution)/shard_map/convert_element_type | solution.py:278
  (4 shorter events, 0.0 us)
Async XLA Ops:
  2.6 9.9 %collective-permute-start = (bf16[592,256]{1,0:T(8,128)(2,1)}, bf16[592,256]{1,0:T(8,128)(2,1)S(1)}, u32[]{:S(2)}, u32[]{:S(2)}) collective-permute-start(bf16[592,256]{1,0:T(8,128)(2,1)} %get-tuple-element.21), channel_id=1, source_target_pairs={{0,16},{16,32},{32,48},{48,64},{64,80},{80,96},{96,112},{112,128},... | collective-permute-start | bytes 909320 | tf_op jit(solution)/shard_map/ppermute | solution.py:26
  7.0 7.9 %collective-permute-start.1 = (bf16[592,256]{1,0:T(8,128)(2,1)}, bf16[592,256]{1,0:T(8,128)(2,1)S(1)}, u32[]{:S(2)}, u32[]{:S(2)}) collective-permute-start(bf16[592,256]{1,0:T(8,128)(2,1)} %get-tuple-element.22), channel_id=1, source_target_pairs={{16,0},{32,16},{48,32},{64,48},{80,64},{96,80},{112,96},{128,112},... | collective-permute-start | bytes 909320 | tf_op jit(solution)/shard_map/ppermute | solution.py:26
  8.3 1.0 copy-start
  9.3 1.0 %copy-start.1 = (bf16[1024,256]{1,0:T(8,128)(2,1)S(1)}, bf16[1024,256]{1,0:T(8,128)(2,1)}, u32[]{:S(2)}) copy-start(bf16[1024,256]{1,0:T(8,128)(2,1)} %weight_ref.1) | copy-start | bytes 1572868
  10.3 1.0 copy-start.2
  11.3 0.9 copy-start.3
  15.0 13.5 %collective-permute-start.2 = (bf16[13,64,256]{2,1,0:T(8,128)(2,1)S(1)}, bf16[13,64,256]{2,1,0:T(8,128)(2,1)S(1)}, u32[]{:S(2)}, u32[]{:S(2)}) collective-permute-start(bf16[13,64,256]{2,1,0:T(8,128)(2,1)S(1)} %get-tuple-element.33), channel_id=1, source_target_pairs={{0,15},{1,2},{2,1},{3,4},{4,3},{5,6},{6,5},{7,8},{8,7},{9,10},{10,... | collective-permute-start | bytes 1277960 | tf_op jit(solution)/shard_map/ppermute | solution.py:232
  21.9 6.5 %collective-permute-start.3 = (bf16[13,64,256]{2,1,0:T(8,128)(2,1)S(1)}, bf16[13,64,256]{2,1,0:T(8,128)(2,1)S(1)}, u32[]{:S(2)}, u32[]{:S(2)}) collective-permute-start(bf16[13,64,256]{2,1,0:T(8,128)(2,1)S(1)} %get-tuple-element.34), channel_id=1, source_target_pairs={{0,1},{1,0},{2,3},{3,2},{4,5},{5,4},{6,7},{7,6},{8,9},{9,8},{10,11... | collective-permute-start | bytes 1277960 | tf_op jit(solution)/shard_map/ppermute | solution.py:235

commit v7 on v5

--- a/solution.py
+++ b/solution.py
@@ -8,9 +8,9 @@
 from jax.experimental.pallas import tpu as pltpu
 from jax.sharding import Mesh, PartitionSpec as P
 
-LAT_AXES = ("yh", "z")
+LAT_AXES = ("yh", "zh", "zl")
 LON_AXES = ("yl", "x", "core")
-PLANE = ("yh", "yl", "x", "core")
+NEAR = ("yh", "zl", "yl", "x", "core")
 
 ROWS, COLS, CH, NK, NR, RAD, HALF = 5, 128, 256, 4, 9, 4, 64
 EXT = ROWS + 2 * RAD
@@ -263,18 +263,17 @@
         name="outer_band",
     )(bands, across, beside, part, field_t, mixing)
 
-    plane, depth = sizes["yh"] * lon_count, lat_count // sizes["yh"]
-    piece = gw.shape[0] // plane
-    got = exchange(gw.reshape(plane, piece, CH), PLANE)
-    mine = jnp.sum(got.astype(jnp.float32), axis=0).astype(jnp.bfloat16)
-    got = exchange(jnp.broadcast_to(mine[None], (depth, piece, CH)), "z")
-    mine = jnp.sum(got.astype(jnp.float32), axis=0).astype(jnp.bfloat16)
-    got = exchange(jnp.broadcast_to(mine[None], (plane, piece, CH)), PLANE)
+    near = math.prod(sizes[a] for a in NEAR)
+    piece = gw.shape[0] // near
+    got = exchange(gw.reshape(near, piece, CH), NEAR)
+    for axes, count in (("zh", sizes["zh"]), (NEAR, near)):
+        mine = jnp.sum(got.astype(jnp.float32), axis=0).astype(jnp.bfloat16)
+        got = exchange(jnp.broadcast_to(mine[None], (count, piece, CH)), axes)
     return (grad_field, got.reshape(NK * CH, CH).astype(jnp.float32))
 
 
 def solution(mesh):
-    fine = Mesh(mesh.devices.reshape(2, 16, 2, 4, 2), LAT_AXES + LON_AXES)
+    fine = Mesh(mesh.devices.reshape(2, 8, 2, 2, 4, 2), LAT_AXES + LON_AXES)
     return jax.shard_map(
         per_device,
         mesh=fine,

time: 100 us -> 98.2 us (0.982)
  blocking collectives: 66.6 us -> 64.4 us
    all_to_all x3, blocking collectives: 66.6 us -> 64.4 us  [exchange(): return lax.all_to_all(x, axes, 0, 0, tiled=True)]
where the time goes in v7:
time: 98.2 us; the launch traced here: 97.8 us
  blocking collectives  64.4 us (66%)
  starting transfers between devices  15.6 us (16%)
  Pallas kernels  9.38 us (10%)
  local copies, waits for them, and re-layouts  3.92 us (4%)
  waiting for transfers between devices  2.47 us (3%)
  other arithmetic  1.2 us (1%)
    all_to_all x3, blocking collectives, exchange(): return lax.all_to_all(x, axes, 0, 0, tiled=True)  64.4 us
    ppermute x1, starting transfers between devices, per_device(): lax.ppermute(across, LON_AXES, [(i, (i - 1 + 2 * (i % 2)) % lon_count) fo...  6.94 us
    ppermute x2, starting transfers between devices, shifted(): return lax.ppermute(x, axes, pairs)  5.68 us
    unnamed x8, local copies, waits for them, and re-layouts  3.87 us
    pallas_call x1, Pallas kernels, per_device(): pl.pallas_call(functools.partial(outer_kernel, scale), out_shape=(jax.Sha...  3.59 us
    pallas_call x1, Pallas kernels, per_device(): pl.pallas_call(inner_kernel, out_shape=(jax.ShapeDtypeStruct((ROWS, NK *...  3.51 us
    ppermute x1, starting transfers between devices, per_device(): beside = lax.ppermute(beside, 'core', [(0, 1), (1, 0)])  3.02 us
    ppermute x2, waiting for transfers between devices, shifted(): return lax.ppermute(x, axes, pairs)  2.47 us
  transfers between devices with their start and end apart: 4, of which 1 were waited for; matrix products, arithmetic and copies ran while one was open for 0% of the time, Pallas kernels for 4%

profile of v7, /device:TPU:1, one launch (start us, length us, event | category | flops | bytes accessed | tf_op | source)
XLA Modules:
  0.0 97.8 jit_solution(10443827397390491207)
XLA Ops:
  0.6 2.0 %prep.1 = (bf16[592,256]{1,0:T(8,128)(2,1)}, bf16[592,256]{1,0:T(8,128)(2,1)}, f32[192,128]{1,0:T(8,128)}) custom-call(s32[5,2,9]{2,1,0:T(2,128)} %bitcast.12, f32[5,9,4,128]{3,2,1,0:T(4,128)} %bitcast.11, bf16[640,256]{1,0:T(8,128)(2,1)} %bitcast.8), custom_call_target="tpu_custom_call" | custom-call | tf_op jit(solution)/shard_map/prep/pallas_call | solution.py:188
  2.6 4.4 %collective-permute-start = (bf16[592,256]{1,0:T(8,128)(2,1)}, bf16[592,256]{1,0:T(8,128)(2,1)S(1)}, u32[]{:S(2)}, u32[]{:S(2)}) collective-permute-start(bf16[592,256]{1,0:T(8,128)(2,1)} %get-tuple-element.21), channel_id=1, source_target_pairs={{0,16},{16,32},{32,48},{48,64},{64,80},{80,96},{96,112},{112,128},... | collective-permute-start | bytes 909320 | tf_op jit(solution)/shard_map/ppermute | solution.py:26
  7.0 1.3 %collective-permute-start.1 = (bf16[592,256]{1,0:T(8,128)(2,1)}, bf16[592,256]{1,0:T(8,128)(2,1)S(1)}, u32[]{:S(2)}, u32[]{:S(2)}) collective-permute-start(bf16[592,256]{1,0:T(8,128)(2,1)} %get-tuple-element.22), channel_id=1, source_target_pairs={{16,0},{32,16},{48,32},{64,48},{80,64},{96,80},{112,96},{128,112},... | collective-permute-start | bytes 909320 | tf_op jit(solution)/shard_map/ppermute | solution.py:26
  8.3 0.0 copy-start
  8.3 1.0 copy-done
  9.3 0.0 copy-start.1
  9.3 1.0 %copy-done.1 = bf16[1024,256]{1,0:T(8,128)(2,1)S(1)} copy-done((bf16[1024,256]{1,0:T(8,128)(2,1)S(1)}, bf16[1024,256]{1,0:T(8,128)(2,1)}, u32[]{:S(2)}) %copy-start.1) | copy-done | bytes 524312
  10.3 0.0 copy-start.2
  10.3 1.0 copy-done.2
  11.3 0.0 copy-start.3
  11.3 0.9 copy-done.3
  12.2 0.3 own.1
  12.4 0.0 collective-permute-done.up_ref
  12.5 2.5 %collective-permute-done.1.down_ref = bf16[592,256]{1,0:T(8,128)(2,1)S(1)} collective-permute-done((bf16[592,256]{1,0:T(8,128)(2,1)}, bf16[592,256]{1,0:T(8,128)(2,1)S(1)}, u32[]{:S(2)}, u32[]{:S(2)}) %collective-permute-start.1) | collective-permute-done | bytes 303136 | tf_op jit(solution)/shard_map/ppermute | solution.py:26
  14.9 0.1 middle.1
  15.0 6.9 %collective-permute-start.2 = (bf16[13,64,256]{2,1,0:T(8,128)(2,1)S(1)}, bf16[13,64,256]{2,1,0:T(8,128)(2,1)S(1)}, u32[]{:S(2)}, u32[]{:S(2)}) collective-permute-start(bf16[13,64,256]{2,1,0:T(8,128)(2,1)S(1)} %get-tuple-element.33), channel_id=1, source_target_pairs={{0,15},{1,2},{2,1},{3,4},{4,3},{5,6},{6,5},{7,8},{8,7},{9,10},{10,... | collective-permute-start | bytes 1277960 | tf_op jit(solution)/shard_map/ppermute | solution.py:226
  21.9 3.0 %collective-permute-start.3 = (bf16[13,64,256]{2,1,0:T(8,128)(2,1)S(1)}, bf16[13,64,256]{2,1,0:T(8,128)(2,1)S(1)}, u32[]{:S(2)}, u32[]{:S(2)}) collective-permute-start(bf16[13,64,256]{2,1,0:T(8,128)(2,1)S(1)} %get-tuple-element.34), channel_id=1, source_target_pairs={{0,1},{1,0},{2,3},{3,2},{4,5},{5,4},{6,7},{7,6},{8,9},{9,8},{10,11... | collective-permute-start | bytes 1277960 | tf_op jit(solution)/shard_map/ppermute | solution.py:229
  25.0 3.5 %inner_band.1 = (f32[5,512,256]{2,1,0:T(8,128)S(1)}, bf16[5,512,1152]{2,1,0:T(8,128)(2,1)S(1)}) custom-call(bf16[592,256]{1,0:T(8,128)(2,1)S(1)} %collective-permute-done.up_ref, bf16[5,128,256]{2,1,0:T(8,128)(2,1)S(1)} %get-tuple-element.29.own_ref, bf16[592,256]{1,0:T(8,128)(2,1)S(1)} %collective-permute-done.1.down_ref, ...), custom_call_target="tpu_custom_call" | custom-call | flops 1509949440 | bytes 4194304 | tf_op jit(solution)/shard_map/inner_band/pallas_call | solution.py:233
  28.5 0.0 collective-permute-done.2.across
  28.5 0.0 collective-permute-done.3.beside
  28.5 3.6 %outer_band.1 = (f32[5,128,256]{2,1,0:T(8,128)}, bf16[1024,256]{1,0:T(8,128)(2,1)S(1)}) custom-call(bf16[5,512,1152]{2,1,0:T(8,128)(2,1)S(1)} %get-tuple-element.32.bands, bf16[13,64,256]{2,1,0:T(8,128)(2,1)S(1)} %collective-permute-done.2.across, bf16[13,64,256]{2,1,0:T(8,128)(2,1)S(1)} %collective-permute-done.3.beside, ...), custom_call_target="tpu_custom_call" | custom-call | flops 3019898880 | bytes 6291456 | tf_op jit(solution)/shard_map/outer_band/pallas_call | solution.py:252
  32.1 25.6 %all_to_all.15 = bf16[64,16,256]{2,1,0:T(8,128)(2,1)S(1)} all-to-all(bf16[64,16,256]{2,1,0:T(8,128)(2,1)S(1)} %bitcast.9), channel_id=1, replica_groups=mesh['yh'=2,'zh'=8,'zl'=2,'yl'=2,'x'=4,'core'=2] {'yh','zl','yl','x','co..., dimensions={0} | all-to-all | bytes 1048576 | tf_op jit(solution)/shard_map/all_to_all | solution.py:178
  57.7 0.1 reduce_sum.24
  57.8 20.2 %all_to_all.16 = bf16[8,16,256]{2,1,0:T(8,128)(2,1)S(1)} all-to-all(bf16[8,16,256]{2,1,0:T(8,128)(2,1)S(1)} %broadcast_in_dim.4), channel_id=1, replica_groups=mesh['yh'=2,'zh'=8,'zl'=2,'yl'=2,'x'=4,'core'=2] {'zh'}, dimensions={0} | all-to-all | bytes 131072 | tf_op jit(solution)/shard_map/all_to_all | solution.py:178
  78.0 18.7 %all_to_all.17 = bf16[64,16,256]{2,1,0:T(8,128)(2,1)S(1)} all-to-all(bf16[64,16,256]{2,1,0:T(8,128)(2,1)S(1)} %broadcast_in_dim.5), channel_id=1, replica_groups=mesh['yh'=2,'zh'=8,'zl'=2,'yl'=2,'x'=4,'core'=2] {'yh','zl','yl','x','co..., dimensions={0} | all-to-all | bytes 1048576 | tf_op jit(solution)/shard_map/all_to_all | solution.py:178
  96.7 1.1 %bitcast_convert_fusion = f32[1024,256]{1,0:T(8,128)} fusion(bf16[64,16,256]{2,1,0:T(8,128)(2,1)S(1)} %all_to_all.17), kind=kLoop, calls=%fused_computation | loop fusion | flops 262144 | bytes 1572864 | tf_op jit(solution)/shard_map/convert_element_type | solution.py:272
  (3 shorter events, 0.1 us)
Async XLA Ops:
  2.6 9.9 %collective-permute-start = (bf16[592,256]{1,0:T(8,128)(2,1)}, bf16[592,256]{1,0:T(8,128)(2,1)S(1)}, u32[]{:S(2)}, u32[]{:S(2)}) collective-permute-start(bf16[592,256]{1,0:T(8,128)(2,1)} %get-tuple-element.21), channel_id=1, source_target_pairs={{0,16},{16,32},{32,48},{48,64},{64,80},{80,96},{96,112},{112,128},... | collective-permute-start | bytes 909320 | tf_op jit(solution)/shard_map/ppermute | solution.py:26
  7.0 7.9 %collective-permute-start.1 = (bf16[592,256]{1,0:T(8,128)(2,1)}, bf16[592,256]{1,0:T(8,128)(2,1)S(1)}, u32[]{:S(2)}, u32[]{:S(2)}) collective-permute-start(bf16[592,256]{1,0:T(8,128)(2,1)} %get-tuple-element.22), channel_id=1, source_target_pairs={{16,0},{32,16},{48,32},{64,48},{80,64},{96,80},{112,96},{128,112},... | collective-permute-start | bytes 909320 | tf_op jit(solution)/shard_map/ppermute | solution.py:26
  8.3 1.0 copy-start
  9.3 1.0 %copy-start.1 = (bf16[1024,256]{1,0:T(8,128)(2,1)S(1)}, bf16[1024,256]{1,0:T(8,128)(2,1)}, u32[]{:S(2)}) copy-start(bf16[1024,256]{1,0:T(8,128)(2,1)} %weight_ref.1) | copy-start | bytes 1572868
  10.3 1.0 copy-start.2
  11.3 0.9 copy-start.3
  15.0 13.5 %collective-permute-start.2 = (bf16[13,64,256]{2,1,0:T(8,128)(2,1)S(1)}, bf16[13,64,256]{2,1,0:T(8,128)(2,1)S(1)}, u32[]{:S(2)}, u32[]{:S(2)}) collective-permute-start(bf16[13,64,256]{2,1,0:T(8,128)(2,1)S(1)} %get-tuple-element.33), channel_id=1, source_target_pairs={{0,15},{1,2},{2,1},{3,4},{4,3},{5,6},{6,5},{7,8},{8,7},{9,10},{10,... | collective-permute-start | bytes 1277960 | tf_op jit(solution)/shard_map/ppermute | solution.py:226
  21.9 6.6 %collective-permute-start.3 = (bf16[13,64,256]{2,1,0:T(8,128)(2,1)S(1)}, bf16[13,64,256]{2,1,0:T(8,128)(2,1)S(1)}, u32[]{:S(2)}, u32[]{:S(2)}) collective-permute-start(bf16[13,64,256]{2,1,0:T(8,128)(2,1)S(1)} %get-tuple-element.34), channel_id=1, source_target_pairs={{0,1},{1,0},{2,3},{3,2},{4,5},{5,4},{6,7},{7,6},{8,9},{9,8},{10,11... | collective-permute-start | bytes 1277960 | tf_op jit(solution)/shard_map/ppermute | solution.py:229

commit v8 on v7

--- a/solution.py
+++ b/solution.py
@@ -15,31 +15,42 @@
 ROWS, COLS, CH, NK, NR, RAD, HALF = 5, 128, 256, 4, 9, 4, 64
 EXT = ROWS + 2 * RAD
 LINES = NK * NR
-LINES_ROWS = RAD * LINES // 2
-PACKED = RAD * COLS + 80
+CELL_ROWS = RAD * COLS
+PACK_ROWS = 32
+PACKED = CELL_ROWS + PACK_ROWS
 VMEM_LIMIT = 32 * 1024 * 1024
 
 
-def shifted(x, axes, step):
+def swapped(x, axes, start):
     count = math.prod(lax.axis_size(a) for a in axes)
-    pairs = [(i, i + step) for i in range(count) if 0 <= i + step < count]
-    return lax.ppermute(x, axes, pairs)
+    pairs = [(i, i + 1) for i in range(start, count - 1, 2)]
+    return lax.ppermute(x, axes, pairs + [(j, i) for i, j in pairs])
+
+
+def packed_groups():
+    above = [(n, NR - 1 - n + t) for n in range(RAD) for t in range(n + 1)]
+    below = [(n, t) for n in range(RAD) for t in range(RAD - n)]
+    for place, (one, two) in enumerate(zip(above, below)):
+        half = len(above) // 2
+        yield (place // half) * PACK_ROWS + (place % half) * NK, one, two
 
 
 def prep_kernel(
-    bounds_hbm, values_hbm, cells_hbm, up_ref, down_ref, own_ref, bounds, values, lines, sems
+    bounds_hbm, values_hbm, cells_hbm, far_ref, near_ref, own_ref, bounds, values, lines, wide, sems
 ):
-    cell_rows = RAD * COLS
+    odd = lax.axis_index("zl")
     copies = [
         pltpu.make_async_copy(bounds_hbm, bounds, sems.at[0]),
         pltpu.make_async_copy(values_hbm, values, sems.at[1]),
         pltpu.make_async_copy(
-            cells_hbm.at[pl.ds((ROWS - RAD) * COLS, cell_rows)],
-            up_ref.at[pl.ds(0, cell_rows)],
+            cells_hbm.at[pl.ds(pl.multiple_of(odd * COLS, COLS), CELL_ROWS)],
+            far_ref.at[pl.ds(0, CELL_ROWS)],
             sems.at[2],
         ),
         pltpu.make_async_copy(
-            cells_hbm.at[pl.ds(0, cell_rows)], down_ref.at[pl.ds(0, cell_rows)], sems.at[3]
+            cells_hbm.at[pl.ds(pl.multiple_of((1 - odd) * COLS, COLS), CELL_ROWS)],
+            near_ref.at[pl.ds(0, CELL_ROWS)],
+            sems.at[3],
         ),
     ]
     for copy in copies:
@@ -59,15 +70,16 @@
     own_ref[...] = jnp.dot(
         lines[...].astype(jnp.bfloat16), flip, preferred_element_type=jnp.float32
     )
-    for ref, row in ((up_ref, ROWS - RAD), (down_ref, 0)):
+    wide[...] = jnp.zeros(wide.shape, jnp.float32)
+    for place, above, below in packed_groups():
+        for side, (row, r) in enumerate(((ROWS - RAD + above[0], above[1]), below)):
+            at = LINES * row + NK * r
+            wide[side, place : place + NK, :] = own_ref[at : at + NK, :]
+    for side, ref in ((1 - odd, far_ref), (odd, near_ref)):
         for half in range(2):
-            at = LINES * row + half * LINES_ROWS
-            ref[cell_rows : cell_rows + LINES_ROWS, half * COLS : (half + 1) * COLS] = own_ref[
-                at : at + LINES_ROWS, :
+            ref[CELL_ROWS:, half * COLS : (half + 1) * COLS] = wide[
+                side, half * PACK_ROWS : (half + 1) * PACK_ROWS, :
             ].astype(jnp.bfloat16)
-        ref[cell_rows + LINES_ROWS :, :] = jnp.zeros(
-            (PACKED - cell_rows - LINES_ROWS, CH), jnp.bfloat16
-        )
     copies[2].wait()
     copies[3].wait()
 
@@ -89,25 +101,45 @@
         yield down_ref[n * COLS : (n + 1) * COLS, :]
 
 
-def middle_kernel(up_ref, own_ref, down_ref, across_ref, beside_ref):
+def by_parity(far_ref, near_ref, body):
+    odd = lax.axis_index("zl")
+
+    @pl.when(odd == 0)
+    def _():
+        body(far_ref, near_ref)
+
+    @pl.when(odd == 1)
+    def _():
+        body(near_ref, far_ref)
+
+
+def middle_kernel(far_ref, own_ref, near_ref, across_ref, beside_ref):
     first = pl.multiple_of(lax.axis_index("core") * HALF, HALF)
     other = pl.multiple_of(HALF - first, HALF)
-    for n in range(RAD):
-        across_ref[n] = up_ref[pl.ds(n * COLS + first, HALF), :]
-        beside_ref[n] = up_ref[pl.ds(n * COLS + other, HALF), :]
-        across_ref[RAD + ROWS + n] = down_ref[pl.ds(n * COLS + first, HALF), :]
-        beside_ref[RAD + ROWS + n] = down_ref[pl.ds(n * COLS + other, HALF), :]
+
+    def halo(up_ref, down_ref):
+        for n in range(RAD):
+            across_ref[n] = up_ref[pl.ds(n * COLS + first, HALF), :]
+            beside_ref[n] = up_ref[pl.ds(n * COLS + other, HALF), :]
+            across_ref[RAD + ROWS + n] = down_ref[pl.ds(n * COLS + first, HALF), :]
+            beside_ref[RAD + ROWS + n] = down_ref[pl.ds(n * COLS + other, HALF), :]
+
+    by_parity(far_ref, near_ref, halo)
     for n in range(ROWS):
         across_ref[RAD + n] = own_ref[n, pl.ds(first, HALF), :]
         beside_ref[RAD + n] = own_ref[n, pl.ds(other, HALF), :]
 
 
-def gather_lines(up_ref, own_ref, down_ref, lines_ref):
-    for ref, at in ((up_ref, 0), (down_ref, (RAD + ROWS) * LINES)):
+def gather_lines(up_ref, own_ref, down_ref, lines_ref, wide):
+    for side, ref in enumerate((up_ref, down_ref)):
         for half in range(2):
-            lines_ref[at + half * LINES_ROWS : at + (half + 1) * LINES_ROWS, :] = ref[
-                RAD * COLS : RAD * COLS + LINES_ROWS, half * COLS : (half + 1) * COLS
+            wide[side, half * PACK_ROWS : (half + 1) * PACK_ROWS, :] = ref[
+                CELL_ROWS:, half * COLS : (half + 1) * COLS
             ].astype(jnp.float32)
+    for place, above, below in packed_groups():
+        for side, (row, r) in enumerate((above, (RAD + ROWS + below[0], below[1]))):
+            at = LINES * row + NK * r
+            lines_ref[at : at + NK, :] = wide[side, place : place + NK, :]
     lines_ref[RAD * LINES : (RAD + ROWS) * LINES, :] = own_ref[: ROWS * LINES, :]
 
 
@@ -132,12 +164,15 @@
 
 
 def inner_kernel(
-    up_ref, own_ref, down_ref, lines_own, part_ref, outer_ref, lines, cells, bands
+    far_ref, own_ref, near_ref, lines_own, part_ref, outer_ref, lines, wide, cells, bands
 ):
-    gather_lines(up_ref, lines_own, down_ref, lines)
-    for row, one in enumerate(rows_in_reach(up_ref, own_ref, down_ref)):
-        cells[row * COLS : row * COLS + HALF, :] = one[HALF:]
-        cells[row * COLS + HALF : (row + 1) * COLS, :] = one[:HALF]
+    def load(up_ref, down_ref):
+        gather_lines(up_ref, lines_own, down_ref, lines, wide)
+        for row, one in enumerate(rows_in_reach(up_ref, own_ref, down_ref)):
+            cells[row * COLS : row * COLS + HALF, :] = one[HALF:]
+            cells[row * COLS + HALF : (row + 1) * COLS, :] = one[:HALF]
+
+    by_parity(far_ref, near_ref, load)
     mask = own_mask().astype(jnp.float32)
     inner_mask, outer_mask = mask.astype(jnp.bfloat16), (1.0 - mask).astype(jnp.bfloat16)
     for l in range(ROWS):
@@ -184,8 +219,9 @@
     lon_count = math.prod(sizes[a] for a in LON_AXES)
     params = pltpu.CompilerParams(vmem_limit_bytes=VMEM_LIMIT)
     hbm = pl.BlockSpec(memory_space=pltpu.HBM)
+    wide = pltpu.VMEM((2, 2 * PACK_ROWS, COLS), jnp.float32)
     packed = jax.ShapeDtypeStruct((PACKED, CH), jnp.bfloat16)
-    up_own, down_own, lines_own = pl.pallas_call(
+    far, near, lines_own = pl.pallas_call(
         prep_kernel,
         out_shape=(packed, packed, jax.ShapeDtypeStruct((192, COLS), jnp.float32)),
         in_specs=[hbm, hbm, hbm],
@@ -193,6 +229,7 @@
             pltpu.SMEM((ROWS, 2, NR), jnp.int32),
             pltpu.VMEM((ROWS, NR, NK, COLS), jnp.float32),
             pltpu.VMEM((192, COLS), jnp.float32),
+            wide,
             pltpu.SemaphoreType.DMA((4,)),
         ],
         compiler_params=pltpu.CompilerParams(vmem_limit_bytes=60 * 1024 * 1024),
@@ -214,15 +251,15 @@
         cost_estimate=pl.CostEstimate(flops=0, bytes_accessed=4 * 1024 * 1024, transcendentals=0),
         name="own",
     )(cotangent, lines_own, field.reshape(ROWS * COLS, CH), weight)
-    up = shifted(up_own, LAT_AXES, 1)
-    down = shifted(down_own, LAT_AXES, -1)
-    up, down, own, lines_own, field_t, mixing = lax.optimization_barrier(
-        (up, down, own, lines_own, field_t, mixing)
+    far = swapped(far, LAT_AXES, 1)
+    near = swapped(near, LAT_AXES, 0)
+    far, near, own, lines_own, field_t, mixing = lax.optimization_barrier(
+        (far, near, own, lines_own, field_t, mixing)
     )
     side = jax.ShapeDtypeStruct((EXT, HALF, CH), jnp.bfloat16)
     across, beside = pl.pallas_call(
         middle_kernel, out_shape=(side, side), compiler_params=params, name="middle"
-    )(up, own, down)
+    )(far, own, near)
     across = lax.ppermute(
         across, LON_AXES, [(i, (i - 1 + 2 * (i % 2)) % lon_count) for i in range(lon_count)]
     )
@@ -238,6 +275,7 @@
         ),
         scratch_shapes=[
             pltpu.VMEM((EXT * LINES, COLS), jnp.float32),
+            wide,
             cells,
             pltpu.VMEM((2, NK * COLS, NR * COLS), jnp.bfloat16),
         ],
@@ -246,7 +284,7 @@
             flops=band_flops, bytes_accessed=4 * 1024 * 1024, transcendentals=0
         ),
         name="inner_band",
-    )(up, own, down, lines_own)
+    )(far, own, near, lines_own)
 
     scale = 1.0 / math.sqrt(ROWS * lat_count * COLS * lon_count)
     grad_field, gw = pl.pallas_call(

time: 98.2 us -> 97.3 us (level)
  waiting for transfers between devices: 2.47 us -> 0.8 us
  starting transfers between devices: 15.6 us -> 16.9 us
    ppermute x2, starting transfers between devices: 5.68 us -> 7.92 us  [swapped(): return lax.ppermute(x, axes, pairs + [(j, i) for i, j in pairs])]
    ppermute x2, waiting for transfers between devices: 2.47 us -> 0.8 us  [swapped(): return lax.ppermute(x, axes, pairs + [(j, i) for i, j in pairs])]
    ppermute x1, starting transfers between devices: 6.94 us -> 5.85 us  [per_device(): lax.ppermute(across, LON_AXES, [(i, (i - 1 + 2 * (i % 2)) % lon_count) fo...]
where the time goes in v8:
time: 97.3 us; the launch traced here: 96.9 us
  blocking collectives  63.9 us (66%)
  starting transfers between devices  16.9 us (17%)
  Pallas kernels  9.4 us (10%)
  local copies, waits for them, and re-layouts  3.92 us (4%)
  other arithmetic  1.2 us (1%)
    all_to_all x3, blocking collectives, exchange(): return lax.all_to_all(x, axes, 0, 0, tiled=True)  63.9 us
    ppermute x2, starting transfers between devices, swapped(): return lax.ppermute(x, axes, pairs + [(j, i) for i, j in pairs])  7.92 us
    ppermute x1, starting transfers between devices, per_device(): lax.ppermute(across, LON_AXES, [(i, (i - 1 + 2 * (i % 2)) % lon_count) fo...  5.85 us
    unnamed x8, local copies, waits for them, and re-layouts  3.87 us
    pallas_call x1, Pallas kernels, per_device(): pl.pallas_call(inner_kernel, out_shape=(jax.ShapeDtypeStruct((ROWS, NK *...  3.57 us
    pallas_call x1, Pallas kernels, per_device(): pl.pallas_call(functools.partial(outer_kernel, scale), out_shape=(jax.Sha...  3.56 us
    ppermute x1, starting transfers between devices, per_device(): beside = lax.ppermute(beside, 'core', [(0, 1), (1, 0)])  3.15 us
  transfers between devices with their start and end apart: 4, of which 1 were waited for; matrix products, arithmetic and copies ran while one was open for 0% of the time, Pallas kernels for 4%

profile of v8, /device:TPU:1, one launch (start us, length us, event | category | flops | bytes accessed | tf_op | source)
XLA Modules:
  0.0 96.9 jit_solution(13729308872712244976)
XLA Ops:
  0.6 1.9 %prep.1 = (bf16[544,256]{1,0:T(8,128)(2,1)}, bf16[544,256]{1,0:T(8,128)(2,1)}, f32[192,128]{1,0:T(8,128)}) custom-call(s32[5,2,9]{2,1,0:T(2,128)} %bitcast.12, f32[5,9,4,128]{3,2,1,0:T(4,128)} %bitcast.11, bf16[640,256]{1,0:T(8,128)(2,1)} %bitcast.8), custom_call_target="tpu_custom_call" | custom-call | tf_op jit(solution)/shard_map/prep/pallas_call | solution.py:224
  2.6 0.7 collective-permute-start
  3.3 7.2 %collective-permute-start.1 = (bf16[544,256]{1,0:T(8,128)(2,1)}, bf16[544,256]{1,0:T(8,128)(2,1)S(1)}, u32[]{:S(2)}, u32[]{:S(2)}) collective-permute-start(bf16[544,256]{1,0:T(8,128)(2,1)} %get-tuple-element.22), channel_id=1, source_target_pairs={{0,16},{32,48},{64,80},{96,112},{128,144},{160,176},{192,208},{224... | collective-permute-start | bytes 835592 | tf_op jit(solution)/shard_map/ppermute | solution.py:27
  10.5 0.0 copy-start
  10.5 1.0 copy-done
  11.5 0.0 copy-start.1
  11.5 1.0 %copy-done.1 = bf16[1024,256]{1,0:T(8,128)(2,1)S(1)} copy-done((bf16[1024,256]{1,0:T(8,128)(2,1)S(1)}, bf16[1024,256]{1,0:T(8,128)(2,1)}, u32[]{:S(2)}) %copy-start.1) | copy-done | bytes 524312
  12.5 0.0 copy-start.2
  12.5 1.0 %copy-done.2 = bf16[5,128,256]{2,1,0:T(8,128)(2,1)S(1)} copy-done((bf16[5,128,256]{2,1,0:T(8,128)(2,1)S(1)}, bf16[5,128,256]{2,1,0:T(8,128)(2,1)}, u32[]{:S(2)}) %copy-start.2) | copy-done | bytes 327704
  13.5 0.0 copy-start.3
  13.5 0.9 copy-done.3
  14.4 0.3 own.1
  14.7 0.0 collective-permute-done.far_ref
  14.7 0.8 collective-permute-done.1.near_ref
  15.5 0.1 middle.1
  15.5 5.8 %collective-permute-start.2 = (bf16[13,64,256]{2,1,0:T(8,128)(2,1)S(1)}, bf16[13,64,256]{2,1,0:T(8,128)(2,1)S(1)}, u32[]{:S(2)}, u32[]{:S(2)}) collective-permute-start(bf16[13,64,256]{2,1,0:T(8,128)(2,1)S(1)} %get-tuple-element.33), channel_id=1, source_target_pairs={{0,15},{1,2},{2,1},{3,4},{4,3},{5,6},{6,5},{7,8},{8,7},{9,10},{10,... | collective-permute-start | bytes 1277960 | tf_op jit(solution)/shard_map/ppermute | solution.py:263
  21.4 3.2 %collective-permute-start.3 = (bf16[13,64,256]{2,1,0:T(8,128)(2,1)S(1)}, bf16[13,64,256]{2,1,0:T(8,128)(2,1)S(1)}, u32[]{:S(2)}, u32[]{:S(2)}) collective-permute-start(bf16[13,64,256]{2,1,0:T(8,128)(2,1)S(1)} %get-tuple-element.34), channel_id=1, source_target_pairs={{0,1},{1,0},{2,3},{3,2},{4,5},{5,4},{6,7},{7,6},{8,9},{9,8},{10,11... | collective-permute-start | bytes 1277960 | tf_op jit(solution)/shard_map/ppermute | solution.py:266
  24.6 3.6 %inner_band.1 = (f32[5,512,256]{2,1,0:T(8,128)S(1)}, bf16[5,512,1152]{2,1,0:T(8,128)(2,1)S(1)}) custom-call(bf16[544,256]{1,0:T(8,128)(2,1)S(1)} %collective-permute-done.far_ref, bf16[5,128,256]{2,1,0:T(8,128)(2,1)S(1)} %get-tuple-element.29.own_ref, bf16[544,256]{1,0:T(8,128)(2,1)S(1)} %collective-permute-done.1.near_ref, ...), custom_call_target="tpu_custom_call" | custom-call | flops 1509949440 | bytes 4194304 | tf_op jit(solution)/shard_map/inner_band/pallas_call | solution.py:270
  28.1 0.0 collective-permute-done.2.across
  28.1 0.0 collective-permute-done.3.beside
  28.2 3.6 %outer_band.1 = (f32[5,128,256]{2,1,0:T(8,128)}, bf16[1024,256]{1,0:T(8,128)(2,1)S(1)}) custom-call(bf16[5,512,1152]{2,1,0:T(8,128)(2,1)S(1)} %get-tuple-element.32.bands, bf16[13,64,256]{2,1,0:T(8,128)(2,1)S(1)} %collective-permute-done.2.across, bf16[13,64,256]{2,1,0:T(8,128)(2,1)S(1)} %collective-permute-done.3.beside, ...), custom_call_target="tpu_custom_call" | custom-call | flops 3019898880 | bytes 6291456 | tf_op jit(solution)/shard_map/outer_band/pallas_call | solution.py:290
  31.7 27.2 %all_to_all.15 = bf16[64,16,256]{2,1,0:T(8,128)(2,1)S(1)} all-to-all(bf16[64,16,256]{2,1,0:T(8,128)(2,1)S(1)} %bitcast.9), channel_id=1, replica_groups=mesh['yh'=2,'zh'=8,'zl'=2,'yl'=2,'x'=4,'core'=2] {'yh','zl','yl','x','co..., dimensions={0} | all-to-all | bytes 1048576 | tf_op jit(solution)/shard_map/all_to_all | solution.py:213
  58.9 0.1 reduce_sum.24
  59.1 18.0 %all_to_all.16 = bf16[8,16,256]{2,1,0:T(8,128)(2,1)S(1)} all-to-all(bf16[8,16,256]{2,1,0:T(8,128)(2,1)S(1)} %broadcast_in_dim.4), channel_id=1, replica_groups=mesh['yh'=2,'zh'=8,'zl'=2,'yl'=2,'x'=4,'core'=2] {'zh'}, dimensions={0} | all-to-all | bytes 131072 | tf_op jit(solution)/shard_map/all_to_all | solution.py:213
  77.1 18.7 %all_to_all.17 = bf16[64,16,256]{2,1,0:T(8,128)(2,1)S(1)} all-to-all(bf16[64,16,256]{2,1,0:T(8,128)(2,1)S(1)} %broadcast_in_dim.5), channel_id=1, replica_groups=mesh['yh'=2,'zh'=8,'zl'=2,'yl'=2,'x'=4,'core'=2] {'yh','zl','yl','x','co..., dimensions={0} | all-to-all | bytes 1048576 | tf_op jit(solution)/shard_map/all_to_all | solution.py:213
  95.8 1.1 %bitcast_convert_fusion = f32[1024,256]{1,0:T(8,128)} fusion(bf16[64,16,256]{2,1,0:T(8,128)(2,1)S(1)} %all_to_all.17), kind=kLoop, calls=%fused_computation | loop fusion | flops 262144 | bytes 1572864 | tf_op jit(solution)/shard_map/convert_element_type | solution.py:310
  (3 shorter events, 0.1 us)
Async XLA Ops:
  2.6 12.1 %collective-permute-start = (bf16[544,256]{1,0:T(8,128)(2,1)}, bf16[544,256]{1,0:T(8,128)(2,1)S(1)}, u32[]{:S(2)}, u32[]{:S(2)}) collective-permute-start(bf16[544,256]{1,0:T(8,128)(2,1)} %get-tuple-element.21), channel_id=1, source_target_pairs={{16,32},{48,64},{80,96},{112,128},{144,160},{176,192},{208,224},{2... | collective-permute-start | bytes 835592 | tf_op jit(solution)/shard_map/ppermute | solution.py:27
  3.3 12.2 %collective-permute-start.1 = (bf16[544,256]{1,0:T(8,128)(2,1)}, bf16[544,256]{1,0:T(8,128)(2,1)S(1)}, u32[]{:S(2)}, u32[]{:S(2)}) collective-permute-start(bf16[544,256]{1,0:T(8,128)(2,1)} %get-tuple-element.22), channel_id=1, source_target_pairs={{0,16},{32,48},{64,80},{96,112},{128,144},{160,176},{192,208},{224... | collective-permute-start | bytes 835592 | tf_op jit(solution)/shard_map/ppermute | solution.py:27
  10.5 1.0 %copy-start = (bf16[5,128,256]{2,1,0:T(8,128)(2,1)S(1)}, bf16[5,128,256]{2,1,0:T(8,128)(2,1)}, u32[]{:S(2)}) copy-start(bf16[5,128,256]{2,1,0:T(8,128)(2,1)} %cells_ref.1) | copy-start | bytes 983044
  11.5 1.0 %copy-start.1 = (bf16[1024,256]{1,0:T(8,128)(2,1)S(1)}, bf16[1024,256]{1,0:T(8,128)(2,1)}, u32[]{:S(2)}) copy-start(bf16[1024,256]{1,0:T(8,128)(2,1)} %weight_ref.1) | copy-start | bytes 1572868
  12.5 1.0 %copy-start.2 = (bf16[5,128,256]{2,1,0:T(8,128)(2,1)S(1)}, bf16[5,128,256]{2,1,0:T(8,128)(2,1)}, u32[]{:S(2)}) copy-start(bf16[5,128,256]{2,1,0:T(8,128)(2,1)} %param.5) | copy-start | bytes 983044
  13.5 0.9 copy-start.3
  15.5 12.6 %collective-permute-start.2 = (bf16[13,64,256]{2,1,0:T(8,128)(2,1)S(1)}, bf16[13,64,256]{2,1,0:T(8,128)(2,1)S(1)}, u32[]{:S(2)}, u32[]{:S(2)}) collective-permute-start(bf16[13,64,256]{2,1,0:T(8,128)(2,1)S(1)} %get-tuple-element.33), channel_id=1, source_target_pairs={{0,15},{1,2},{2,1},{3,4},{4,3},{5,6},{6,5},{7,8},{8,7},{9,10},{10,... | collective-permute-start | bytes 1277960 | tf_op jit(solution)/shard_map/ppermute | solution.py:263
  21.4 6.7 %collective-permute-start.3 = (bf16[13,64,256]{2,1,0:T(8,128)(2,1)S(1)}, bf16[13,64,256]{2,1,0:T(8,128)(2,1)S(1)}, u32[]{:S(2)}, u32[]{:S(2)}) collective-permute-start(bf16[13,64,256]{2,1,0:T(8,128)(2,1)S(1)} %get-tuple-element.34), channel_id=1, source_target_pairs={{0,1},{1,0},{2,3},{3,2},{4,5},{5,4},{6,7},{7,6},{8,9},{9,8},{10,11... | collective-permute-start | bytes 1277960 | tf_op jit(solution)/shard_map/ppermute | solution.py:266

commit v9 on v8

--- a/solution.py
+++ b/solution.py
@@ -8,8 +8,9 @@
 from jax.experimental.pallas import tpu as pltpu
 from jax.sharding import Mesh, PartitionSpec as P
 
-LAT_AXES = ("yh", "zh", "zl")
+LAT_AXES = ("yh", "z3", "z2", "z1", "zl")
 LON_AXES = ("yl", "x", "core")
+DEPTH = ("z1", "z2", "z3")
 NEAR = ("yh", "zl", "yl", "x", "core")
 
 ROWS, COLS, CH, NK, NR, RAD, HALF = 5, 128, 256, 4, 9, 4, 64
@@ -304,14 +305,14 @@
     near = math.prod(sizes[a] for a in NEAR)
     piece = gw.shape[0] // near
     got = exchange(gw.reshape(near, piece, CH), NEAR)
-    for axes, count in (("zh", sizes["zh"]), (NEAR, near)):
+    for axes, count in ((DEPTH, math.prod(sizes[a] for a in DEPTH)), (NEAR, near)):
         mine = jnp.sum(got.astype(jnp.float32), axis=0).astype(jnp.bfloat16)
         got = exchange(jnp.broadcast_to(mine[None], (count, piece, CH)), axes)
     return (grad_field, got.reshape(NK * CH, CH).astype(jnp.float32))
 
 
 def solution(mesh):
-    fine = Mesh(mesh.devices.reshape(2, 8, 2, 2, 4, 2), LAT_AXES + LON_AXES)
+    fine = Mesh(mesh.devices.reshape(2, 2, 2, 2, 2, 2, 4, 2), LAT_AXES + LON_AXES)
     return jax.shard_map(
         per_device,
         mesh=fine,

time: 97.3 us -> 96.6 us (level)
  no operation moved by 1% of the time
where the time goes in v9:
time: 96.6 us; the launch traced here: 96.1 us
  blocking collectives  63.1 us (65%)
  starting transfers between devices  16.9 us (17%)
  Pallas kernels  9.4 us (10%)
  local copies, waits for them, and re-layouts  3.92 us (4%)
  other arithmetic  1.2 us (1%)
    all_to_all x3, blocking collectives, exchange(): return lax.all_to_all(x, axes, 0, 0, tiled=True)  63.1 us
    ppermute x2, starting transfers between devices, swapped(): return lax.ppermute(x, axes, pairs + [(j, i) for i, j in pairs])  7.92 us
    ppermute x1, starting transfers between devices, per_device(): lax.ppermute(across, LON_AXES, [(i, (i - 1 + 2 * (i % 2)) % lon_count) fo...  5.85 us
    unnamed x8, local copies, waits for them, and re-layouts  3.87 us
    pallas_call x1, Pallas kernels, per_device(): pl.pallas_call(inner_kernel, out_shape=(jax.ShapeDtypeStruct((ROWS, NK *...  3.57 us
    pallas_call x1, Pallas kernels, per_device(): pl.pallas_call(functools.partial(outer_kernel, scale), out_shape=(jax.Sha...  3.56 us
    ppermute x1, starting transfers between devices, per_device(): beside = lax.ppermute(beside, 'core', [(0, 1), (1, 0)])  3.15 us
    pallas_call x1, Pallas kernels, per_device(): pl.pallas_call(prep_kernel, out_shape=(packed, packed, jax.ShapeDtypeStru...  1.94 us
  transfers between devices with their start and end apart: 4, of which 1 were waited for; matrix products, arithmetic and copies ran while one was open for 0% of the time, Pallas kernels for 4%

profile of v9, /device:TPU:1, one launch (start us, length us, event | category | flops | bytes accessed | tf_op | source)
XLA Modules:
  0.0 96.1 jit_solution(816906868376923920)
XLA Ops:
  0.6 1.9 %prep.1 = (bf16[544,256]{1,0:T(8,128)(2,1)}, bf16[544,256]{1,0:T(8,128)(2,1)}, f32[192,128]{1,0:T(8,128)}) custom-call(s32[5,2,9]{2,1,0:T(2,128)} %bitcast.12, f32[5,9,4,128]{3,2,1,0:T(4,128)} %bitcast.11, bf16[640,256]{1,0:T(8,128)(2,1)} %bitcast.8), custom_call_target="tpu_custom_call" | custom-call | tf_op jit(solution)/shard_map/prep/pallas_call | solution.py:225
  2.6 0.7 collective-permute-start
  3.3 7.2 %collective-permute-start.1 = (bf16[544,256]{1,0:T(8,128)(2,1)}, bf16[544,256]{1,0:T(8,128)(2,1)S(1)}, u32[]{:S(2)}, u32[]{:S(2)}) collective-permute-start(bf16[544,256]{1,0:T(8,128)(2,1)} %get-tuple-element.22), channel_id=1, source_target_pairs={{0,16},{32,48},{64,80},{96,112},{128,144},{160,176},{192,208},{224... | collective-permute-start | bytes 835592 | tf_op jit(solution)/shard_map/ppermute | solution.py:28
  10.5 0.0 copy-start
  10.5 1.0 %copy-done = bf16[5,128,256]{2,1,0:T(8,128)(2,1)S(1)} copy-done((bf16[5,128,256]{2,1,0:T(8,128)(2,1)S(1)}, bf16[5,128,256]{2,1,0:T(8,128)(2,1)}, u32[]{:S(2)}) %copy-start) | copy-done | bytes 327704
  11.5 0.0 copy-start.1
  11.5 1.0 %copy-done.1 = bf16[1024,256]{1,0:T(8,128)(2,1)S(1)} copy-done((bf16[1024,256]{1,0:T(8,128)(2,1)S(1)}, bf16[1024,256]{1,0:T(8,128)(2,1)}, u32[]{:S(2)}) %copy-start.1) | copy-done | bytes 524312
  12.5 0.0 copy-start.2
  12.5 1.0 %copy-done.2 = bf16[5,128,256]{2,1,0:T(8,128)(2,1)S(1)} copy-done((bf16[5,128,256]{2,1,0:T(8,128)(2,1)S(1)}, bf16[5,128,256]{2,1,0:T(8,128)(2,1)}, u32[]{:S(2)}) %copy-start.2) | copy-done | bytes 327704
  13.5 0.0 copy-start.3
  13.5 0.9 copy-done.3
  14.4 0.3 own.1
  14.7 0.0 collective-permute-done.far_ref
  14.7 0.8 collective-permute-done.1.near_ref
  15.5 0.1 middle.1
  15.5 5.8 %collective-permute-start.2 = (bf16[13,64,256]{2,1,0:T(8,128)(2,1)S(1)}, bf16[13,64,256]{2,1,0:T(8,128)(2,1)S(1)}, u32[]{:S(2)}, u32[]{:S(2)}) collective-permute-start(bf16[13,64,256]{2,1,0:T(8,128)(2,1)S(1)} %get-tuple-element.33), channel_id=1, source_target_pairs={{0,15},{1,2},{2,1},{3,4},{4,3},{5,6},{6,5},{7,8},{8,7},{9,10},{10,... | collective-permute-start | bytes 1277960 | tf_op jit(solution)/shard_map/ppermute | solution.py:264
  21.4 3.2 %collective-permute-start.3 = (bf16[13,64,256]{2,1,0:T(8,128)(2,1)S(1)}, bf16[13,64,256]{2,1,0:T(8,128)(2,1)S(1)}, u32[]{:S(2)}, u32[]{:S(2)}) collective-permute-start(bf16[13,64,256]{2,1,0:T(8,128)(2,1)S(1)} %get-tuple-element.34), channel_id=1, source_target_pairs={{0,1},{1,0},{2,3},{3,2},{4,5},{5,4},{6,7},{7,6},{8,9},{9,8},{10,11... | collective-permute-start | bytes 1277960 | tf_op jit(solution)/shard_map/ppermute | solution.py:267
  24.6 3.6 %inner_band.1 = (f32[5,512,256]{2,1,0:T(8,128)S(1)}, bf16[5,512,1152]{2,1,0:T(8,128)(2,1)S(1)}) custom-call(bf16[544,256]{1,0:T(8,128)(2,1)S(1)} %collective-permute-done.far_ref, bf16[5,128,256]{2,1,0:T(8,128)(2,1)S(1)} %get-tuple-element.29.own_ref, bf16[544,256]{1,0:T(8,128)(2,1)S(1)} %collective-permute-done.1.near_ref, ...), custom_call_target="tpu_custom_call" | custom-call | flops 1509949440 | bytes 4194304 | tf_op jit(solution)/shard_map/inner_band/pallas_call | solution.py:271
  28.1 0.0 collective-permute-done.2.across
  28.1 0.0 collective-permute-done.3.beside
  28.2 3.6 %outer_band.1 = (f32[5,128,256]{2,1,0:T(8,128)}, bf16[1024,256]{1,0:T(8,128)(2,1)S(1)}) custom-call(bf16[5,512,1152]{2,1,0:T(8,128)(2,1)S(1)} %get-tuple-element.32.bands, bf16[13,64,256]{2,1,0:T(8,128)(2,1)S(1)} %collective-permute-done.2.across, bf16[13,64,256]{2,1,0:T(8,128)(2,1)S(1)} %collective-permute-done.3.beside, ...), custom_call_target="tpu_custom_call" | custom-call | flops 3019898880 | bytes 6291456 | tf_op jit(solution)/shard_map/outer_band/pallas_call | solution.py:291
  31.7 27.2 %all_to_all.15 = bf16[64,16,256]{2,1,0:T(8,128)(2,1)S(1)} all-to-all(bf16[64,16,256]{2,1,0:T(8,128)(2,1)S(1)} %bitcast.9), channel_id=1, replica_groups=mesh['yh'=2,'z3'=2,'z2'=2,'z1'=2,'zl'=2,'yl'=2,'x'=4,'core'=2] {'yh','zl..., dimensions={0} | all-to-all | bytes 1048576 | tf_op jit(solution)/shard_map/all_to_all | solution.py:214
  58.9 0.1 reduce_sum.24
  59.1 17.5 %all_to_all.16 = bf16[8,16,256]{2,1,0:T(8,128)(2,1)S(1)} all-to-all(bf16[8,16,256]{2,1,0:T(8,128)(2,1)S(1)} %broadcast_in_dim.4), channel_id=1, replica_groups=mesh['yh'=2,'z3'=2,'z2'=2,'z1'=2,'zl'=2,'yl'=2,'x'=4,'core'=2] {'z1','z2..., dimensions={0} | all-to-all | bytes 131072 | tf_op jit(solution)/shard_map/all_to_all | solution.py:214
  76.6 18.4 %all_to_all.17 = bf16[64,16,256]{2,1,0:T(8,128)(2,1)S(1)} all-to-all(bf16[64,16,256]{2,1,0:T(8,128)(2,1)S(1)} %broadcast_in_dim.5), channel_id=1, replica_groups=mesh['yh'=2,'z3'=2,'z2'=2,'z1'=2,'zl'=2,'yl'=2,'x'=4,'core'=2] {'yh','zl..., dimensions={0} | all-to-all | bytes 1048576 | tf_op jit(solution)/shard_map/all_to_all | solution.py:214
  95.0 1.1 %bitcast_convert_fusion = f32[1024,256]{1,0:T(8,128)} fusion(bf16[64,16,256]{2,1,0:T(8,128)(2,1)S(1)} %all_to_all.17), kind=kLoop, calls=%fused_computation | loop fusion | flops 262144 | bytes 1572864 | tf_op jit(solution)/shard_map/convert_element_type | solution.py:311
  (3 shorter events, 0.1 us)
Async XLA Ops:
  2.6 12.1 %collective-permute-start = (bf16[544,256]{1,0:T(8,128)(2,1)}, bf16[544,256]{1,0:T(8,128)(2,1)S(1)}, u32[]{:S(2)}, u32[]{:S(2)}) collective-permute-start(bf16[544,256]{1,0:T(8,128)(2,1)} %get-tuple-element.21), channel_id=1, source_target_pairs={{16,32},{48,64},{80,96},{112,128},{144,160},{176,192},{208,224},{2... | collective-permute-start | bytes 835592 | tf_op jit(solution)/shard_map/ppermute | solution.py:28
  3.3 12.2 %collective-permute-start.1 = (bf16[544,256]{1,0:T(8,128)(2,1)}, bf16[544,256]{1,0:T(8,128)(2,1)S(1)}, u32[]{:S(2)}, u32[]{:S(2)}) collective-permute-start(bf16[544,256]{1,0:T(8,128)(2,1)} %get-tuple-element.22), channel_id=1, source_target_pairs={{0,16},{32,48},{64,80},{96,112},{128,144},{160,176},{192,208},{224... | collective-permute-start | bytes 835592 | tf_op jit(solution)/shard_map/ppermute | solution.py:28
  10.5 1.0 %copy-start = (bf16[5,128,256]{2,1,0:T(8,128)(2,1)S(1)}, bf16[5,128,256]{2,1,0:T(8,128)(2,1)}, u32[]{:S(2)}) copy-start(bf16[5,128,256]{2,1,0:T(8,128)(2,1)} %cells_ref.1) | copy-start | bytes 983044
  11.5 1.0 %copy-start.1 = (bf16[1024,256]{1,0:T(8,128)(2,1)S(1)}, bf16[1024,256]{1,0:T(8,128)(2,1)}, u32[]{:S(2)}) copy-start(bf16[1024,256]{1,0:T(8,128)(2,1)} %weight_ref.1) | copy-start | bytes 1572868
  12.5 1.0 %copy-start.2 = (bf16[5,128,256]{2,1,0:T(8,128)(2,1)S(1)}, bf16[5,128,256]{2,1,0:T(8,128)(2,1)}, u32[]{:S(2)}) copy-start(bf16[5,128,256]{2,1,0:T(8,128)(2,1)} %param.5) | copy-start | bytes 983044
  13.5 0.9 copy-start.3
  15.5 12.6 %collective-permute-start.2 = (bf16[13,64,256]{2,1,0:T(8,128)(2,1)S(1)}, bf16[13,64,256]{2,1,0:T(8,128)(2,1)S(1)}, u32[]{:S(2)}, u32[]{:S(2)}) collective-permute-start(bf16[13,64,256]{2,1,0:T(8,128)(2,1)S(1)} %get-tuple-element.33), channel_id=1, source_target_pairs={{0,15},{1,2},{2,1},{3,4},{4,3},{5,6},{6,5},{7,8},{8,7},{9,10},{10,... | collective-permute-start | bytes 1277960 | tf_op jit(solution)/shard_map/ppermute | solution.py:264
  21.4 6.7 %collective-permute-start.3 = (bf16[13,64,256]{2,1,0:T(8,128)(2,1)S(1)}, bf16[13,64,256]{2,1,0:T(8,128)(2,1)S(1)}, u32[]{:S(2)}, u32[]{:S(2)}) collective-permute-start(bf16[13,64,256]{2,1,0:T(8,128)(2,1)S(1)} %get-tuple-element.34), channel_id=1, source_target_pairs={{0,1},{1,0},{2,3},{3,2},{4,5},{5,4},{6,7},{7,6},{8,9},{9,8},{10,11... | collective-permute-start | bytes 1277960 | tf_op jit(solution)/shard_map/ppermute | solution.py:267

commit v10 on v9

--- a/solution.py
+++ b/solution.py
@@ -88,7 +88,9 @@
 def own_kernel(cells_ref, lines_ref, field_ref, weight_ref, own_ref, lines_own, field_t, mixing):
     own_ref[...] = cells_ref[...]
     lines_own[...] = lines_ref[...]
-    field_t[...] = field_ref[...].T
+    turned = field_ref[...].T
+    field_t[:, : ROWS * COLS] = turned
+    field_t[:, ROWS * COLS :] = turned
     for k in range(NK):
         mixing[k * CH : (k + 1) * CH, :] = weight_ref[k * CH : (k + 1) * CH, :].T
 
@@ -187,7 +189,7 @@
 
 
 def outer_kernel(
-    scale, bands, across, beside, part_ref, field_t, mixing, grad_ref, gw_ref, cells, spreads
+    scale, bands, across, beside, part_ref, field_t, mixing, grad_hbm, gw_ref, cells, spreads, grad, sem
 ):
     first = pl.multiple_of(lax.axis_index("core") * HALF, HALF)
     other = pl.multiple_of(HALF - first, HALF)
@@ -201,13 +203,30 @@
             spread = part_ref[l, rows, :] + jnp.dot(
                 bands[l, rows, :], window, preferred_element_type=jnp.float32
             )
-            spreads[l * COLS : (l + 1) * COLS, k * CH : (k + 1) * CH] = spread.astype(jnp.bfloat16)
+            high = spread.astype(jnp.bfloat16)
+            low = (spread - high.astype(jnp.float32)).astype(jnp.bfloat16)
+            at = slice(k * CH, (k + 1) * CH)
+            spreads[l * COLS : (l + 1) * COLS, at] = high
+            spreads[(ROWS + l) * COLS : (ROWS + l + 1) * COLS, at] = low
+    grad[...] = jnp.dot(spreads[: ROWS * COLS, :], mixing[...], preferred_element_type=jnp.float32)
+    store = pltpu.make_async_copy(grad, grad_hbm, sem)
+    store.start()
     total = jnp.dot(field_t[...], spreads[...], preferred_element_type=jnp.float32) * scale
     for k in range(NK):
         gw_ref[k * CH : (k + 1) * CH, :] = total[:, k * CH : (k + 1) * CH].astype(jnp.bfloat16)
-    grad = jnp.dot(spreads[...], mixing[...], preferred_element_type=jnp.float32)
-    for l in range(ROWS):
-        grad_ref[l] = grad[l * COLS : (l + 1) * COLS, :]
+    store.wait()
+
+
+def widen_kernel(sum_ref, out_hbm, wide, sems):
+    copies = []
+    for k in range(NK):
+        rows = slice(k * CH, (k + 1) * CH)
+        wide[rows, :] = sum_ref[rows, :].astype(jnp.float32)
+        at = pl.ds(k * CH, CH)
+        copies.append(pltpu.make_async_copy(wide.at[at], out_hbm.at[at], sems.at[k]))
+        copies[-1].start()
+    for copy in copies:
+        copy.wait()
 
 
 def exchange(x, axes):
@@ -245,7 +264,7 @@
         out_shape=(
             jax.ShapeDtypeStruct(cotangent.shape, jnp.bfloat16),
             jax.ShapeDtypeStruct(lines_own.shape, jnp.float32),
-            jax.ShapeDtypeStruct((CH, ROWS * COLS), jnp.bfloat16),
+            jax.ShapeDtypeStruct((CH, 2 * ROWS * COLS), jnp.bfloat16),
             jax.ShapeDtypeStruct((NK * CH, CH), jnp.bfloat16),
         ),
         compiler_params=params,
@@ -291,10 +310,16 @@
     grad_field, gw = pl.pallas_call(
         functools.partial(outer_kernel, scale),
         out_shape=(
-            jax.ShapeDtypeStruct((ROWS, COLS, CH), jnp.float32),
+            jax.ShapeDtypeStruct((ROWS * COLS, CH), jnp.float32),
             jax.ShapeDtypeStruct((NK * CH, CH), jnp.bfloat16),
         ),
-        scratch_shapes=[cells, pltpu.VMEM((ROWS * COLS, NK * CH), jnp.bfloat16)],
+        out_specs=(hbm, pl.BlockSpec(memory_space=pltpu.VMEM)),
+        scratch_shapes=[
+            cells,
+            pltpu.VMEM((2 * ROWS * COLS, NK * CH), jnp.bfloat16),
+            pltpu.VMEM((ROWS * COLS, CH), jnp.float32),
+            pltpu.SemaphoreType.DMA,
+        ],
         compiler_params=params,
         cost_estimate=pl.CostEstimate(
             flops=band_flops * 2, bytes_accessed=6 * 1024 * 1024, transcendentals=0
@@ -308,7 +333,18 @@
     for axes, count in ((DEPTH, math.prod(sizes[a] for a in DEPTH)), (NEAR, near)):
         mine = jnp.sum(got.astype(jnp.float32), axis=0).astype(jnp.bfloat16)
         got = exchange(jnp.broadcast_to(mine[None], (count, piece, CH)), axes)
-    return (grad_field, got.reshape(NK * CH, CH).astype(jnp.float32))
+    grad_weight = pl.pallas_call(
+        widen_kernel,
+        out_shape=jax.ShapeDtypeStruct((NK * CH, CH), jnp.float32),
+        out_specs=hbm,
+        scratch_shapes=[
+            pltpu.VMEM((NK * CH, CH), jnp.float32),
+            pltpu.SemaphoreType.DMA((NK,)),
+        ],
+        compiler_params=params,
+        name="widen",
+    )(got.reshape(NK * CH, CH))
+    return (grad_field.reshape(ROWS, COLS, CH), grad_weight)
 
 
 def solution(mesh):

time: 96.6 us -> 96.5 us (level)
  other arithmetic: 1.2 us -> 0.12 us
  Pallas kernels: 9.4 us -> 10.4 us
    convert_element_type x1 -> x0, other arithmetic: 1.08 us -> none  [per_device(): return (grad_field, got.reshape(NK * CH, CH).astype(jnp.float32))]
    pallas_call x0 -> x1, Pallas kernels: none -> 1.01 us  [per_device(): pl.pallas_call(widen_kernel, out_shape=jax.ShapeDtypeStruct((NK * CH, CH)...]
where the time goes in v10:
time: 96.5 us; the launch traced here: 96 us
  blocking collectives  63.1 us (65%)
  starting transfers between devices  16.9 us (18%)
  Pallas kernels  10.4 us (11%)
  local copies, waits for them, and re-layouts  3.92 us (4%)
    all_to_all x3, blocking collectives, exchange(): return lax.all_to_all(x, axes, 0, 0, tiled=True)  63.1 us
    ppermute x2, starting transfers between devices, swapped(): return lax.ppermute(x, axes, pairs + [(j, i) for i, j in pairs])  7.92 us
    ppermute x1, starting transfers between devices, per_device(): lax.ppermute(across, LON_AXES, [(i, (i - 1 + 2 * (i % 2)) % lon_count) fo...  5.85 us
    unnamed x8, local copies, waits for them, and re-layouts  3.87 us
    pallas_call x1, Pallas kernels, per_device(): pl.pallas_call(inner_kernel, out_shape=(jax.ShapeDtypeStruct((ROWS, NK *...  3.57 us
    pallas_call x1, Pallas kernels, per_device(): pl.pallas_call(functools.partial(outer_kernel, scale), out_shape=(jax.Sha...  3.53 us
    ppermute x1, starting transfers between devices, per_device(): beside = lax.ppermute(beside, 'core', [(0, 1), (1, 0)])  3.15 us
    pallas_call x1, Pallas kernels, per_device(): pl.pallas_call(prep_kernel, out_shape=(packed, packed, jax.ShapeDtypeStru...  1.94 us
  transfers between devices with their start and end apart: 4, of which 1 were waited for; matrix products, arithmetic and copies ran while one was open for 0% of the time, Pallas kernels for 4%

profile of v10, /device:TPU:1, one launch (start us, length us, event | category | flops | bytes accessed | tf_op | source)
XLA Modules:
  0.0 96.0 jit_solution(13212556537739324128)
XLA Ops:
  0.6 1.9 %prep.1 = (bf16[544,256]{1,0:T(8,128)(2,1)}, bf16[544,256]{1,0:T(8,128)(2,1)}, f32[192,128]{1,0:T(8,128)}) custom-call(s32[5,2,9]{2,1,0:T(2,128)} %bitcast.12, f32[5,9,4,128]{3,2,1,0:T(4,128)} %bitcast.11, bf16[640,256]{1,0:T(8,128)(2,1)} %bitcast.8), custom_call_target="tpu_custom_call" | custom-call | tf_op jit(solution)/shard_map/prep/pallas_call | solution.py:244
  2.6 0.7 collective-permute-start
  3.3 7.2 %collective-permute-start.1 = (bf16[544,256]{1,0:T(8,128)(2,1)}, bf16[544,256]{1,0:T(8,128)(2,1)S(1)}, u32[]{:S(2)}, u32[]{:S(2)}) collective-permute-start(bf16[544,256]{1,0:T(8,128)(2,1)} %get-tuple-element.22), channel_id=1, source_target_pairs={{0,16},{32,48},{64,80},{96,112},{128,144},{160,176},{192,208},{224... | collective-permute-start | bytes 835592 | tf_op jit(solution)/shard_map/ppermute | solution.py:28
  10.5 0.0 copy-start
  10.5 1.0 %copy-done = bf16[5,128,256]{2,1,0:T(8,128)(2,1)S(1)} copy-done((bf16[5,128,256]{2,1,0:T(8,128)(2,1)S(1)}, bf16[5,128,256]{2,1,0:T(8,128)(2,1)}, u32[]{:S(2)}) %copy-start) | copy-done | bytes 327704
  11.5 0.0 copy-start.1
  11.5 1.0 %copy-done.1 = bf16[1024,256]{1,0:T(8,128)(2,1)S(1)} copy-done((bf16[1024,256]{1,0:T(8,128)(2,1)S(1)}, bf16[1024,256]{1,0:T(8,128)(2,1)}, u32[]{:S(2)}) %copy-start.1) | copy-done | bytes 524312
  12.5 0.0 copy-start.2
  12.5 1.0 %copy-done.2 = bf16[5,128,256]{2,1,0:T(8,128)(2,1)S(1)} copy-done((bf16[5,128,256]{2,1,0:T(8,128)(2,1)S(1)}, bf16[5,128,256]{2,1,0:T(8,128)(2,1)}, u32[]{:S(2)}) %copy-start.2) | copy-done | bytes 327704
  13.5 0.0 copy-start.3
  13.5 0.9 copy-done.3
  14.4 0.3 own.1
  14.7 0.0 collective-permute-done.far_ref
  14.7 0.8 collective-permute-done.1.near_ref
  15.5 0.1 middle.1
  15.5 5.8 %collective-permute-start.2 = (bf16[13,64,256]{2,1,0:T(8,128)(2,1)S(1)}, bf16[13,64,256]{2,1,0:T(8,128)(2,1)S(1)}, u32[]{:S(2)}, u32[]{:S(2)}) collective-permute-start(bf16[13,64,256]{2,1,0:T(8,128)(2,1)S(1)} %get-tuple-element.33), channel_id=1, source_target_pairs={{0,15},{1,2},{2,1},{3,4},{4,3},{5,6},{6,5},{7,8},{8,7},{9,10},{10,... | collective-permute-start | bytes 1277960 | tf_op jit(solution)/shard_map/ppermute | solution.py:283
  21.4 3.2 %collective-permute-start.3 = (bf16[13,64,256]{2,1,0:T(8,128)(2,1)S(1)}, bf16[13,64,256]{2,1,0:T(8,128)(2,1)S(1)}, u32[]{:S(2)}, u32[]{:S(2)}) collective-permute-start(bf16[13,64,256]{2,1,0:T(8,128)(2,1)S(1)} %get-tuple-element.34), channel_id=1, source_target_pairs={{0,1},{1,0},{2,3},{3,2},{4,5},{5,4},{6,7},{7,6},{8,9},{9,8},{10,11... | collective-permute-start | bytes 1277960 | tf_op jit(solution)/shard_map/ppermute | solution.py:286
  24.6 3.6 %inner_band.1 = (f32[5,512,256]{2,1,0:T(8,128)S(1)}, bf16[5,512,1152]{2,1,0:T(8,128)(2,1)S(1)}) custom-call(bf16[544,256]{1,0:T(8,128)(2,1)S(1)} %collective-permute-done.far_ref, bf16[5,128,256]{2,1,0:T(8,128)(2,1)S(1)} %get-tuple-element.29.own_ref, bf16[544,256]{1,0:T(8,128)(2,1)S(1)} %collective-permute-done.1.near_ref, ...), custom_call_target="tpu_custom_call" | custom-call | flops 1509949440 | bytes 4194304 | tf_op jit(solution)/shard_map/inner_band/pallas_call | solution.py:290
  28.1 0.0 collective-permute-done.2.across
  28.1 0.0 collective-permute-done.3.beside
  28.2 3.5 %outer_band.1 = (f32[640,256]{1,0:T(8,128)}, bf16[1024,256]{1,0:T(8,128)(2,1)S(1)}) custom-call(bf16[5,512,1152]{2,1,0:T(8,128)(2,1)S(1)} %get-tuple-element.32.bands, bf16[13,64,256]{2,1,0:T(8,128)(2,1)S(1)} %collective-permute-done.2.across, bf16[13,64,256]{2,1,0:T(8,128)(2,1)S(1)} %collective-permute-done.3.beside, ...), custom_call_target="tpu_custom_call" | custom-call | flops 3019898880 | bytes 6291456 | tf_op jit(solution)/shard_map/outer_band/pallas_call | solution.py:310
  31.7 27.2 %all_to_all.15 = bf16[64,16,256]{2,1,0:T(8,128)(2,1)S(1)} all-to-all(bf16[64,16,256]{2,1,0:T(8,128)(2,1)S(1)} %bitcast.9), channel_id=1, replica_groups=mesh['yh'=2,'z3'=2,'z2'=2,'z1'=2,'zl'=2,'yl'=2,'x'=4,'core'=2] {'yh','zl..., dimensions={0} | all-to-all | bytes 1048576 | tf_op jit(solution)/shard_map/all_to_all | solution.py:233
  58.9 0.1 reduce_sum.24
  59.0 17.5 %all_to_all.16 = bf16[8,16,256]{2,1,0:T(8,128)(2,1)S(1)} all-to-all(bf16[8,16,256]{2,1,0:T(8,128)(2,1)S(1)} %broadcast_in_dim.4), channel_id=1, replica_groups=mesh['yh'=2,'z3'=2,'z2'=2,'z1'=2,'zl'=2,'yl'=2,'x'=4,'core'=2] {'z1','z2..., dimensions={0} | all-to-all | bytes 131072 | tf_op jit(solution)/shard_map/all_to_all | solution.py:233
  76.6 18.4 %all_to_all.17 = bf16[64,16,256]{2,1,0:T(8,128)(2,1)S(1)} all-to-all(bf16[64,16,256]{2,1,0:T(8,128)(2,1)S(1)} %broadcast_in_dim.5), channel_id=1, replica_groups=mesh['yh'=2,'z3'=2,'z2'=2,'z1'=2,'zl'=2,'yl'=2,'x'=4,'core'=2] {'yh','zl..., dimensions={0} | all-to-all | bytes 1048576 | tf_op jit(solution)/shard_map/all_to_all | solution.py:233
  95.0 1.0 %widen.1 = f32[1024,256]{1,0:T(8,128)} custom-call(bf16[1024,256]{1,0:T(8,128)(2,1)S(1)} %bitcast.7), custom_call_target="tpu_custom_call" | custom-call | tf_op jit(solution)/shard_map/widen/pallas_call | solution.py:336
  (3 shorter events, 0.1 us)
Async XLA Ops:
  2.6 12.1 %collective-permute-start = (bf16[544,256]{1,0:T(8,128)(2,1)}, bf16[544,256]{1,0:T(8,128)(2,1)S(1)}, u32[]{:S(2)}, u32[]{:S(2)}) collective-permute-start(bf16[544,256]{1,0:T(8,128)(2,1)} %get-tuple-element.21), channel_id=1, source_target_pairs={{16,32},{48,64},{80,96},{112,128},{144,160},{176,192},{208,224},{2... | collective-permute-start | bytes 835592 | tf_op jit(solution)/shard_map/ppermute | solution.py:28
  3.3 12.2 %collective-permute-start.1 = (bf16[544,256]{1,0:T(8,128)(2,1)}, bf16[544,256]{1,0:T(8,128)(2,1)S(1)}, u32[]{:S(2)}, u32[]{:S(2)}) collective-permute-start(bf16[544,256]{1,0:T(8,128)(2,1)} %get-tuple-element.22), channel_id=1, source_target_pairs={{0,16},{32,48},{64,80},{96,112},{128,144},{160,176},{192,208},{224... | collective-permute-start | bytes 835592 | tf_op jit(solution)/shard_map/ppermute | solution.py:28
  10.5 1.0 %copy-start = (bf16[5,128,256]{2,1,0:T(8,128)(2,1)S(1)}, bf16[5,128,256]{2,1,0:T(8,128)(2,1)}, u32[]{:S(2)}) copy-start(bf16[5,128,256]{2,1,0:T(8,128)(2,1)} %cells_ref.1) | copy-start | bytes 983044
  11.5 1.0 %copy-start.1 = (bf16[1024,256]{1,0:T(8,128)(2,1)S(1)}, bf16[1024,256]{1,0:T(8,128)(2,1)}, u32[]{:S(2)}) copy-start(bf16[1024,256]{1,0:T(8,128)(2,1)} %weight_ref.1) | copy-start | bytes 1572868
  12.5 1.0 %copy-start.2 = (bf16[5,128,256]{2,1,0:T(8,128)(2,1)S(1)}, bf16[5,128,256]{2,1,0:T(8,128)(2,1)}, u32[]{:S(2)}) copy-start(bf16[5,128,256]{2,1,0:T(8,128)(2,1)} %param.5) | copy-start | bytes 983044
  13.5 0.9 copy-start.3
  15.5 12.6 %collective-permute-start.2 = (bf16[13,64,256]{2,1,0:T(8,128)(2,1)S(1)}, bf16[13,64,256]{2,1,0:T(8,128)(2,1)S(1)}, u32[]{:S(2)}, u32[]{:S(2)}) collective-permute-start(bf16[13,64,256]{2,1,0:T(8,128)(2,1)S(1)} %get-tuple-element.33), channel_id=1, source_target_pairs={{0,15},{1,2},{2,1},{3,4},{4,3},{5,6},{6,5},{7,8},{8,7},{9,10},{10,... | collective-permute-start | bytes 1277960 | tf_op jit(solution)/shard_map/ppermute | solution.py:283
  21.4 6.7 %collective-permute-start.3 = (bf16[13,64,256]{2,1,0:T(8,128)(2,1)S(1)}, bf16[13,64,256]{2,1,0:T(8,128)(2,1)S(1)}, u32[]{:S(2)}, u32[]{:S(2)}) collective-permute-start(bf16[13,64,256]{2,1,0:T(8,128)(2,1)S(1)} %get-tuple-element.34), channel_id=1, source_target_pairs={{0,1},{1,0},{2,3},{3,2},{4,5},{5,4},{6,7},{7,6},{8,9},{9,8},{10,11... | collective-permute-start | bytes 1277960 | tf_op jit(solution)/shard_map/ppermute | solution.py:286

commit v11 on v10

--- a/solution.py
+++ b/solution.py
@@ -181,11 +181,12 @@
     for l in range(ROWS):
         band = bands.at[l % 2]
         fill_bands(band, outer_ref.at[l], lines, inner_mask, outer_mask, l)
-        part_ref[l] = jnp.dot(
-            band[...],
-            cells[l * COLS : (l + NR) * COLS, :],
-            preferred_element_type=jnp.float32,
-        )
+        window = cells[l * COLS : (l + NR) * COLS, :]
+        for k in range(NK):
+            rows = slice(k * COLS, (k + 1) * COLS)
+            part_ref[l, rows, :] = jnp.dot(
+                band[rows, :], window, preferred_element_type=jnp.float32
+            )
 
 
 def outer_kernel(

time: 96.5 us -> 96.5 us (level)
  no operation moved by 1% of the time
where the time goes in v11:
time: 96.5 us; the launch traced here: 96 us
  blocking collectives  63 us (65%)
  starting transfers between devices  16.9 us (18%)
  Pallas kernels  10.5 us (11%)
  local copies, waits for them, and re-layouts  3.92 us (4%)
    all_to_all x3, blocking collectives, exchange(): return lax.all_to_all(x, axes, 0, 0, tiled=True)  63 us
    ppermute x2, starting transfers between devices, swapped(): return lax.ppermute(x, axes, pairs + [(j, i) for i, j in pairs])  7.92 us
    ppermute x1, starting transfers between devices, per_device(): lax.ppermute(across, LON_AXES, [(i, (i - 1 + 2 * (i % 2)) % lon_count) fo...  5.85 us
    unnamed x8, local copies, waits for them, and re-layouts  3.87 us
    pallas_call x1, Pallas kernels, per_device(): pl.pallas_call(inner_kernel, out_shape=(jax.ShapeDtypeStruct((ROWS, NK *...  3.7 us
    pallas_call x1, Pallas kernels, per_device(): pl.pallas_call(functools.partial(outer_kernel, scale), out_shape=(jax.Sha...  3.53 us
    ppermute x1, starting transfers between devices, per_device(): beside = lax.ppermute(beside, 'core', [(0, 1), (1, 0)])  3.15 us
    pallas_call x1, Pallas kernels, per_device(): pl.pallas_call(prep_kernel, out_shape=(packed, packed, jax.ShapeDtypeStru...  1.94 us
  transfers between devices with their start and end apart: 4, of which 1 were waited for; matrix products, arithmetic and copies ran while one was open for 0% of the time, Pallas kernels for 4%

profile of v11, /device:TPU:1, one launch (start us, length us, event | category | flops | bytes accessed | tf_op | source)
XLA Modules:
  0.0 96.0 jit_solution(632625857439945024)
XLA Ops:
  0.6 1.9 %prep.1 = (bf16[544,256]{1,0:T(8,128)(2,1)}, bf16[544,256]{1,0:T(8,128)(2,1)}, f32[192,128]{1,0:T(8,128)}) custom-call(s32[5,2,9]{2,1,0:T(2,128)} %bitcast.12, f32[5,9,4,128]{3,2,1,0:T(4,128)} %bitcast.11, bf16[640,256]{1,0:T(8,128)(2,1)} %bitcast.8), custom_call_target="tpu_custom_call" | custom-call | tf_op jit(solution)/shard_map/prep/pallas_call | solution.py:245
  2.6 0.7 collective-permute-start
  3.3 7.2 %collective-permute-start.1 = (bf16[544,256]{1,0:T(8,128)(2,1)}, bf16[544,256]{1,0:T(8,128)(2,1)S(1)}, u32[]{:S(2)}, u32[]{:S(2)}) collective-permute-start(bf16[544,256]{1,0:T(8,128)(2,1)} %get-tuple-element.22), channel_id=1, source_target_pairs={{0,16},{32,48},{64,80},{96,112},{128,144},{160,176},{192,208},{224... | collective-permute-start | bytes 835592 | tf_op jit(solution)/shard_map/ppermute | solution.py:28
  10.5 0.0 copy-start
  10.5 1.0 %copy-done = bf16[5,128,256]{2,1,0:T(8,128)(2,1)S(1)} copy-done((bf16[5,128,256]{2,1,0:T(8,128)(2,1)S(1)}, bf16[5,128,256]{2,1,0:T(8,128)(2,1)}, u32[]{:S(2)}) %copy-start) | copy-done | bytes 327704
  11.5 0.0 copy-start.1
  11.5 1.0 %copy-done.1 = bf16[1024,256]{1,0:T(8,128)(2,1)S(1)} copy-done((bf16[1024,256]{1,0:T(8,128)(2,1)S(1)}, bf16[1024,256]{1,0:T(8,128)(2,1)}, u32[]{:S(2)}) %copy-start.1) | copy-done | bytes 524312
  12.5 0.0 copy-start.2
  12.5 1.0 %copy-done.2 = bf16[5,128,256]{2,1,0:T(8,128)(2,1)S(1)} copy-done((bf16[5,128,256]{2,1,0:T(8,128)(2,1)S(1)}, bf16[5,128,256]{2,1,0:T(8,128)(2,1)}, u32[]{:S(2)}) %copy-start.2) | copy-done | bytes 327704
  13.5 0.0 copy-start.3
  13.5 0.9 copy-done.3
  14.4 0.3 own.1
  14.7 0.0 collective-permute-done.far_ref
  14.7 0.8 collective-permute-done.1.near_ref
  15.5 0.1 middle.1
  15.5 5.8 %collective-permute-start.2 = (bf16[13,64,256]{2,1,0:T(8,128)(2,1)S(1)}, bf16[13,64,256]{2,1,0:T(8,128)(2,1)S(1)}, u32[]{:S(2)}, u32[]{:S(2)}) collective-permute-start(bf16[13,64,256]{2,1,0:T(8,128)(2,1)S(1)} %get-tuple-element.33), channel_id=1, source_target_pairs={{0,15},{1,2},{2,1},{3,4},{4,3},{5,6},{6,5},{7,8},{8,7},{9,10},{10,... | collective-permute-start | bytes 1277960 | tf_op jit(solution)/shard_map/ppermute | solution.py:284
  21.4 3.2 %collective-permute-start.3 = (bf16[13,64,256]{2,1,0:T(8,128)(2,1)S(1)}, bf16[13,64,256]{2,1,0:T(8,128)(2,1)S(1)}, u32[]{:S(2)}, u32[]{:S(2)}) collective-permute-start(bf16[13,64,256]{2,1,0:T(8,128)(2,1)S(1)} %get-tuple-element.34), channel_id=1, source_target_pairs={{0,1},{1,0},{2,3},{3,2},{4,5},{5,4},{6,7},{7,6},{8,9},{9,8},{10,11... | collective-permute-start | bytes 1277960 | tf_op jit(solution)/shard_map/ppermute | solution.py:287
  24.6 3.7 %inner_band.1 = (f32[5,512,256]{2,1,0:T(8,128)S(1)}, bf16[5,512,1152]{2,1,0:T(8,128)(2,1)S(1)}) custom-call(bf16[544,256]{1,0:T(8,128)(2,1)S(1)} %collective-permute-done.far_ref, bf16[5,128,256]{2,1,0:T(8,128)(2,1)S(1)} %get-tuple-element.29.own_ref, bf16[544,256]{1,0:T(8,128)(2,1)S(1)} %collective-permute-done.1.near_ref, ...), custom_call_target="tpu_custom_call" | custom-call | flops 1509949440 | bytes 4194304 | tf_op jit(solution)/shard_map/inner_band/pallas_call | solution.py:291
  28.3 0.0 collective-permute-done.2.across
  28.3 0.0 collective-permute-done.3.beside
  28.3 3.5 %outer_band.1 = (f32[640,256]{1,0:T(8,128)}, bf16[1024,256]{1,0:T(8,128)(2,1)S(1)}) custom-call(bf16[5,512,1152]{2,1,0:T(8,128)(2,1)S(1)} %get-tuple-element.32.bands, bf16[13,64,256]{2,1,0:T(8,128)(2,1)S(1)} %collective-permute-done.2.across, bf16[13,64,256]{2,1,0:T(8,128)(2,1)S(1)} %collective-permute-done.3.beside, ...), custom_call_target="tpu_custom_call" | custom-call | flops 3019898880 | bytes 6291456 | tf_op jit(solution)/shard_map/outer_band/pallas_call | solution.py:311
  31.8 27.1 %all_to_all.15 = bf16[64,16,256]{2,1,0:T(8,128)(2,1)S(1)} all-to-all(bf16[64,16,256]{2,1,0:T(8,128)(2,1)S(1)} %bitcast.9), channel_id=1, replica_groups=mesh['yh'=2,'z3'=2,'z2'=2,'z1'=2,'zl'=2,'yl'=2,'x'=4,'core'=2] {'yh','zl..., dimensions={0} | all-to-all | bytes 1048576 | tf_op jit(solution)/shard_map/all_to_all | solution.py:234
  58.9 0.1 reduce_sum.24
  59.0 17.5 %all_to_all.16 = bf16[8,16,256]{2,1,0:T(8,128)(2,1)S(1)} all-to-all(bf16[8,16,256]{2,1,0:T(8,128)(2,1)S(1)} %broadcast_in_dim.4), channel_id=1, replica_groups=mesh['yh'=2,'z3'=2,'z2'=2,'z1'=2,'zl'=2,'yl'=2,'x'=4,'core'=2] {'z1','z2..., dimensions={0} | all-to-all | bytes 131072 | tf_op jit(solution)/shard_map/all_to_all | solution.py:234
  76.6 18.4 %all_to_all.17 = bf16[64,16,256]{2,1,0:T(8,128)(2,1)S(1)} all-to-all(bf16[64,16,256]{2,1,0:T(8,128)(2,1)S(1)} %broadcast_in_dim.5), channel_id=1, replica_groups=mesh['yh'=2,'z3'=2,'z2'=2,'z1'=2,'zl'=2,'yl'=2,'x'=4,'core'=2] {'yh','zl..., dimensions={0} | all-to-all | bytes 1048576 | tf_op jit(solution)/shard_map/all_to_all | solution.py:234
  95.0 1.0 %widen.1 = f32[1024,256]{1,0:T(8,128)} custom-call(bf16[1024,256]{1,0:T(8,128)(2,1)S(1)} %bitcast.7), custom_call_target="tpu_custom_call" | custom-call | tf_op jit(solution)/shard_map/widen/pallas_call | solution.py:337
  (3 shorter events, 0.1 us)
Async XLA Ops:
  2.6 12.1 %collective-permute-start = (bf16[544,256]{1,0:T(8,128)(2,1)}, bf16[544,256]{1,0:T(8,128)(2,1)S(1)}, u32[]{:S(2)}, u32[]{:S(2)}) collective-permute-start(bf16[544,256]{1,0:T(8,128)(2,1)} %get-tuple-element.21), channel_id=1, source_target_pairs={{16,32},{48,64},{80,96},{112,128},{144,160},{176,192},{208,224},{2... | collective-permute-start | bytes 835592 | tf_op jit(solution)/shard_map/ppermute | solution.py:28
  3.3 12.2 %collective-permute-start.1 = (bf16[544,256]{1,0:T(8,128)(2,1)}, bf16[544,256]{1,0:T(8,128)(2,1)S(1)}, u32[]{:S(2)}, u32[]{:S(2)}) collective-permute-start(bf16[544,256]{1,0:T(8,128)(2,1)} %get-tuple-element.22), channel_id=1, source_target_pairs={{0,16},{32,48},{64,80},{96,112},{128,144},{160,176},{192,208},{224... | collective-permute-start | bytes 835592 | tf_op jit(solution)/shard_map/ppermute | solution.py:28
  10.5 1.0 %copy-start = (bf16[5,128,256]{2,1,0:T(8,128)(2,1)S(1)}, bf16[5,128,256]{2,1,0:T(8,128)(2,1)}, u32[]{:S(2)}) copy-start(bf16[5,128,256]{2,1,0:T(8,128)(2,1)} %cells_ref.1) | copy-start | bytes 983044
  11.5 1.0 %copy-start.1 = (bf16[1024,256]{1,0:T(8,128)(2,1)S(1)}, bf16[1024,256]{1,0:T(8,128)(2,1)}, u32[]{:S(2)}) copy-start(bf16[1024,256]{1,0:T(8,128)(2,1)} %weight_ref.1) | copy-start | bytes 1572868
  12.5 1.0 %copy-start.2 = (bf16[5,128,256]{2,1,0:T(8,128)(2,1)S(1)}, bf16[5,128,256]{2,1,0:T(8,128)(2,1)}, u32[]{:S(2)}) copy-start(bf16[5,128,256]{2,1,0:T(8,128)(2,1)} %param.5) | copy-start | bytes 983044
  13.5 0.9 copy-start.3
  15.5 12.7 %collective-permute-start.2 = (bf16[13,64,256]{2,1,0:T(8,128)(2,1)S(1)}, bf16[13,64,256]{2,1,0:T(8,128)(2,1)S(1)}, u32[]{:S(2)}, u32[]{:S(2)}) collective-permute-start(bf16[13,64,256]{2,1,0:T(8,128)(2,1)S(1)} %get-tuple-element.33), channel_id=1, source_target_pairs={{0,15},{1,2},{2,1},{3,4},{4,3},{5,6},{6,5},{7,8},{8,7},{9,10},{10,... | collective-permute-start | bytes 1277960 | tf_op jit(solution)/shard_map/ppermute | solution.py:284
  21.4 6.9 %collective-permute-start.3 = (bf16[13,64,256]{2,1,0:T(8,128)(2,1)S(1)}, bf16[13,64,256]{2,1,0:T(8,128)(2,1)S(1)}, u32[]{:S(2)}, u32[]{:S(2)}) collective-permute-start(bf16[13,64,256]{2,1,0:T(8,128)(2,1)S(1)} %get-tuple-element.34), channel_id=1, source_target_pairs={{0,1},{1,0},{2,3},{3,2},{4,5},{5,4},{6,7},{7,6},{8,9},{9,8},{10,11... | collective-permute-start | bytes 1277960 | tf_op jit(solution)/shard_map/ppermute | solution.py:287

commit v12 on v10

--- a/solution.py
+++ b/solution.py
@@ -179,7 +179,7 @@
     mask = own_mask().astype(jnp.float32)
     inner_mask, outer_mask = mask.astype(jnp.bfloat16), (1.0 - mask).astype(jnp.bfloat16)
     for l in range(ROWS):
-        band = bands.at[l % 2]
+        band = bands.at[l]
         fill_bands(band, outer_ref.at[l], lines, inner_mask, outer_mask, l)
         part_ref[l] = jnp.dot(
             band[...],
@@ -297,7 +297,7 @@
             pltpu.VMEM((EXT * LINES, COLS), jnp.float32),
             wide,
             cells,
-            pltpu.VMEM((2, NK * COLS, NR * COLS), jnp.bfloat16),
+            pltpu.VMEM((ROWS, NK * COLS, NR * COLS), jnp.bfloat16),
         ],
         compiler_params=params,
         cost_estimate=pl.CostEstimate(

time: 96.5 us -> 96.5 us (level)
  no operation moved by 1% of the time
where the time goes in v12:
time: 96.5 us; the launch traced here: 96 us
  blocking collectives  63.2 us (65%)
  starting transfers between devices  16.9 us (18%)
  Pallas kernels  10.3 us (11%)
  local copies, waits for them, and re-layouts  3.92 us (4%)
    all_to_all x3, blocking collectives, exchange(): return lax.all_to_all(x, axes, 0, 0, tiled=True)  63.2 us
    ppermute x2, starting transfers between devices, swapped(): return lax.ppermute(x, axes, pairs + [(j, i) for i, j in pairs])  7.92 us
    ppermute x1, starting transfers between devices, per_device(): lax.ppermute(across, LON_AXES, [(i, (i - 1 + 2 * (i % 2)) % lon_count) fo...  5.85 us
    unnamed x8, local copies, waits for them, and re-layouts  3.87 us
    pallas_call x1, Pallas kernels, per_device(): pl.pallas_call(inner_kernel, out_shape=(jax.ShapeDtypeStruct((ROWS, NK *...  3.55 us
    pallas_call x1, Pallas kernels, per_device(): pl.pallas_call(functools.partial(outer_kernel, scale), out_shape=(jax.Sha...  3.52 us
    ppermute x1, starting transfers between devices, per_device(): beside = lax.ppermute(beside, 'core', [(0, 1), (1, 0)])  3.15 us
    pallas_call x1, Pallas kernels, per_device(): pl.pallas_call(prep_kernel, out_shape=(packed, packed, jax.ShapeDtypeStru...  1.94 us
  transfers between devices with their start and end apart: 4, of which 1 were waited for; matrix products, arithmetic and copies ran while one was open for 0% of the time, Pallas kernels for 4%

profile of v12, /device:TPU:1, one launch (start us, length us, event | category | flops | bytes accessed | tf_op | source)
XLA Modules:
  0.0 96.0 jit_solution(5873906829800533577)
XLA Ops:
  0.6 1.9 %prep.1 = (bf16[544,256]{1,0:T(8,128)(2,1)}, bf16[544,256]{1,0:T(8,128)(2,1)}, f32[192,128]{1,0:T(8,128)}) custom-call(s32[5,2,9]{2,1,0:T(2,128)} %bitcast.12, f32[5,9,4,128]{3,2,1,0:T(4,128)} %bitcast.11, bf16[640,256]{1,0:T(8,128)(2,1)} %bitcast.8), custom_call_target="tpu_custom_call" | custom-call | tf_op jit(solution)/shard_map/prep/pallas_call | solution.py:244
  2.6 0.7 collective-permute-start
  3.3 7.2 %collective-permute-start.1 = (bf16[544,256]{1,0:T(8,128)(2,1)}, bf16[544,256]{1,0:T(8,128)(2,1)S(1)}, u32[]{:S(2)}, u32[]{:S(2)}) collective-permute-start(bf16[544,256]{1,0:T(8,128)(2,1)} %get-tuple-element.22), channel_id=1, source_target_pairs={{0,16},{32,48},{64,80},{96,112},{128,144},{160,176},{192,208},{224... | collective-permute-start | bytes 835592 | tf_op jit(solution)/shard_map/ppermute | solution.py:28
  10.5 0.0 copy-start
  10.5 1.0 %copy-done = bf16[5,128,256]{2,1,0:T(8,128)(2,1)S(1)} copy-done((bf16[5,128,256]{2,1,0:T(8,128)(2,1)S(1)}, bf16[5,128,256]{2,1,0:T(8,128)(2,1)}, u32[]{:S(2)}) %copy-start) | copy-done | bytes 327704
  11.5 0.0 copy-start.1
  11.5 1.0 %copy-done.1 = bf16[1024,256]{1,0:T(8,128)(2,1)S(1)} copy-done((bf16[1024,256]{1,0:T(8,128)(2,1)S(1)}, bf16[1024,256]{1,0:T(8,128)(2,1)}, u32[]{:S(2)}) %copy-start.1) | copy-done | bytes 524312
  12.5 0.0 copy-start.2
  12.5 1.0 %copy-done.2 = bf16[5,128,256]{2,1,0:T(8,128)(2,1)S(1)} copy-done((bf16[5,128,256]{2,1,0:T(8,128)(2,1)S(1)}, bf16[5,128,256]{2,1,0:T(8,128)(2,1)}, u32[]{:S(2)}) %copy-start.2) | copy-done | bytes 327704
  13.5 0.0 copy-start.3
  13.5 0.9 copy-done.3
  14.4 0.3 own.1
  14.7 0.0 collective-permute-done.far_ref
  14.7 0.8 collective-permute-done.1.near_ref
  15.5 0.1 middle.1
  15.5 5.8 %collective-permute-start.2 = (bf16[13,64,256]{2,1,0:T(8,128)(2,1)S(1)}, bf16[13,64,256]{2,1,0:T(8,128)(2,1)S(1)}, u32[]{:S(2)}, u32[]{:S(2)}) collective-permute-start(bf16[13,64,256]{2,1,0:T(8,128)(2,1)S(1)} %get-tuple-element.33), channel_id=1, source_target_pairs={{0,15},{1,2},{2,1},{3,4},{4,3},{5,6},{6,5},{7,8},{8,7},{9,10},{10,... | collective-permute-start | bytes 1277960 | tf_op jit(solution)/shard_map/ppermute | solution.py:283
  21.4 3.2 %collective-permute-start.3 = (bf16[13,64,256]{2,1,0:T(8,128)(2,1)S(1)}, bf16[13,64,256]{2,1,0:T(8,128)(2,1)S(1)}, u32[]{:S(2)}, u32[]{:S(2)}) collective-permute-start(bf16[13,64,256]{2,1,0:T(8,128)(2,1)S(1)} %get-tuple-element.34), channel_id=1, source_target_pairs={{0,1},{1,0},{2,3},{3,2},{4,5},{5,4},{6,7},{7,6},{8,9},{9,8},{10,11... | collective-permute-start | bytes 1277960 | tf_op jit(solution)/shard_map/ppermute | solution.py:286
  24.6 3.5 %inner_band.1 = (f32[5,512,256]{2,1,0:T(8,128)S(1)}, bf16[5,512,1152]{2,1,0:T(8,128)(2,1)S(1)}) custom-call(bf16[544,256]{1,0:T(8,128)(2,1)S(1)} %collective-permute-done.far_ref, bf16[5,128,256]{2,1,0:T(8,128)(2,1)S(1)} %get-tuple-element.29.own_ref, bf16[544,256]{1,0:T(8,128)(2,1)S(1)} %collective-permute-done.1.near_ref, ...), custom_call_target="tpu_custom_call" | custom-call | flops 1509949440 | bytes 4194304 | tf_op jit(solution)/shard_map/inner_band/pallas_call | solution.py:290
  28.1 0.0 collective-permute-done.2.across
  28.1 0.0 collective-permute-done.3.beside
  28.1 3.5 %outer_band.1 = (f32[640,256]{1,0:T(8,128)}, bf16[1024,256]{1,0:T(8,128)(2,1)S(1)}) custom-call(bf16[5,512,1152]{2,1,0:T(8,128)(2,1)S(1)} %get-tuple-element.32.bands, bf16[13,64,256]{2,1,0:T(8,128)(2,1)S(1)} %collective-permute-done.2.across, bf16[13,64,256]{2,1,0:T(8,128)(2,1)S(1)} %collective-permute-done.3.beside, ...), custom_call_target="tpu_custom_call" | custom-call | flops 3019898880 | bytes 6291456 | tf_op jit(solution)/shard_map/outer_band/pallas_call | solution.py:310
  31.7 27.3 %all_to_all.15 = bf16[64,16,256]{2,1,0:T(8,128)(2,1)S(1)} all-to-all(bf16[64,16,256]{2,1,0:T(8,128)(2,1)S(1)} %bitcast.9), channel_id=1, replica_groups=mesh['yh'=2,'z3'=2,'z2'=2,'z1'=2,'zl'=2,'yl'=2,'x'=4,'core'=2] {'yh','zl..., dimensions={0} | all-to-all | bytes 1048576 | tf_op jit(solution)/shard_map/all_to_all | solution.py:233
  58.9 0.1 reduce_sum.24
  59.0 17.5 %all_to_all.16 = bf16[8,16,256]{2,1,0:T(8,128)(2,1)S(1)} all-to-all(bf16[8,16,256]{2,1,0:T(8,128)(2,1)S(1)} %broadcast_in_dim.4), channel_id=1, replica_groups=mesh['yh'=2,'z3'=2,'z2'=2,'z1'=2,'zl'=2,'yl'=2,'x'=4,'core'=2] {'z1','z2..., dimensions={0} | all-to-all | bytes 131072 | tf_op jit(solution)/shard_map/all_to_all | solution.py:233
  76.6 18.4 %all_to_all.17 = bf16[64,16,256]{2,1,0:T(8,128)(2,1)S(1)} all-to-all(bf16[64,16,256]{2,1,0:T(8,128)(2,1)S(1)} %broadcast_in_dim.5), channel_id=1, replica_groups=mesh['yh'=2,'z3'=2,'z2'=2,'z1'=2,'zl'=2,'yl'=2,'x'=4,'core'=2] {'yh','zl..., dimensions={0} | all-to-all | bytes 1048576 | tf_op jit(solution)/shard_map/all_to_all | solution.py:233
  95.0 1.0 %widen.1 = f32[1024,256]{1,0:T(8,128)} custom-call(bf16[1024,256]{1,0:T(8,128)(2,1)S(1)} %bitcast.7), custom_call_target="tpu_custom_call" | custom-call | tf_op jit(solution)/shard_map/widen/pallas_call | solution.py:336
  (3 shorter events, 0.1 us)
Async XLA Ops:
  2.6 12.1 %collective-permute-start = (bf16[544,256]{1,0:T(8,128)(2,1)}, bf16[544,256]{1,0:T(8,128)(2,1)S(1)}, u32[]{:S(2)}, u32[]{:S(2)}) collective-permute-start(bf16[544,256]{1,0:T(8,128)(2,1)} %get-tuple-element.21), channel_id=1, source_target_pairs={{16,32},{48,64},{80,96},{112,128},{144,160},{176,192},{208,224},{2... | collective-permute-start | bytes 835592 | tf_op jit(solution)/shard_map/ppermute | solution.py:28
  3.3 12.2 %collective-permute-start.1 = (bf16[544,256]{1,0:T(8,128)(2,1)}, bf16[544,256]{1,0:T(8,128)(2,1)S(1)}, u32[]{:S(2)}, u32[]{:S(2)}) collective-permute-start(bf16[544,256]{1,0:T(8,128)(2,1)} %get-tuple-element.22), channel_id=1, source_target_pairs={{0,16},{32,48},{64,80},{96,112},{128,144},{160,176},{192,208},{224... | collective-permute-start | bytes 835592 | tf_op jit(solution)/shard_map/ppermute | solution.py:28
  10.5 1.0 %copy-start = (bf16[5,128,256]{2,1,0:T(8,128)(2,1)S(1)}, bf16[5,128,256]{2,1,0:T(8,128)(2,1)}, u32[]{:S(2)}) copy-start(bf16[5,128,256]{2,1,0:T(8,128)(2,1)} %cells_ref.1) | copy-start | bytes 983044
  11.5 1.0 %copy-start.1 = (bf16[1024,256]{1,0:T(8,128)(2,1)S(1)}, bf16[1024,256]{1,0:T(8,128)(2,1)}, u32[]{:S(2)}) copy-start(bf16[1024,256]{1,0:T(8,128)(2,1)} %weight_ref.1) | copy-start | bytes 1572868
  12.5 1.0 %copy-start.2 = (bf16[5,128,256]{2,1,0:T(8,128)(2,1)S(1)}, bf16[5,128,256]{2,1,0:T(8,128)(2,1)}, u32[]{:S(2)}) copy-start(bf16[5,128,256]{2,1,0:T(8,128)(2,1)} %param.5) | copy-start | bytes 983044
  13.5 0.9 copy-start.3
  15.5 12.6 %collective-permute-start.2 = (bf16[13,64,256]{2,1,0:T(8,128)(2,1)S(1)}, bf16[13,64,256]{2,1,0:T(8,128)(2,1)S(1)}, u32[]{:S(2)}, u32[]{:S(2)}) collective-permute-start(bf16[13,64,256]{2,1,0:T(8,128)(2,1)S(1)} %get-tuple-element.33), channel_id=1, source_target_pairs={{0,15},{1,2},{2,1},{3,4},{4,3},{5,6},{6,5},{7,8},{8,7},{9,10},{10,... | collective-permute-start | bytes 1277960 | tf_op jit(solution)/shard_map/ppermute | solution.py:283
  21.4 6.7 %collective-permute-start.3 = (bf16[13,64,256]{2,1,0:T(8,128)(2,1)S(1)}, bf16[13,64,256]{2,1,0:T(8,128)(2,1)S(1)}, u32[]{:S(2)}, u32[]{:S(2)}) collective-permute-start(bf16[13,64,256]{2,1,0:T(8,128)(2,1)S(1)} %get-tuple-element.34), channel_id=1, source_target_pairs={{0,1},{1,0},{2,3},{3,2},{4,5},{5,4},{6,7},{7,6},{8,9},{9,8},{10,11... | collective-permute-start | bytes 1277960 | tf_op jit(solution)/shard_map/ppermute | solution.py:286
